TPU v7x, 32 devices: a whole 2x2x4 slice. The times are simulated.
32 devices in a mesh: gx: 4 (over y, x), gy: 8 (over z, core).
Axes of the slice: x: 2, y: 2, z: 4, core: 2. Of those that a mesh axis runs over, the one named last changes fastest.
Arguments:
- rhs: bfloat16 [256, 384, 128], P(('gx', 'gy')), may hold values from -6 to 6
- diag_blocks: bfloat16 [256, 384, 384], P(('gx', 'gy'))
- inverse_blocks: bfloat16 [256, 384, 384], P(('gx', 'gy'))
- couplings: bfloat16 [256, 6, 384, 96], P(('gx', 'gy')), may hold values from -0.25 to 0.25
- prolong: bfloat16 [384, 48], replicated, may hold values from -0.3125 to 0.3125
- face_source: int32 [256, 6], P(('gx', 'gy')), may hold values from 0 to 5, as said below
- subset: int32 [256], P(('gx', 'gy')), may hold values from 0 to 7
Outputs:
- solution: float32 [256, 384, 128], P(('gx', 'gy'))
Inputs may be any that keep to these rules, and one draw needn't show every extreme that they name: `face_source`: face f of an element and face f xor 1 of its neighbour are both boundary faces or both not. A face that is not a boundary face has code 1 where its neighbour lies inside the same partition and the code of its direction otherwise; face 4 at k = 0 and face 5 at k = 1 are boundary faces. `subset`: subsets of different rows of partitions are different.
All inputs are finite; a program needn't handle non-finite values.
Results may differ from a plain program's by a relative error of at most 0.0055.
Values may be sent and summed in bfloat16 or wider, within the bound.
No kernel may reach another device: no remote copies, remote signals or barrier semaphores. Data moves between devices by JAX's collectives and lax.ppermute only.
A program may use at most 64 MiB of HBM per device.

v0:
```python
import jax
import jax.numpy as jnp
from jax import lax
from jax.sharding import PartitionSpec as P

NVAR = 6
NP = 4
CITER = 4


relax_fine = 0.7
relax_coarse = 0.5


def padded(cells, sides, width):
    for axis, dim in sides:
        count = lax.axis_size(axis)
        head = lax.slice_in_dim(cells, 0, width, axis=dim)
        tail = lax.slice_in_dim(cells, cells.shape[dim] - width, cells.shape[dim], axis=dim)
        cells = jnp.concatenate(
            [
                lax.ppermute(tail, axis, [(i, (i + 1) % count) for i in range(count)]),
                cells,
                lax.ppermute(head, axis, [((i + 1) % count, i) for i in range(count)]),
            ],
            axis=dim,
        )
    return cells


def face_trace(values, face_id):
    leading = values.shape[0]
    columns = values.shape[-1]
    volume = values.reshape(leading, NVAR, NP, NP, NP, columns)
    sliced = lax.index_in_dim(volume, (NP - 1) * (face_id % 2), 4 - face_id // 2, keepdims=False)
    return sliced.reshape(leading, NVAR * NP * NP, columns)


def gathered_traces(state_b, face_source):
    elements = state_b.shape[0]
    layers = elements // 4
    live = face_source > 0
    own_traces = jnp.stack([face_trace(state_b, face_id) for face_id in range(6)], axis=1)
    cube = own_traces.reshape((layers, 2, 2) + own_traces.shape[1:])
    x_side = jnp.stack([cube[:, :, 0, 0], cube[:, :, 1, 1]], axis=0)
    x_ext = padded(x_side, (("gx", 0),), 1)
    y_side = jnp.stack([cube[:, 0, :, 2], cube[:, 1, :, 3]], axis=0)
    y_ext = padded(y_side, (("gy", 0),), 1)
    near0 = jnp.stack([x_ext[0], cube[:, :, 0, 1]], axis=2)
    near1 = jnp.stack([cube[:, :, 1, 0], x_ext[3]], axis=2)
    near2 = jnp.stack([y_ext[0], cube[:, 0, :, 3]], axis=1)
    near3 = jnp.stack([cube[:, 1, :, 2], y_ext[3]], axis=1)
    blank = jnp.zeros_like(cube[:1, :, :, 5])
    near4 = jnp.concatenate([blank, cube[:-1, :, :, 5]], axis=0)
    near5 = jnp.concatenate([cube[1:, :, :, 4], blank], axis=0)
    traces = jnp.stack([near0, near1, near2, near3, near4, near5], axis=3).reshape(own_traces.shape)
    return jnp.where(live[:, :, None, None], traces, jnp.zeros_like(traces))


def residual_of(state, rhs, diag_blocks, couplings, face_source):
    state_b = state.astype(jnp.bfloat16)
    near = gathered_traces(state_b, face_source)
    local_part = jnp.einsum(
        "edk,ekr->edr", diag_blocks, state_b, preferred_element_type=jnp.float32
    )
    remote_part = jnp.einsum("efdt,eftr->edr", couplings, near, preferred_element_type=jnp.float32)
    return rhs.astype(jnp.float32) - local_part - remote_part


def coarse_relax(coarse_rhs, coarse_matrix, members):
    theta = relax_coarse / jnp.maximum(members, 1.0)
    coarse = jnp.zeros_like(coarse_rhs)
    for sweep in range(CITER):
        applied = jnp.einsum("sck,skr->scr", coarse_matrix, coarse, precision=lax.Precision.HIGHEST)
        coarse = coarse + theta[:, None, None] * (coarse_rhs - applied)
    return coarse.astype(jnp.bfloat16)


def on_device(rhs, diag_blocks, inverse_blocks, couplings, prolong, face_source, subset):
    live = face_source > 0
    first = relax_fine * jnp.einsum(
        "edk,ekr->edr", inverse_blocks, rhs, preferred_element_type=jnp.float32
    )
    resid = residual_of(first, rhs, diag_blocks, couplings, face_source)
    resid_b = resid.astype(jnp.bfloat16)
    restricted = jnp.einsum("dc,edr->ecr", prolong, resid_b, preferred_element_type=jnp.float32)
    face_rows = jnp.stack(
        [face_trace(prolong[None], face_id ^ 1)[0] for face_id in range(6)], axis=0
    )
    masked_rows = jnp.where(
        live[:, :, None, None], face_rows[None], jnp.zeros_like(face_rows[None])
    )
    inner = jnp.einsum("edk,kc->edc", diag_blocks, prolong, preferred_element_type=jnp.float32)
    outer = jnp.einsum("efdt,eftc->edc", couplings, masked_rows, preferred_element_type=jnp.float32)
    stiff = (inner + outer).astype(jnp.bfloat16)
    block = jnp.einsum("dc,edk->eck", prolong, stiff, preferred_element_type=jnp.float32)
    subsets = lax.axis_size("gy")
    member = (subset[None, :] == jnp.arange(subsets, dtype=jnp.int32)[:, None]).astype(jnp.float32)
    part_rhs = jnp.einsum("se,ecr->scr", member, restricted, precision=lax.Precision.HIGHEST)
    part_matrix = jnp.einsum("se,eck->sck", member, block, precision=lax.Precision.HIGHEST)
    part_count = jnp.sum(member, axis=1)
    own_rhs, own_matrix, own_count = (
        lax.psum_scatter(
            part_rhs.astype(jnp.bfloat16), "gy", scatter_dimension=0, tiled=True
        ).astype(jnp.float32),
        lax.psum_scatter(
            part_matrix.astype(jnp.bfloat16), "gy", scatter_dimension=0, tiled=True
        ).astype(jnp.float32),
        lax.psum_scatter(
            part_count.astype(jnp.bfloat16), "gy", scatter_dimension=0, tiled=True
        ).astype(jnp.float32),
    )
    coarse_own = coarse_relax(own_rhs, own_matrix, own_count)
    coarse_all = lax.all_gather(coarse_own, "gy", axis=0, tiled=True)
    element_coarse = jnp.einsum(
        "se,scr->ecr", member.astype(jnp.bfloat16), coarse_all, preferred_element_type=jnp.float32
    )
    state = first + jnp.einsum(
        "dc,ecr->edr",
        prolong,
        element_coarse.astype(jnp.bfloat16),
        preferred_element_type=jnp.float32,
    )
    for sweep in range(2):
        resid = residual_of(state, rhs, diag_blocks, couplings, face_source)
        state = state + relax_fine * jnp.einsum(
            "edk,ekr->edr",
            inverse_blocks,
            resid.astype(jnp.bfloat16),
            preferred_element_type=jnp.float32,
        )
    return state


def solution(mesh):
    return jax.shard_map(
        on_device,
        mesh=mesh,
        in_specs=(
            P(("gx", "gy"), None, None),
            P(("gx", "gy"), None, None),
            P(("gx", "gy"), None, None),
            P(("gx", "gy"), None, None, None),
            P(),
            P(("gx", "gy"), None),
            P(("gx", "gy")),
        ),
        out_specs=P(("gx", "gy"), None, None),
        check_vma=False,
    )
```

profile of v0, /device:TPU:0, one launch (start us, length us, event | category | flops | bytes accessed | tf_op | source)
XLA Modules:
  0.0 173.7 jit_solution(2036778758407781080)
XLA Ops:
  6.5 1.7 copy.133
  15.2 1.6 copy.134
  16.9 2.7 %convolution_bitcast_fusion = f32[8,384,48]{1,2,0:T(8,128)} fusion(bf16[8,6,384,96]{2,3,1,0:T(8,128)(2,1)S(1)} %copy-done, pred[8,6]{1,0:T(8,128)(4,1)S(1)} %broadcast_compare_fusion, bf16[6,96,48]{1,2,0:T(8,128)(2,1)} %copy.134), kind=kOutput, calls=%fused_computation.19 | convolution fusion | flops 170090496 | bytes 4184112 | tf_op jit(solution)/shard_map/efdt,eftc->edc/dot_general | solution.py:94
  19.5 3.5 %fusion.39 = f32[8,48,48]{1,2,0:T(8,128)} fusion(f32[8,384,48]{1,2,0:T(8,128)} %convolution_bitcast_fusion, bf16[8,384,384]{2,1,0:T(8,128)(2,1)} %param.8, bf16[384,48]{0,1:T(8,128)(2,1)} %param.11), kind=kOutput, calls=%fused_computation.30 | convolution fusion | flops 127696896 | bytes 3059712 | tf_op jit(solution)/shard_map/dc,edk->eck/dot_general | solution.py:96
  23.1 1.7 copy.136
  24.8 1.3 convolution_convert_fusion.1
  26.8 3.8 %fusion.110 = (bf16[8,384,128]{2,1,0:T(8,128)(2,1)S(1)}, f32[8,384,128]{2,1,0:T(8,128)}) fusion(bf16[8,384,384]{2,1,0:T(8,128)(2,1)} %param.9, bf16[8,384,128]{2,1,0:T(8,128)(2,1)} %param.7), kind=kOutput, calls=%fused_computation.158 | convolution fusion | flops 302776320 | bytes 5505024 | tf_op jit(solution)/shard_map/edk,ekr->edr/dot_general | solution.py:81
  31.4 4.5 %collective-permute-start.3 = (bf16[1,2,2,96,128]{4,3,2,1,0:T(8,128)(2,1)}, bf16[1,2,2,96,128]{4,3,2,1,0:T(8,128)(2,1)}, u32[]{:S(2)}, u32[]{:S(2)}) collective-permute-start(bf16[1,2,2,96,128]{4,3,2,1,0:T(8,128)(2,1)} %get-tuple-element.40), channel_id=1, source_target_pairs={{1,0},{2,1},{3,2},{4,3},{5,4},{6,5},{7,6},{0,7},{9,8},{10,9},{11,1... | collective-permute-start | bytes 294920 | tf_op jit(solution)/shard_map/ppermute | solution.py:24
  38.0 2.4 %collective-permute-start.1 = (bf16[1,2,2,96,128]{4,3,2,1,0:T(8,128)(2,1)}, bf16[1,2,2,96,128]{4,3,2,1,0:T(8,128)(2,1)}, u32[]{:S(2)}, u32[]{:S(2)}) collective-permute-start(bf16[1,2,2,96,128]{4,3,2,1,0:T(8,128)(2,1)} %get-tuple-element.44), channel_id=1, source_target_pairs={{8,0},{16,8},{24,16},{0,24},{9,1},{17,9},{25,17},{1,25},{10,2},{18... | collective-permute-start | bytes 294920 | tf_op jit(solution)/shard_map/ppermute | solution.py:24
  41.2 2.1 %fusion.117 = f32[8,128,384]{2,1,0:T(8,128)} fusion(bf16[8,384,128]{2,1,0:T(8,128)(2,1)S(1)} %get-tuple-element.53, bf16[8,384,384]{2,1,0:T(8,128)(2,1)S(1)} %copy-done.1), kind=kOutput, calls=%fused_computation.161 | convolution fusion | flops 301989888 | bytes 4718592 | tf_op jit(solution)/shard_map/edk,ekr->edr/dot_general | solution.py:63
  44.1 2.3 %copy.113 = bf16[8,384,128]{1,2,0:T(8,128)(2,1)} copy(bf16[8,384,128]{2,1,0:T(8,128)(2,1)} %param.7) | data formatting | bytes 1572864 | tf_op args[0]
  56.4 4.5 %fusion.40 = f32[8,48,128]{2,1,0:T(8,128)} fusion(bf16[8,384,128]{1,2,0:T(8,128)(2,1)} %copy.113, f32[8,128,384]{2,1,0:T(8,128)} %fusion.117, bf16[8,6,384,96]{2,3,1,0:T(8,128)(2,1)S(1)} %copy-done, bf16[8,6,96,128]{3,2,0,1:T(8,128)(2,1)} %constant_dynamic-update-slice_fusion, pred[8,6]{0,1:T(8,128)(4,1)S(1)} %copy.115, bf16[384,48]{0,1:T(8,128)(2,1)} %param.11), kind=kOutput, calls=%fused_computation.31 | convolution fusion | flops 492896256 | bytes 7311408 | tf_op jit(solution)/shard_map/dc,edr->ecr/dot_general | solution.py:86
  60.9 1.3 convolution_convert_fusion.2
  63.4 17.0 %all-reduce.6 = bf16[8]{0:T(256)(128)(2,1)S(1)} all-reduce(bf16[8]{0:T(256)(128)(2,1)} %convert_reduce_fusion), channel_id=2, replica_groups=mesh['gx'=4,'gy'=8] {'gy'}, use_global_device_ids=true, to_apply=%region_1.2.clone | all-reduce | flops 8 | bytes 32
  81.0 1.2 dynamic-slice.1
  82.9 11.4 %reduce-scatter.3.cloned.1.call-done = bf16[1,48,128]{2,1,0:T(8,128)(2,1)} async-done(((bf16[8,48,128]{2,1,0:T(8,128)(2,1)}), bf16[1,48,128]{2,1,0:T(8,128)(2,1)}) %reduce-scatter.3.cloned.1.call-update) | async-done | bytes 12304 | tf_op jit(solution)/shard_map/reduce_scatter | solution.py:103
  97.7 13.9 %all_gather.3 = bf16[8,48,128]{2,1,0:T(8,128)(2,1)S(1)} all-gather(bf16[1,48,128]{2,1,0:T(8,128)(2,1)S(1)} %fusion.56), channel_id=1, replica_groups=mesh['gx'=4,'gy'=8] {'gy'}, dimensions={0}, use_global_device_ids=true | all-gather | bytes 110592 | tf_op jit(solution)/shard_map/all_gather | solution.py:114
  111.9 3.0 %fusion.111 = (bf16[8,384,128]{2,1,0:T(8,128)(2,1)S(1)}, f32[8,384,128]{2,1,0:T(8,128)}) fusion(f32[8,384,128]{2,1,0:T(8,128)} %get-tuple-element.54, bf16[384,48]{0,1:T(8,128)(2,1)} %param.11, bf16[8,48,128]{2,0,1:T(8,128)(2,1)S(1)} %convolution_convert_fusion), kind=kOutput, calls=%fused_computation.159 | convolution fusion | flops 38535168 | bytes 4067328 | tf_op jit(solution)/shard_map/dc,ecr->edr/dot_general | solution.py:118
  116.5 2.1 %fusion.118 = f32[8,128,384]{2,1,0:T(8,128)} fusion(bf16[8,384,128]{2,1,0:T(8,128)(2,1)S(1)} %get-tuple-element.55, bf16[8,384,384]{2,1,0:T(8,128)(2,1)S(1)} %copy-done.2), kind=kOutput, calls=%fused_computation.162 | convolution fusion | flops 301989888 | bytes 4718592 | tf_op jit(solution)/shard_map/edk,ekr->edr/dot_general | solution.py:63
  119.3 2.5 %collective-permute-start.5 = (bf16[1,2,2,96,128]{4,3,2,1,0:T(8,128)(2,1)S(1)}, bf16[1,2,2,96,128]{4,3,2,1,0:T(8,128)(2,1)S(1)}, u32[]{:S(2)}, u32[]{:S(2)}) collective-permute-start(bf16[1,2,2,96,128]{4,3,2,1,0:T(8,128)(2,1)S(1)} %get-tuple-element.36), channel_id=1, source_target_pairs={{8,0},{16,8},{24,16},{0,24},{9,1},{17,9},{25,17},{1,25},{10,2},{18... | collective-permute-start | bytes 294920 | tf_op jit(solution)/shard_map/ppermute | solution.py:24
  122.2 2.4 %collective-permute-done.6 = bf16[1,2,2,96,128]{4,3,2,1,0:T(8,128)(2,1)S(1)} collective-permute-done((bf16[1,2,2,96,128]{4,3,2,1,0:T(8,128)(2,1)S(1)}, bf16[1,2,2,96,128]{4,3,2,1,0:T(8,128)(2,1)S(1)}, u32[]{:S(2)}, u32[]{:S(2)}) %collective-permute-start.6) | collective-permute-done | bytes 98336 | tf_op jit(solution)/shard_map/ppermute | solution.py:22
  124.8 3.6 %collective-permute-done.4 = bf16[1,2,2,96,128]{4,3,2,1,0:T(8,128)(2,1)S(1)} collective-permute-done((bf16[1,2,2,96,128]{4,3,2,1,0:T(8,128)(2,1)S(1)}, bf16[1,2,2,96,128]{4,3,2,1,0:T(8,128)(2,1)S(1)}, u32[]{:S(2)}, u32[]{:S(2)}) %collective-permute-start.4) | collective-permute-done | bytes 98336 | tf_op jit(solution)/shard_map/ppermute | solution.py:22
  132.6 6.8 %fusion.112 = (bf16[8,384,128]{2,1,0:T(8,128)(2,1)}, f32[8,384,128]{2,1,0:T(8,128)}) fusion(f32[8,384,128]{2,1,0:T(8,128)} %get-tuple-element.56, bf16[8,384,384]{2,1,0:T(8,128)(2,1)} %param.9, bf16[8,384,128]{1,2,0:T(8,128)(2,1)} %copy.113, f32[8,128,384]{2,1,0:T(8,128)} %fusion.118, bf16[8,6,384,96]{2,3,1,0:T(8,128)(2,1)S(1)} %copy-done, ...), kind=kOutput, calls=%fused_computation.160 | convolution fusion | flops 758317056 | bytes 13369392 | tf_op jit(solution)/shard_map/edk,ekr->edr/dot_general | solution.py:126
  139.4 1.2 fusion.98
  140.6 1.2 fusion.99
  141.7 2.2 %fusion.100 = (bf16[8,6,4,4,1,128]{5,4,3,2,1,0:T(2,128)(2,1)S(1)}, bf16[8,6,4,4,1,128]{5,4,3,2,1,0:T(2,128)(2,1)S(1)}) fusion(bf16[8,6,4,4,4,128]{5,4,3,2,1,0:T(4,128)(2,1)} %bitcast.286), kind=kLoop, calls=%fused_computation.148 | loop fusion | bytes 786432 | tf_op jit(solution)/shard_map/slice | solution.py:35
  143.9 3.2 %fusion.119 = f32[8,128,384]{2,1,0:T(8,128)} fusion(bf16[8,384,128]{2,1,0:T(8,128)(2,1)} %get-tuple-element.57, bf16[8,384,384]{2,1,0:T(8,128)(2,1)S(1)} %copy-done.3), kind=kOutput, calls=%fused_computation.163 | convolution fusion | flops 301989888 | bytes 4718592 | tf_op jit(solution)/shard_map/edk,ekr->edr/dot_general | solution.py:63
  147.2 1.3 collective-permute-start.11
  149.6 1.3 collective-permute-start.8
  151.7 2.6 %collective-permute-done.10 = bf16[1,2,2,96,128]{4,3,2,1,0:T(8,128)(2,1)S(1)} collective-permute-done((bf16[1,2,2,96,128]{4,3,2,1,0:T(8,128)(2,1)S(1)}, bf16[1,2,2,96,128]{4,3,2,1,0:T(8,128)(2,1)S(1)}, u32[]{:S(2)}, u32[]{:S(2)}) %collective-permute-start.10) | collective-permute-done | bytes 98336 | tf_op jit(solution)/shard_map/ppermute | solution.py:22
  154.4 1.7 collective-permute-done.8
  160.3 6.6 %bitcast_add_fusion = f32[8,384,128]{2,1,0:T(8,128)} fusion(f32[8,384,128]{2,1,0:T(8,128)} %get-tuple-element.58, bf16[8,384,384]{2,1,0:T(8,128)(2,1)} %param.9, bf16[8,384,128]{1,2,0:T(8,128)(2,1)} %copy.113, f32[8,128,384]{2,1,0:T(8,128)} %fusion.119, bf16[8,6,384,96]{2,3,1,0:T(8,128)(2,1)S(1)} %copy-done, ...), kind=kOutput, calls=%fused_computation.15 | convolution fusion | flops 757923840 | bytes 12582960 | tf_op jit(solution)/shard_map/edk,ekr->edr/dot_general | solution.py:126
  (130 shorter events, 40.8 us)
Async XLA Ops:
  6.5 10.3 %copy-start = (bf16[8,6,384,96]{2,3,1,0:T(8,128)(2,1)S(1)}, bf16[8,6,384,96]{2,3,1,0:T(8,128)(2,1)}, u32[]{:S(2)}) copy-start(bf16[8,6,384,96]{2,3,1,0:T(8,128)(2,1)} %param.10) | copy-start | bytes 10616836
  6.5 76.3 %reduce-scatter.5.cloned.1.call-start = ((), (), s32[]{:S(2)}) async-start(), calls=%async_computation.3 | async-start | bytes 110592 | tf_op jit(solution)/shard_map/reduce_scatter | solution.py:106
  19.5 5.2 %copy-start.6 = (s32[8]{0:T(128)S(1)}, s32[8]{0:T(128)}, u32[]{:S(2)}) copy-start(s32[8]{0:T(128)} %param.13) | copy-start | bytes 100
  26.7 67.5 %reduce-scatter.3.cloned.1.call-start = ((), (), s32[]{:S(2)}) async-start(), calls=%async_computation.2 | async-start | bytes 110592 | tf_op jit(solution)/shard_map/reduce_scatter | solution.py:103
  31.4 16.9 %collective-permute-start.3 = (bf16[1,2,2,96,128]{4,3,2,1,0:T(8,128)(2,1)}, bf16[1,2,2,96,128]{4,3,2,1,0:T(8,128)(2,1)}, u32[]{:S(2)}, u32[]{:S(2)}) collective-permute-start(bf16[1,2,2,96,128]{4,3,2,1,0:T(8,128)(2,1)} %get-tuple-element.40), channel_id=1, source_target_pairs={{1,0},{2,1},{3,2},{4,3},{5,4},{6,5},{7,6},{0,7},{9,8},{10,9},{11,1... | collective-permute-start | bytes 294920 | tf_op jit(solution)/shard_map/ppermute | solution.py:24
  36.6 4.7 %copy-start.1 = (bf16[8,384,384]{2,1,0:T(8,128)(2,1)S(1)}, bf16[8,384,384]{2,1,0:T(8,128)(2,1)}, u32[]{:S(2)}) copy-start(bf16[8,384,384]{2,1,0:T(8,128)(2,1)} %param.8) | copy-start | bytes 7077892
  36.6 12.8 %collective-permute-start.2 = (bf16[1,2,2,96,128]{4,3,2,1,0:T(8,128)(2,1)}, bf16[1,2,2,96,128]{4,3,2,1,0:T(8,128)(2,1)}, u32[]{:S(2)}, u32[]{:S(2)}) collective-permute-start(bf16[1,2,2,96,128]{4,3,2,1,0:T(8,128)(2,1)} %get-tuple-element.41), channel_id=1, source_target_pairs={{0,1},{1,2},{2,3},{3,4},{4,5},{5,6},{6,7},{7,0},{8,9},{9,10},{10,1... | collective-permute-start | bytes 294920 | tf_op jit(solution)/shard_map/ppermute | solution.py:22
  38.0 12.3 %collective-permute-start.1 = (bf16[1,2,2,96,128]{4,3,2,1,0:T(8,128)(2,1)}, bf16[1,2,2,96,128]{4,3,2,1,0:T(8,128)(2,1)}, u32[]{:S(2)}, u32[]{:S(2)}) collective-permute-start(bf16[1,2,2,96,128]{4,3,2,1,0:T(8,128)(2,1)} %get-tuple-element.44), channel_id=1, source_target_pairs={{8,0},{16,8},{24,16},{0,24},{9,1},{17,9},{25,17},{1,25},{10,2},{18... | collective-permute-start | bytes 294920 | tf_op jit(solution)/shard_map/ppermute | solution.py:24
  41.2 10.1 %collective-permute-start = (bf16[1,2,2,96,128]{4,3,2,1,0:T(8,128)(2,1)}, bf16[1,2,2,96,128]{4,3,2,1,0:T(8,128)(2,1)}, u32[]{:S(2)}, u32[]{:S(2)}) collective-permute-start(bf16[1,2,2,96,128]{4,3,2,1,0:T(8,128)(2,1)} %get-tuple-element.45), channel_id=1, source_target_pairs={{0,8},{8,16},{16,24},{24,0},{1,9},{9,17},{17,25},{25,1},{2,10},{10... | collective-permute-start | bytes 294920 | tf_op jit(solution)/shard_map/ppermute | solution.py:22
  46.5 3.9 %copy-start.4 = (bf16[2,2,1,96,128]{4,3,1,0,2:T(8,128)(2,1)S(1)}, bf16[2,2,1,96,128]{4,3,1,0,2:T(8,128)(2,1)}, u32[]{:S(2)}) copy-start(bf16[2,2,1,96,128]{4,3,1,0,2:T(8,128)(2,1)} %get-tuple-element.43) | copy-start | bytes 294916
  46.5 4.8 %copy-start.5 = (bf16[2,2,1,96,128]{4,3,1,0,2:T(8,128)(2,1)S(1)}, bf16[2,2,1,96,128]{4,3,1,0,2:T(8,128)(2,1)}, u32[]{:S(2)}) copy-start(bf16[2,2,1,96,128]{4,3,1,0,2:T(8,128)(2,1)} %get-tuple-element.46) | copy-start | bytes 294916
  56.4 24.0 %copy-start.7 = (u32[32]{0:T(128)S(1)}, u32[32]{0:T(128)}, u32[]{:S(2)}) copy-start(u32[32]{0:T(128)} %constant.35) | copy-start | bytes 388
  114.9 1.7 copy-start.2
  118.7 3.5 %collective-permute-start.7 = (bf16[1,2,2,96,128]{4,3,2,1,0:T(8,128)(2,1)S(1)}, bf16[1,2,2,96,128]{4,3,2,1,0:T(8,128)(2,1)S(1)}, u32[]{:S(2)}, u32[]{:S(2)}) collective-permute-start(bf16[1,2,2,96,128]{4,3,2,1,0:T(8,128)(2,1)S(1)} %get-tuple-element.32), channel_id=1, source_target_pairs={{1,0},{2,1},{3,2},{4,3},{5,4},{6,5},{7,6},{0,7},{9,8},{10,9},{11,1... | collective-permute-start | bytes 294920 | tf_op jit(solution)/shard_map/ppermute | solution.py:24
  118.8 5.9 %collective-permute-start.6 = (bf16[1,2,2,96,128]{4,3,2,1,0:T(8,128)(2,1)S(1)}, bf16[1,2,2,96,128]{4,3,2,1,0:T(8,128)(2,1)S(1)}, u32[]{:S(2)}, u32[]{:S(2)}) collective-permute-start(bf16[1,2,2,96,128]{4,3,2,1,0:T(8,128)(2,1)S(1)} %get-tuple-element.33), channel_id=1, source_target_pairs={{0,1},{1,2},{2,3},{3,4},{4,5},{5,6},{6,7},{7,0},{8,9},{9,10},{10,1... | collective-permute-start | bytes 294920 | tf_op jit(solution)/shard_map/ppermute | solution.py:22
  119.3 5.3 %collective-permute-start.5 = (bf16[1,2,2,96,128]{4,3,2,1,0:T(8,128)(2,1)S(1)}, bf16[1,2,2,96,128]{4,3,2,1,0:T(8,128)(2,1)S(1)}, u32[]{:S(2)}, u32[]{:S(2)}) collective-permute-start(bf16[1,2,2,96,128]{4,3,2,1,0:T(8,128)(2,1)S(1)} %get-tuple-element.36), channel_id=1, source_target_pairs={{8,0},{16,8},{24,16},{0,24},{9,1},{17,9},{25,17},{1,25},{10,2},{18... | collective-permute-start | bytes 294920 | tf_op jit(solution)/shard_map/ppermute | solution.py:24
  121.9 6.5 %collective-permute-start.4 = (bf16[1,2,2,96,128]{4,3,2,1,0:T(8,128)(2,1)S(1)}, bf16[1,2,2,96,128]{4,3,2,1,0:T(8,128)(2,1)S(1)}, u32[]{:S(2)}, u32[]{:S(2)}) collective-permute-start(bf16[1,2,2,96,128]{4,3,2,1,0:T(8,128)(2,1)S(1)} %get-tuple-element.37), channel_id=1, source_target_pairs={{0,8},{8,16},{16,24},{24,0},{1,9},{9,17},{17,25},{25,1},{2,10},{10... | collective-permute-start | bytes 294920 | tf_op jit(solution)/shard_map/ppermute | solution.py:22
  139.4 4.5 %copy-start.3 = (bf16[8,384,384]{2,1,0:T(8,128)(2,1)S(1)}, bf16[8,384,384]{2,1,0:T(8,128)(2,1)}, u32[]{:S(2)}) copy-start(bf16[8,384,384]{2,1,0:T(8,128)(2,1)} %param.8) | copy-start | bytes 7077892
  147.2 4.4 %collective-permute-start.11 = (bf16[1,2,2,96,128]{4,3,2,1,0:T(8,128)(2,1)S(1)}, bf16[1,2,2,96,128]{4,3,2,1,0:T(8,128)(2,1)S(1)}, u32[]{:S(2)}, u32[]{:S(2)}) collective-permute-start(bf16[1,2,2,96,128]{4,3,2,1,0:T(8,128)(2,1)S(1)} %get-tuple-element.24), channel_id=1, source_target_pairs={{1,0},{2,1},{3,2},{4,3},{5,4},{6,5},{7,6},{0,7},{9,8},{10,9},{11,1... | collective-permute-start | bytes 294920 | tf_op jit(solution)/shard_map/ppermute | solution.py:24
  148.5 5.8 %collective-permute-start.10 = (bf16[1,2,2,96,128]{4,3,2,1,0:T(8,128)(2,1)S(1)}, bf16[1,2,2,96,128]{4,3,2,1,0:T(8,128)(2,1)S(1)}, u32[]{:S(2)}, u32[]{:S(2)}) collective-permute-start(bf16[1,2,2,96,128]{4,3,2,1,0:T(8,128)(2,1)S(1)} %get-tuple-element.25), channel_id=1, source_target_pairs={{0,1},{1,2},{2,3},{3,4},{4,5},{5,6},{6,7},{7,0},{8,9},{9,10},{10,1... | collective-permute-start | bytes 294920 | tf_op jit(solution)/shard_map/ppermute | solution.py:22
  148.6 5.8 %collective-permute-start.9 = (bf16[1,2,2,96,128]{4,3,2,1,0:T(8,128)(2,1)S(1)}, bf16[1,2,2,96,128]{4,3,2,1,0:T(8,128)(2,1)S(1)}, u32[]{:S(2)}, u32[]{:S(2)}) collective-permute-start(bf16[1,2,2,96,128]{4,3,2,1,0:T(8,128)(2,1)S(1)} %get-tuple-element.28), channel_id=1, source_target_pairs={{8,0},{16,8},{24,16},{0,24},{9,1},{17,9},{25,17},{1,25},{10,2},{18... | collective-permute-start | bytes 294920 | tf_op jit(solution)/shard_map/ppermute | solution.py:24
  149.6 6.5 %collective-permute-start.8 = (bf16[1,2,2,96,128]{4,3,2,1,0:T(8,128)(2,1)S(1)}, bf16[1,2,2,96,128]{4,3,2,1,0:T(8,128)(2,1)S(1)}, u32[]{:S(2)}, u32[]{:S(2)}) collective-permute-start(bf16[1,2,2,96,128]{4,3,2,1,0:T(8,128)(2,1)S(1)} %get-tuple-element.29), channel_id=1, source_target_pairs={{0,8},{8,16},{16,24},{24,0},{1,9},{9,17},{17,25},{25,1},{2,10},{10... | collective-permute-start | bytes 294920 | tf_op jit(solution)/shard_map/ppermute | solution.py:22
Sparse Core Ops, SparseCore 0:
  26.9 32.8 reduce-scatter.4
  62.9 31.2 reduce-scatter.2
where the time goes:
time: 175 us; the launch traced here: 174 us
  matrix products  44.4 us (25%)
  local copies, waits for them, and re-layouts  42.4 us (24%)
  blocking collectives  30.9 us (18%)
  waiting for transfers between devices  22.6 us (13%)
  between operations  14.5 us (8%)
  starting transfers between devices  13.6 us (8%)
  other arithmetic  5.22 us (3%)
    unnamed x48, local copies, waits for them, and re-layouts  20.3 us
    unnamed x1, blocking collectives  17 us
    all_gather x1, blocking collectives, on_device(): coarse_all = lax.all_gather(coarse_own, 'gy', axis=0, tiled=True)  13.9 us
    dot_general x2, matrix products, on_device(): jnp.einsum('edk,ekr->edr', inverse_blocks, resid.astype(jnp.bfloat16), pr...  13.4 us
    ppermute x6, starting transfers between devices, padded(): lax.ppermute(head, axis, [((i + 1) % count, i) for i in range(count)])  11.6 us
    reduce_scatter x1, waiting for transfers between devices, on_device(): lax.psum_scatter(part_rhs.astype(jnp.bfloat16), 'gy', scatter_dimension=0...  11.4 us
    ppermute x6, waiting for transfers between devices, padded(): lax.ppermute(tail, axis, [(i, (i + 1) % count) for i in range(count)])  10.3 us
    slice x9, local copies, waits for them, and re-layouts, face_trace(): lax.index_in_dim(volume, (NP - 1) * (face_id % 2), 4 - face_id // 2, keep...  7.65 us
  transfers between devices with their start and end apart: 14, of which 6 were waited for; matrix products, arithmetic and copies ran while one was open for 18% of the time, Pallas kernels for 0%

commit v1 on v0

v1 whole, which is shorter than its diff:
```python
import functools

import jax
import jax.numpy as jnp
from jax import lax
from jax.experimental import pallas as pl
from jax.experimental.pallas import tpu as pltpu
from jax.sharding import PartitionSpec as P

NVAR = 6
NP = 4
CITER = 4

relax_fine = 0.7
relax_coarse = 0.5

F32 = jnp.float32
BF16 = jnp.bfloat16
LIMIT = 40 * 1024 * 1024


def dot(a, b, precision=None):
    return jnp.dot(a, b, preferred_element_type=F32, precision=precision)


def place(e):
    return lax.rem(e, 2), lax.rem(lax.div(e, 2), 2), lax.div(e, 4)


def whole(shape):
    return pl.BlockSpec(shape, lambda e: (0,) * len(shape))


def each(shape):
    return pl.BlockSpec((1,) + shape, lambda e: (e,) + (0,) * len(shape))


def scalars():
    return pl.BlockSpec(memory_space=pltpu.SMEM)


def run(body, ins, in_specs, outs, out_specs, scratch, grid, flops):
    size = sum(a.size * a.dtype.itemsize for a in list(ins) + list(outs))
    return pl.pallas_call(
        body,
        grid=grid,
        in_specs=in_specs,
        out_specs=out_specs,
        out_shape=outs,
        scratch_shapes=scratch,
        compiler_params=pltpu.CompilerParams(vmem_limit_bytes=LIMIT),
        cost_estimate=pl.CostEstimate(flops=flops, bytes_accessed=size, transcendentals=0),
    )(*ins)


def read_traces(load, tmp):
    side = NP * NP
    layers = NVAR * NP
    faces = [load(0, layers * NP, NP), load(NP - 1, layers * NP, NP)]
    for g in (0, 1):
        for ii in range(NP):
            tmp[g, pl.ds(ii, layers, stride=NP), :] = load(g * NP * (NP - 1) + ii, layers, side)
        faces.append(tmp[g])
    for g in (0, 1):
        faces.append(
            jnp.concatenate(
                [load((v * NP + g * (NP - 1)) * side, side, 1) for v in range(NVAR)], axis=0
            )
        )
    return faces


def emit_traces(e, state_ref, tr_ref, gxm, gxp, gym, gyp, tmp):
    def load(start, size, stride):
        if stride == 1:
            return state_ref[0, pl.ds(start, size), :]
        return state_ref[0, pl.ds(start, size, stride=stride), :]

    faces = [face.astype(BF16) for face in read_traces(load, tmp)]
    for f in range(6):
        tr_ref[0, f] = faces[f]
    i, j, k = place(e)
    at_x = lax.div(e, 2)
    at_y = i + 2 * k

    @pl.when(i == 0)
    def _():
        gxm[at_x] = faces[0]

    @pl.when(i == 1)
    def _():
        gxp[at_x] = faces[1]

    @pl.when(j == 0)
    def _():
        gym[at_y] = faces[2]

    @pl.when(j == 1)
    def _():
        gyp[at_y] = faces[3]


def masked(face_source, e, f, value):
    return jnp.where(face_source[e, f] > 0, value, jnp.zeros_like(value))


def first_body(rhs, inv, first, tr, gxm, gxp, gym, gyp, tmp):
    e = pl.program_id(0)
    first[0] = relax_fine * dot(inv[0], rhs[0])
    emit_traces(e, first, tr, gxm, gxp, gym, gyp, tmp)


def local_body(rhs, state, diag, coup, tr, prolong, face_source, subset, acc, mats, pf, pt, wide, tmp, msum):
    e = pl.program_id(0)
    last = pl.num_programs(0) - 1
    coarse = prolong.shape[1]

    @pl.when(e == 0)
    def _():
        wide[...] = jnp.zeros_like(wide)
        wide[:, 0:coarse] = prolong[...].astype(F32)

        def load(start, size, stride):
            if stride == 1:
                return wide[pl.ds(start, size), :]
            return wide[pl.ds(start, size, stride=stride), :]

        for f, face in enumerate(read_traces(load, tmp)):
            pf[f] = face.astype(BF16)
        pt[...] = wide[...].T[0:coarse].astype(BF16)
        msum[...] = jnp.zeros_like(msum)

    i, j, k = place(e)
    cols = acc.shape[2]
    both = jnp.concatenate([state[0].astype(BF16), wide[...].astype(BF16)], axis=1)
    total = dot(diag[0], both)
    for f, near, face in (
        (1 - i, jnp.bitwise_xor(e, 1), i),
        (3 - j, jnp.bitwise_xor(e, 2), 2 + j),
        (5 - k, jnp.bitwise_xor(e, 4), 4 + k),
    ):
        rows = jnp.concatenate([tr[near, face], pf[face]], axis=1)
        total = total + dot(coup[0, f], masked(face_source, e, f, rows))
    acc[0] = rhs[0].astype(F32) - total[:, 0:cols]
    stiff = total[:, cols:]
    for f, face in ((i, 1 - i), (2 + j, 3 - j)):
        stiff = stiff + dot(coup[0, f], masked(face_source, e, f, pf[face]))
    block = dot(pt[...], stiff.astype(BF16))
    lane = lax.broadcasted_iota(jnp.int32, block.shape, 1)
    s = subset[e]
    msum[s] += block + jnp.where(lane == coarse, 1.0, 0.0)
    msum[0] += jnp.where(lane == coarse + 1 + e, s.astype(F32), 0.0)

    @pl.when(e == last)
    def _():
        mats[...] = msum[...].astype(BF16)


def pick_x(e, from_m, from_p):
    i = lax.rem(e, 2)
    at = lax.div(e, 2)
    return jnp.where(i == 0, from_m[at], from_p[at])


def pick_y(e, from_m, from_p):
    i, j, k = place(e)
    at = i + 2 * k
    return jnp.where(j == 0, from_m[at], from_p[at])


def restrict_body(part, cx, cy, xm, xp, ym, yp, pt, face_source, subset, resid, sums, total):
    e = pl.program_id(0)
    i, j, k = place(e)

    @pl.when(e == 0)
    def _():
        total[...] = jnp.zeros_like(total)

    r = part[0] - dot(cx[0, 0], masked(face_source, e, i, pick_x(e, xm, xp)))
    r = r - dot(cy[0, 0], masked(face_source, e, 2 + j, pick_y(e, ym, yp)))
    resid[0] = r
    total[subset[e]] += dot(pt[...], r.astype(BF16))

    @pl.when(e == pl.num_programs(0) - 1)
    def _():
        sums[...] = total[...].astype(BF16)


def coarse_body(one, two, mats, subset, y_all, y_m, y_p):
    groups = one.shape[0]
    coarse = one.shape[1]
    high = lax.Precision.HIGHEST
    rights, blocks, thetas, ys = [], [], [], []
    for s in range(groups):
        block = mats[0, s].astype(F32)
        for d in range(1, mats.shape[0]):
            block = block + mats[d, s].astype(F32)
        theta = relax_coarse / jnp.maximum(block[:, coarse : coarse + 1], 1.0)
        right = one[s].astype(F32) + two[s].astype(F32)
        rights.append(right)
        blocks.append(block[:, 0:coarse])
        thetas.append(theta)
        ys.append(theta * right)
    for sweep in range(CITER - 1):
        applied = [dot(blocks[s], ys[s], high) for s in range(groups)]
        ys = [ys[s] + thetas[s] * (rights[s] - applied[s]) for s in range(groups)]
    for s in range(groups):
        y_all[s] = ys[s].astype(BF16)
    for e in range(subset.shape[0]):
        (y_p if e % 2 else y_m)[e // 2] = y_all[subset[e]]


def second_body(resid, state, diag, coup, y_all, prolong, pf, face_source, subset, near_sets, acc, second):
    e = pl.program_id(0)
    i, j, k = place(e)
    coarse = prolong.shape[1]
    step = dot(prolong[...], y_all[subset[e]])
    second[0] = state[0] + step
    total = dot(diag[0], step.astype(BF16))
    for f, s, face in (
        (1 - i, subset[jnp.bitwise_xor(e, 1)], i),
        (3 - j, subset[jnp.bitwise_xor(e, 2)], 2 + j),
        (5 - k, subset[jnp.bitwise_xor(e, 4)], 4 + k),
        (2 + j, near_sets[j, jnp.bitwise_xor(e, 2)], 3 - j),
    ):
        rows = dot(pf[face][:, 0:coarse], y_all[s]).astype(BF16)
        total = total + dot(coup[0, f], masked(face_source, e, f, rows))
    acc[0] = resid[0] - total


def smooth_body(part, second, cx, inv, ym, yp, pf, face_source, state, tr, gxm, gxp, gym, gyp, tmp):
    e = pl.program_id(0)
    i, j, k = place(e)
    coarse = ym.shape[1]
    rows = dot(pf[1 - i][:, 0:coarse], pick_x(e, ym, yp)).astype(BF16)
    r = part[0] - dot(cx[0, 0], masked(face_source, e, i, rows))
    state[0] = second[0] + relax_fine * dot(inv[0], r.astype(BF16))
    emit_traces(e, state, tr, gxm, gxp, gym, gyp, tmp)


def inner_body(rhs, state, diag, coup, tr, face_source, acc):
    e = pl.program_id(0)
    i, j, k = place(e)
    total = dot(diag[0], state[0].astype(BF16))
    for f, near, face in (
        (1 - i, jnp.bitwise_xor(e, 1), i),
        (3 - j, jnp.bitwise_xor(e, 2), 2 + j),
        (5 - k, jnp.bitwise_xor(e, 4), 4 + k),
    ):
        total = total + dot(coup[0, f], masked(face_source, e, f, tr[near, face]))
    acc[0] = rhs[0].astype(F32) - total


def final_body(part, state, cx, cy, inv, xm, xp, ym, yp, face_source, out):
    e = pl.program_id(0)
    i, j, k = place(e)
    r = part[0] - dot(cx[0, 0], masked(face_source, e, i, pick_x(e, xm, xp)))
    r = r - dot(cy[0, 0], masked(face_source, e, 2 + j, pick_y(e, ym, yp)))
    out[0] = state[0] + relax_fine * dot(inv[0], r.astype(BF16))


def shift(value, axis, step):
    count = lax.axis_size(axis)
    return lax.ppermute(value, axis, [(i, (i + step) % count) for i in range(count)])


def exchange(sends):
    gxm, gxp, gym, gyp = sends
    return (
        shift(gxp, "gx", 1),
        shift(gxm, "gx", -1),
        shift(gyp, "gy", 1),
        shift(gym, "gy", -1),
    )


def row_sum(part):
    count = lax.axis_size("gy")
    if count & (count - 1):
        return lax.psum(part, "gy"), jnp.zeros_like(part)
    step = 1
    while True:
        other = lax.ppermute(part, "gy", [(i, i ^ step) for i in range(count)])
        step *= 2
        if step >= count:
            return part, other
        part = (part.astype(F32) + other.astype(F32)).astype(BF16)


def on_device(rhs, diag_blocks, inverse_blocks, couplings, prolong, face_source, subset):
    elements, dof, cols = rhs.shape
    fdof = couplings.shape[3]
    coarse = prolong.shape[1]
    groups = lax.axis_size("gy")
    grid = (elements,)
    half = elements // 2
    shape = jax.ShapeDtypeStruct
    state_s = shape((elements, dof, cols), F32)
    tr_s = shape((elements, 6, fdof, cols), BF16)
    send_s = shape((half, fdof, cols), BF16)
    sends_s = [send_s] * 4
    fine = each((dof, cols))
    square = each((dof, dof))
    faces = each((6, dof, fdof))
    traced = each((6, fdof, cols))
    side = whole((half, fdof, cols))
    face_x = pl.BlockSpec((1, 1, dof, fdof), lambda e: (e, lax.rem(e, 2), 0, 0))
    face_y = pl.BlockSpec((1, 1, dof, fdof), lambda e: (e, 2 + lax.rem(lax.div(e, 2), 2), 0, 0))
    tmp = pltpu.VMEM((2, fdof, cols), F32)
    apply_flops = 2 * elements * dof * cols * (dof + 3 * fdof)
    inv_flops = 2 * elements * dof * dof * cols
    far_flops = 4 * elements * dof * fdof * cols

    first, tr, *sends = run(
        first_body,
        (rhs, inverse_blocks),
        [fine, square],
        [state_s, tr_s] + sends_s,
        [fine, traced] + [side] * 4,
        [tmp],
        grid,
        inv_flops,
    )
    xm, xp, ym, yp = exchange(sends)
    acc, mats, pf, pt = run(
        local_body,
        (rhs, first, diag_blocks, couplings, tr, prolong, face_source, subset),
        [fine, fine, square, faces, whole(tr.shape), whole(prolong.shape), scalars(), scalars()],
        [
            state_s,
            shape((groups, coarse, cols), BF16),
            shape((6, fdof, cols), BF16),
            shape((coarse, dof), BF16),
        ],
        [
            fine,
            whole((groups, coarse, cols)),
            whole((6, fdof, cols)),
            whole((coarse, dof)),
        ],
        [pltpu.VMEM((dof, cols), F32), tmp, pltpu.VMEM((groups, coarse, cols), F32)],
        grid,
        2 * apply_flops,
    )
    all_mats = lax.all_gather(mats, "gy", axis=0)
    all_sets = all_mats[:, 0, 0, coarse + 1 : coarse + 1 + elements].astype(jnp.int32)
    me = lax.axis_index("gy")
    near_sets = jnp.stack(
        [
            lax.dynamic_index_in_dim(all_sets, (me - 1) % groups, 0, keepdims=False),
            lax.dynamic_index_in_dim(all_sets, (me + 1) % groups, 0, keepdims=False),
        ]
    )
    resid, sums = run(
        restrict_body,
        (acc, couplings, couplings, xm, xp, ym, yp, pt, face_source, subset),
        [fine, face_x, face_y, side, side, side, side, whole(pt.shape), scalars(), scalars()],
        [state_s, shape((groups, coarse, cols), BF16)],
        [fine, whole((groups, coarse, cols))],
        [pltpu.VMEM((groups, coarse, cols), F32)],
        grid,
        far_flops,
    )
    one, two = row_sum(sums)
    y_s = shape((half, coarse, cols), BF16)
    vmem = pl.BlockSpec(memory_space=pltpu.VMEM)
    y_all, y_m, y_p = run(
        coarse_body,
        (one, two, all_mats, subset),
        [vmem, vmem, vmem, scalars()],
        [shape((groups, coarse, cols), BF16), y_s, y_s],
        [vmem, vmem, vmem],
        [],
        (),
        6 * 2 * groups * coarse * coarse * cols * CITER,
    )
    yxm = shift(y_p, "gx", 1)
    yxp = shift(y_m, "gx", -1)
    acc, second = run(
        second_body,
        (resid, first, diag_blocks, couplings, y_all, prolong, pf, face_source, subset, near_sets),
        [
            fine,
            fine,
            square,
            faces,
            whole(y_all.shape),
            whole(prolong.shape),
            whole(pf.shape),
            scalars(),
            scalars(),
            scalars(),
        ],
        [state_s, state_s],
        [fine, fine],
        [],
        grid,
        apply_flops,
    )
    state, tr, *sends = run(
        smooth_body,
        (acc, second, couplings, inverse_blocks, yxm, yxp, pf, face_source),
        [fine, fine, face_x, square, whole(y_m.shape), whole(y_m.shape), whole(pf.shape), scalars()],
        [state_s, tr_s] + sends_s,
        [fine, traced] + [side] * 4,
        [tmp],
        grid,
        inv_flops,
    )
    xm, xp, ym, yp = exchange(sends)
    acc = run(
        inner_body,
        (rhs, state, diag_blocks, couplings, tr, face_source),
        [fine, fine, square, faces, whole(tr.shape), scalars()],
        [state_s],
        [fine],
        [],
        grid,
        apply_flops,
    )[0]
    return run(
        final_body,
        (acc, state, couplings, couplings, inverse_blocks, xm, xp, ym, yp, face_source),
        [fine, fine, face_x, face_y, square, side, side, side, side, scalars()],
        [state_s],
        [fine],
        [],
        grid,
        inv_flops + far_flops,
    )[0]


def solution(mesh):
    return jax.shard_map(
        on_device,
        mesh=mesh,
        in_specs=(
            P(("gx", "gy"), None, None),
            P(("gx", "gy"), None, None),
            P(("gx", "gy"), None, None),
            P(("gx", "gy"), None, None, None),
            P(),
            P(("gx", "gy"), None),
            P(("gx", "gy")),
        ),
        out_specs=P(("gx", "gy"), None, None),
        check_vma=False,
    )
```

time: 175 us -> 114 us (0.65)
  matrix products: 44.4 us -> 0 us
  Pallas kernels: 0 us -> 34.2 us
  blocking collectives: 30.9 us -> 15.7 us
  between operations: 14.5 us -> 0.22 us
  local copies, waits for them, and re-layouts: 42.4 us -> 31.2 us
  waiting for transfers between devices: 22.6 us -> 11.7 us
  starting transfers between devices: 13.6 us -> 19 us
  other arithmetic: 5.22 us -> 1.04 us
    dot_general x17 -> x0, matrix products: 44.4 us -> none  [the longest x2 13.4 us: on_device(): jnp.einsum('edk,ekr->edr', inverse_blocks, resid.astype(jnp.bfloat16), pr...]
    pallas_call x0 -> x8, Pallas kernels: none -> 34.2 us  [run(): pl.pallas_call(body, grid=grid, in_specs=in_specs, out_specs=out_specs, o...]
    unnamed x1 -> x0, blocking collectives: 17 us -> none
    reduce_scatter x2 -> x0, waiting for transfers between devices: 11.4 us -> none  [the longest x1 11.4 us: on_device(): lax.psum_scatter(part_rhs.astype(jnp.bfloat16), 'gy', scatter_dimension=0...]
    unnamed x48 -> x58, local copies, waits for them, and re-layouts: 20.3 us -> 31.2 us
    slice x12 -> x0, local copies, waits for them, and re-layouts: 9.62 us -> none  [the longest x9 7.65 us: face_trace(): lax.index_in_dim(volume, (NP - 1) * (face_id % 2), 4 - face_id // 2, keep...]
    another operation x29 -> x0, local copies, waits for them, and re-layouts: 7.35 us -> none  [the longest x2 2.25 us: on_device(): jnp.stack([face_trace(prolong[None], face_id ^ 1)[0] for face_id in range...]
    ppermute x12 -> x13, starting transfers between devices: 13.6 us -> 19 us  [the longest x10 16.9 us: shift(): lax.ppermute(value, axis, [(i, (i + step) % count) for i in range(count)])]
  transfers between devices with their start and end apart: 14 -> 13, of which waited for: 6 -> 3; matrix products, arithmetic and copies ran while one was open for 18% -> 6% of each run, Pallas kernels for 0% -> 14%
where the time goes in v1:
time: 114 us; the launch traced here: 113 us
  Pallas kernels  34.2 us (30%)
  local copies, waits for them, and re-layouts  31.2 us (27%)
  starting transfers between devices  19 us (17%)
  blocking collectives  15.7 us (14%)
  waiting for transfers between devices  11.7 us (10%)
    pallas_call x8, Pallas kernels, run(): pl.pallas_call(body, grid=grid, in_specs=in_specs, out_specs=out_specs, o...  34.2 us
    unnamed x58, local copies, waits for them, and re-layouts  31.2 us
    ppermute x10, starting transfers between devices, shift(): lax.ppermute(value, axis, [(i, (i + step) % count) for i in range(count)])  16.9 us
    all_gather x1, blocking collectives, on_device(): all_mats = lax.all_gather(mats, 'gy', axis=0)  15.7 us
    ppermute x3, waiting for transfers between devices, row_sum(): other = lax.ppermute(part, 'gy', [(i, i ^ step) for i in range(count)])  11.7 us
  transfers between devices with their start and end apart: 13, of which 3 were waited for; matrix products, arithmetic and copies ran while one was open for 6% of the time, Pallas kernels for 14%

profile of v1, /device:TPU:0, one launch (start us, length us, event | category | flops | bytes accessed | tf_op | source)
XLA Modules:
  0.0 113.0 jit_solution(6818639410678851024)
XLA Ops:
  0.0 1.7 %copy-done.4 = bf16[8,384,384]{2,1,0:T(8,128)(2,1)S(1)} copy-done((bf16[8,384,384]{2,1,0:T(8,128)(2,1)S(1)}, bf16[8,384,384]{2,1,0:T(8,128)(2,1)}, u32[]{:S(2)}) %copy-start.4) | copy-done | bytes 2359320
  2.8 2.4 %shard_map.73 = (f32[8,384,128]{2,1,0:T(8,128)S(1)}, bf16[8,6,96,128]{3,2,1,0:T(8,128)(2,1)S(1)}, bf16[4,96,128]{2,1,0:T(8,128)(2,1)S(1)}, bf16[4,96,128]{2,1,0:...) custom-call(bf16[8,384,128]{2,1,0:T(8,128)(2,1)S(1)} %copy-done.7, ...), custom_call_target="tpu_custom_call" | custom-call | flops 301989888 | bytes 6291456 | tf_op jit(solution)/shard_map/pallas_call | solution.py:44
  5.2 1.1 %copy-done.10 = f32[8,384,128]{2,1,0:T(8,128)} copy-done((f32[8,384,128]{2,1,0:T(8,128)}, f32[8,384,128]{2,1,0:T(8,128)S(1)}, u32[]{:S(2)}) %copy-start.10) | copy-done | bytes 1572888
  7.4 2.9 %collective-permute-start = (bf16[4,96,128]{2,1,0:T(8,128)(2,1)S(1)}, bf16[4,96,128]{2,1,0:T(8,128)(2,1)S(1)}, u32[]{:S(2)}, u32[]{:S(2)}) collective-permute-start(bf16[4,96,128]{2,1,0:T(8,128)(2,1)S(1)} %get-tuple-element.31), channel_id=1, source_target_pairs={{0,8},{8,16},{16,24},{24,0},{1,9},{9,17},{17,25},{25,1},{2,10},{10... | collective-permute-start | bytes 294920 | tf_op jit(solution)/shard_map/ppermute | solution.py:264
  11.3 3.5 %collective-permute-start.3 = (bf16[4,96,128]{2,1,0:T(8,128)(2,1)S(1)}, bf16[4,96,128]{2,1,0:T(8,128)(2,1)S(1)}, u32[]{:S(2)}, u32[]{:S(2)}) collective-permute-start(bf16[4,96,128]{2,1,0:T(8,128)(2,1)S(1)} %get-tuple-element.34), channel_id=1, source_target_pairs={{0,7},{1,0},{2,1},{3,2},{4,3},{5,4},{6,5},{7,6},{8,15},{9,8},{10,9... | collective-permute-start | bytes 294920 | tf_op jit(solution)/shard_map/ppermute | solution.py:264
  15.0 6.4 %copy.18.coup.cx.cy = bf16[8,6,384,96]{3,2,1,0:T(8,128)(2,1)} copy(bf16[8,6,384,96]{2,3,1,0:T(8,128)(2,1)} %param.10) | data formatting | bytes 7077888 | tf_op args[3]
  21.4 2.3 %copy-done = bf16[8,6,384,96]{3,2,1,0:T(8,128)(2,1)S(1)} copy-done((bf16[8,6,384,96]{3,2,1,0:T(8,128)(2,1)S(1)}, bf16[8,6,384,96]{3,2,1,0:T(8,128)(2,1)}, u32[]{:S(2)}) %copy-start) | copy-done | bytes 3538968
  24.9 1.4 %copy-done.11 = f32[8,384,128]{2,1,0:T(8,128)S(1)} copy-done((f32[8,384,128]{2,1,0:T(8,128)S(1)}, f32[8,384,128]{2,1,0:T(8,128)}, u32[]{:S(2)}) %copy-start.11) | copy-done | bytes 1572888
  26.3 1.3 %copy-done.22 = bf16[8,6,96,128]{3,2,1,0:T(8,128)(2,1)S(1)} copy-done((bf16[8,6,96,128]{3,2,1,0:T(8,128)(2,1)S(1)}, bf16[8,6,96,128]{3,2,1,0:T(8,128)(2,1)}, u32[]{:S(2)}) %copy-start.22) | copy-done | bytes 1179672
  27.6 5.9 %shard_map.74 = (f32[8,384,128]{2,1,0:T(8,128)S(1)}, bf16[8,48,128]{2,1,0:T(8,128)(2,1)S(1)}, bf16[6,96,128]{2,1,0:T(8,128)(2,1)S(1)}, bf16[48,384]{1,0:T(8,128)(2,1)S(1)}) custom-call(bf16[8,384,128]{2,1,0:T(8,128)(2,1)S(1)} %copy-done.8, f32[8,384,128]{2,1,0:T(8,128)S(1)} %copy-done.11, bf16[8,384,384]{2,1,0:T(8,128)(2,1)S(1)} %copy-done.6, ...), custom_call_target="tpu_custom_call" | custom-call | flops 1056964608 | bytes 11329760 | tf_op jit(solution)/shard_map/pallas_call | solution.py:44
  33.5 15.7 %all-gather = bf16[64,48,128]{2,1,0:T(8,128)(2,1)S(1)} all-gather(bf16[8,48,128]{2,1,0:T(8,128)(2,1)S(1)} %get-tuple-element.38), channel_id=2, replica_groups=mesh['gx'=4,'gy'=8] {'gy'}, dimensions={0}, use_global_device_ids=true | all-gather | bytes 884736 | tf_op jit(solution)/shard_map/all_gather | solution.py:345
  49.2 4.1 %shard_map.75 = (f32[8,384,128]{2,1,0:T(8,128)S(1)}, bf16[8,48,128]{2,1,0:T(8,128)(2,1)}) custom-call(f32[8,384,128]{2,1,0:T(8,128)S(1)} %get-tuple-element.30.part, bf16[8,6,384,96]{3,2,1,0:T(8,128)(2,1)S(1)} %copy-done.1, bf16[8,6,384,96]{3,2,1,0:T(8,128)(2,1)S(1)} %copy-done.1, bf16[4,96,128]{2,1,0:T(8,128)(2,1)S(1)} %collective-permute-done.xm, ...), custom_call_target="tpu_custom_call" | custom-call | flops 150994944 | bytes 10752224 | tf_op jit(solution)/shard_map/pallas_call | solution.py:44
  53.3 1.2 %copy-done.19 = f32[8,384,128]{2,1,0:T(8,128)} copy-done((f32[8,384,128]{2,1,0:T(8,128)}, f32[8,384,128]{2,1,0:T(8,128)S(1)}, u32[]{:S(2)}) %copy-start.19) | copy-done | bytes 1572888
  57.4 4.7 %collective-permute-done.5 = bf16[8,48,128]{2,1,0:T(8,128)(2,1)S(1)} collective-permute-done((bf16[8,48,128]{2,1,0:T(8,128)(2,1)S(1)}, bf16[8,48,128]{2,1,0:T(8,128)(2,1)S(1)}, u32[]{:S(2)}, u32[]{:S(2)}) %collective-permute-start.5) | collective-permute-done | bytes 98336 | tf_op jit(solution)/shard_map/ppermute | solution.py:283
  62.1 1.2 %collective-permute-start.6 = (bf16[8,48,128]{2,1,0:T(8,128)(2,1)S(1)}, bf16[8,48,128]{2,1,0:T(8,128)(2,1)S(1)}, u32[]{:S(2)}, u32[]{:S(2)}) collective-permute-start(bf16[8,48,128]{2,1,0:T(8,128)(2,1)S(1)} %add_convert_fusion.one), channel_id=1, source_target_pairs={{0,4},{1,5},{2,6},{3,7},{4,0},{5,1},{6,2},{7,3},{8,12},{9,13},{10,... | collective-permute-start | bytes 294920 | tf_op jit(solution)/shard_map/ppermute | solution.py:283
  63.3 5.9 %collective-permute-done.6.two = bf16[8,48,128]{2,1,0:T(8,128)(2,1)S(1)} collective-permute-done((bf16[8,48,128]{2,1,0:T(8,128)(2,1)S(1)}, bf16[8,48,128]{2,1,0:T(8,128)(2,1)S(1)}, u32[]{:S(2)}, u32[]{:S(2)}) %collective-permute-start.6) | collective-permute-done | bytes 98336 | tf_op jit(solution)/shard_map/ppermute | solution.py:283
  70.4 1.4 %shard_map.76 = (bf16[8,48,128]{2,1,0:T(8,128)(2,1)S(1)}, bf16[4,48,128]{2,1,0:T(8,128)(2,1)S(1)}, bf16[4,48,128]{2,1,0:T(8,128)(2,1)S(1)}) custom-call(bf16[8,48,128]{2,1,0:T(8,128)(2,1)S(1)} %add_convert_fusion.one, bf16[8,48,128]{2,1,0:T(8,128)(2,1)S(1)} %collective-permute-done.6.two, bf16[8,8,48,128]{3,2,1,0:T(8,128)(2,1)S(1)} %bitcast.8, s32[8]{0:T(128)S(1)} %copy-done.24), custom_call_target="tpu_custom_call" | custom-call | flops 113246208 | bytes 1179680 | tf_op jit(solution)/shard_map/pallas_call | solution.py:44
  71.7 1.2 %collective-permute-start.7 = (bf16[4,48,128]{2,1,0:T(8,128)(2,1)S(1)}, bf16[4,48,128]{2,1,0:T(8,128)(2,1)S(1)}, u32[]{:S(2)}, u32[]{:S(2)}) collective-permute-start(bf16[4,48,128]{2,1,0:T(8,128)(2,1)S(1)} %get-tuple-element.43), channel_id=1, source_target_pairs={{0,8},{8,16},{16,24},{24,0},{1,9},{9,17},{17,25},{25,1},{2,10},{10... | collective-permute-start | bytes 147464 | tf_op jit(solution)/shard_map/ppermute | solution.py:264
  73.0 1.7 %collective-permute-start.8 = (bf16[4,48,128]{2,1,0:T(8,128)(2,1)S(1)}, bf16[4,48,128]{2,1,0:T(8,128)(2,1)S(1)}, u32[]{:S(2)}, u32[]{:S(2)}) collective-permute-start(bf16[4,48,128]{2,1,0:T(8,128)(2,1)S(1)} %get-tuple-element.44), channel_id=1, source_target_pairs={{0,24},{8,0},{16,8},{24,16},{1,25},{9,1},{17,9},{25,17},{2,26},{10... | collective-permute-start | bytes 147464 | tf_op jit(solution)/shard_map/ppermute | solution.py:264
  74.7 2.3 %copy-done.2 = bf16[8,6,384,96]{3,2,1,0:T(8,128)(2,1)S(1)} copy-done((bf16[8,6,384,96]{3,2,1,0:T(8,128)(2,1)S(1)}, bf16[8,6,384,96]{3,2,1,0:T(8,128)(2,1)}, u32[]{:S(2)}) %copy-start.2) | copy-done | bytes 3538968
  77.0 1.4 %copy-done.20 = f32[8,384,128]{2,1,0:T(8,128)S(1)} copy-done((f32[8,384,128]{2,1,0:T(8,128)S(1)}, f32[8,384,128]{2,1,0:T(8,128)}, u32[]{:S(2)}) %copy-start.20) | copy-done | bytes 1572888
  78.5 6.5 %shard_map.77 = (f32[8,384,128]{2,1,0:T(8,128)S(1)}, f32[8,384,128]{2,1,0:T(8,128)S(1)}) custom-call(f32[8,384,128]{2,1,0:T(8,128)S(1)} %copy-done.20, f32[8,384,128]{2,1,0:T(8,128)S(1)} %copy-done.12, bf16[8,384,384]{2,1,0:T(8,128)(2,1)S(1)} %copy-done.6, bf16[8,6,384,96]{3,2,1,0:T(8,128)(2,1)S(1)} %copy-done.2, ...), custom_call_target="tpu_custom_call" | custom-call | flops 528482304 | bytes 12472608 | tf_op jit(solution)/shard_map/pallas_call | solution.py:44
  85.0 1.1 %copy-done.15 = f32[8,384,128]{2,1,0:T(8,128)} copy-done((f32[8,384,128]{2,1,0:T(8,128)}, f32[8,384,128]{2,1,0:T(8,128)S(1)}, u32[]{:S(2)}) %copy-start.15) | copy-done | bytes 1572888
  86.1 1.2 %copy-done.17 = f32[8,384,128]{2,1,0:T(8,128)} copy-done((f32[8,384,128]{2,1,0:T(8,128)}, f32[8,384,128]{2,1,0:T(8,128)S(1)}, u32[]{:S(2)}) %copy-start.17) | copy-done | bytes 1572888
  87.3 2.3 %copy-done.3 = bf16[8,6,384,96]{3,2,1,0:T(8,128)(2,1)S(1)} copy-done((bf16[8,6,384,96]{3,2,1,0:T(8,128)(2,1)S(1)}, bf16[8,6,384,96]{3,2,1,0:T(8,128)(2,1)}, u32[]{:S(2)}) %copy-start.3) | copy-done | bytes 3538968
  89.6 1.4 %copy-done.16 = f32[8,384,128]{2,1,0:T(8,128)S(1)} copy-done((f32[8,384,128]{2,1,0:T(8,128)S(1)}, f32[8,384,128]{2,1,0:T(8,128)}, u32[]{:S(2)}) %copy-start.16) | copy-done | bytes 1572888
  91.1 1.4 %copy-done.18 = f32[8,384,128]{2,1,0:T(8,128)S(1)} copy-done((f32[8,384,128]{2,1,0:T(8,128)S(1)}, f32[8,384,128]{2,1,0:T(8,128)}, u32[]{:S(2)}) %copy-start.18) | copy-done | bytes 1572888
  92.5 5.3 %shard_map.78 = (f32[8,384,128]{2,1,0:T(8,128)S(1)}, bf16[8,6,96,128]{3,2,1,0:T(8,128)(2,1)S(1)}, bf16[4,96,128]{2,1,0:T(8,128)(2,1)S(1)}, bf16[4,96,128]{2,1,0:...) custom-call(f32[8,384,128]{2,1,0:T(8,128)S(1)} %copy-done.16, ...), custom_call_target="tpu_custom_call" | custom-call | flops 301989888 | bytes 12435648 | tf_op jit(solution)/shard_map/pallas_call | solution.py:44
  98.4 2.3 %collective-permute-start.10 = (bf16[4,96,128]{2,1,0:T(8,128)(2,1)S(1)}, bf16[4,96,128]{2,1,0:T(8,128)(2,1)S(1)}, u32[]{:S(2)}, u32[]{:S(2)}) collective-permute-start(bf16[4,96,128]{2,1,0:T(8,128)(2,1)S(1)} %get-tuple-element.48), channel_id=1, source_target_pairs={{0,24},{8,0},{16,8},{24,16},{1,25},{9,1},{17,9},{25,17},{2,26},{10... | collective-permute-start | bytes 294920 | tf_op jit(solution)/shard_map/ppermute | solution.py:264
  100.7 3.5 %collective-permute-start.12 = (bf16[4,96,128]{2,1,0:T(8,128)(2,1)S(1)}, bf16[4,96,128]{2,1,0:T(8,128)(2,1)S(1)}, u32[]{:S(2)}, u32[]{:S(2)}) collective-permute-start(bf16[4,96,128]{2,1,0:T(8,128)(2,1)S(1)} %get-tuple-element.50), channel_id=1, source_target_pairs={{0,7},{1,0},{2,1},{3,2},{4,3},{5,4},{6,5},{7,6},{8,15},{9,8},{10,9... | collective-permute-start | bytes 294920 | tf_op jit(solution)/shard_map/ppermute | solution.py:264
  104.3 3.3 %shard_map.79.part = f32[8,384,128]{2,1,0:T(8,128)S(1)} custom-call(bf16[8,384,128]{2,1,0:T(8,128)(2,1)S(1)} %copy-done.9, f32[8,384,128]{2,1,0:T(8,128)S(1)} %get-tuple-element.45.state, bf16[8,384,384]{2,1,0:T(8,128)(2,1)S(1)} %copy-done.6, bf16[8,6,384,96]{3,2,1,0:T(8,128)(2,1)S(1)} %bitcast.6, bf16[8,6,96,128]{3,2,1,0:T(8,128)(2,1)S(1)} %get-tuple-element.46.tr, ...), custom_call_target="tpu_custom_call" | custom-call | flops 528482304 | bytes 11010240 | tf_op jit(solution)/shard_map/pallas_call | solution.py:44
  107.6 5.4 %shard_map.80 = f32[8,384,128]{2,1,0:T(8,128)} custom-call(f32[8,384,128]{2,1,0:T(8,128)S(1)} %shard_map.79.part, f32[8,384,128]{2,1,0:T(8,128)S(1)} %get-tuple-element.45.state, bf16[8,6,384,96]{3,2,1,0:T(8,128)(2,1)S(1)} %bitcast.6, bf16[8,6,384,96]{3,2,1,0:T(8,128)(2,1)S(1)} %bitcast.6, bf16[8,384,384]{2,1,0:T(8,128)(2,1)S(1)} %copy-done.5, ...), custom_call_target="tpu_custom_call" | custom-call | flops 452984832 | bytes 14549184 | tf_op jit(solution)/shard_map/pallas_call | solution.py:44
  (67 shorter events, 9.3 us)
Async XLA Ops:
  0.0 1.7 %copy-start.4 = (bf16[8,384,384]{2,1,0:T(8,128)(2,1)S(1)}, bf16[8,384,384]{2,1,0:T(8,128)(2,1)}, u32[]{:S(2)}) copy-start(bf16[8,384,384]{2,1,0:T(8,128)(2,1)} %inv.5) | copy-start | bytes 7077892
  2.8 12.0 %copy-start.25 = (bf16[384,48]{0,1:T(8,128)(2,1)S(1)}, bf16[384,48]{0,1:T(8,128)(2,1)}, u32[]{:S(2)}) copy-start(bf16[384,48]{0,1:T(8,128)(2,1)} %param.11) | copy-start | bytes 110596
  7.4 41.8 %collective-permute-start = (bf16[4,96,128]{2,1,0:T(8,128)(2,1)S(1)}, bf16[4,96,128]{2,1,0:T(8,128)(2,1)S(1)}, u32[]{:S(2)}, u32[]{:S(2)}) collective-permute-start(bf16[4,96,128]{2,1,0:T(8,128)(2,1)S(1)} %get-tuple-element.31), channel_id=1, source_target_pairs={{0,8},{8,16},{16,24},{24,0},{1,9},{9,17},{17,25},{25,1},{2,10},{10... | collective-permute-start | bytes 294920 | tf_op jit(solution)/shard_map/ppermute | solution.py:264
  10.3 38.9 %collective-permute-start.1 = (bf16[4,96,128]{2,1,0:T(8,128)(2,1)S(1)}, bf16[4,96,128]{2,1,0:T(8,128)(2,1)S(1)}, u32[]{:S(2)}, u32[]{:S(2)}) collective-permute-start(bf16[4,96,128]{2,1,0:T(8,128)(2,1)S(1)} %get-tuple-element.32), channel_id=1, source_target_pairs={{0,24},{8,0},{16,8},{24,16},{1,25},{9,1},{17,9},{25,17},{2,26},{10... | collective-permute-start | bytes 294920 | tf_op jit(solution)/shard_map/ppermute | solution.py:264
  11.3 37.9 %collective-permute-start.2 = (bf16[4,96,128]{2,1,0:T(8,128)(2,1)S(1)}, bf16[4,96,128]{2,1,0:T(8,128)(2,1)S(1)}, u32[]{:S(2)}, u32[]{:S(2)}) collective-permute-start(bf16[4,96,128]{2,1,0:T(8,128)(2,1)S(1)} %get-tuple-element.33), channel_id=1, source_target_pairs={{0,1},{1,2},{2,3},{3,4},{4,5},{5,6},{6,7},{7,0},{8,9},{9,10},{10,1... | collective-permute-start | bytes 294920 | tf_op jit(solution)/shard_map/ppermute | solution.py:264
  11.3 37.9 %collective-permute-start.3 = (bf16[4,96,128]{2,1,0:T(8,128)(2,1)S(1)}, bf16[4,96,128]{2,1,0:T(8,128)(2,1)S(1)}, u32[]{:S(2)}, u32[]{:S(2)}) collective-permute-start(bf16[4,96,128]{2,1,0:T(8,128)(2,1)S(1)} %get-tuple-element.34), channel_id=1, source_target_pairs={{0,7},{1,0},{2,1},{3,2},{4,3},{5,4},{6,5},{7,6},{8,15},{9,8},{10,9... | collective-permute-start | bytes 294920 | tf_op jit(solution)/shard_map/ppermute | solution.py:264
  14.9 6.5 %copy-start.6 = (bf16[8,384,384]{2,1,0:T(8,128)(2,1)S(1)}, bf16[8,384,384]{2,1,0:T(8,128)(2,1)}, u32[]{:S(2)}) copy-start(bf16[8,384,384]{2,1,0:T(8,128)(2,1)} %diag.5) | copy-start | bytes 7077892
  15.0 6.5 %copy-start.23 = (s32[8,6]{1,0:T(8,128)S(1)}, s32[8,6]{1,0:T(8,128)}, u32[]{:S(2)}) copy-start(s32[8,6]{1,0:T(8,128)} %face_source.11) | copy-start | bytes 580
  15.0 6.5 %copy-start.24 = (s32[8]{0:T(128)S(1)}, s32[8]{0:T(128)}, u32[]{:S(2)}) copy-start(s32[8]{0:T(128)} %subset.7) | copy-start | bytes 100
  21.4 2.3 %copy-start = (bf16[8,6,384,96]{3,2,1,0:T(8,128)(2,1)S(1)}, bf16[8,6,384,96]{3,2,1,0:T(8,128)(2,1)}, u32[]{:S(2)}) copy-start(bf16[8,6,384,96]{3,2,1,0:T(8,128)(2,1)} %copy.18.coup.cx.cy) | copy-start | bytes 10616836
  24.9 1.4 %copy-start.11 = (f32[8,384,128]{2,1,0:T(8,128)S(1)}, f32[8,384,128]{2,1,0:T(8,128)}, u32[]{:S(2)}) copy-start(f32[8,384,128]{2,1,0:T(8,128)} %copy-done.10) | copy-start | bytes 4718596
  27.6 21.6 %copy-start.1 = (bf16[8,6,384,96]{3,2,1,0:T(8,128)(2,1)S(1)}, bf16[8,6,384,96]{3,2,1,0:T(8,128)(2,1)}, u32[]{:S(2)}) copy-start(bf16[8,6,384,96]{3,2,1,0:T(8,128)(2,1)} %copy.18.coup.cx.cy) | copy-start | bytes 10616836
  49.2 5.7 %copy-start.13 = (bf16[64,48,128]{2,1,0:T(8,128)(2,1)}, bf16[64,48,128]{2,1,0:T(8,128)(2,1)S(1)}, u32[]{:S(2)}) copy-start(bf16[64,48,128]{2,1,0:T(8,128)(2,1)S(1)} %all-gather) | copy-start | bytes 2359300
  49.2 55.1 %slice-start = ((s8[4718592]{0:T(1024)(128)(4,1)}), s8[524288]{0:T(1024)(128)(4,1)S(1)}, s32[]{:S(2)}) async-start(s8[4718592]{0:T(1024)(128)(4,1)} %bitcast.5), calls=%async_computation | async-start | bytes 1048576
  54.5 1.5 %collective-permute-start.4 = (bf16[8,48,128]{2,1,0:T(8,128)(2,1)}, bf16[8,48,128]{2,1,0:T(8,128)(2,1)S(1)}, u32[]{:S(2)}, u32[]{:S(2)}) collective-permute-start(bf16[8,48,128]{2,1,0:T(8,128)(2,1)} %get-tuple-element.37), channel_id=1, source_target_pairs={{0,1},{1,0},{2,3},{3,2},{4,5},{5,4},{6,7},{7,6},{8,9},{9,8},{10,11... | collective-permute-start | bytes 294920 | tf_op jit(solution)/shard_map/ppermute | solution.py:283
  54.9 19.8 %copy-start.12 = (f32[8,384,128]{2,1,0:T(8,128)S(1)}, f32[8,384,128]{2,1,0:T(8,128)}, u32[]{:S(2)}) copy-start(f32[8,384,128]{2,1,0:T(8,128)} %copy-done.10) | copy-start | bytes 4718596
  56.9 5.1 %collective-permute-start.5 = (bf16[8,48,128]{2,1,0:T(8,128)(2,1)S(1)}, bf16[8,48,128]{2,1,0:T(8,128)(2,1)S(1)}, u32[]{:S(2)}, u32[]{:S(2)}) collective-permute-start(bf16[8,48,128]{2,1,0:T(8,128)(2,1)S(1)} %add_convert_fusion.1), channel_id=1, source_target_pairs={{0,2},{1,3},{2,0},{3,1},{4,6},{5,7},{6,4},{7,5},{8,10},{9,11},{10,... | collective-permute-start | bytes 294920 | tf_op jit(solution)/shard_map/ppermute | solution.py:283
  62.1 7.2 %collective-permute-start.6 = (bf16[8,48,128]{2,1,0:T(8,128)(2,1)S(1)}, bf16[8,48,128]{2,1,0:T(8,128)(2,1)S(1)}, u32[]{:S(2)}, u32[]{:S(2)}) collective-permute-start(bf16[8,48,128]{2,1,0:T(8,128)(2,1)S(1)} %add_convert_fusion.one), channel_id=1, source_target_pairs={{0,4},{1,5},{2,6},{3,7},{4,0},{5,1},{6,2},{7,3},{8,12},{9,13},{10,... | collective-permute-start | bytes 294920 | tf_op jit(solution)/shard_map/ppermute | solution.py:283
  71.7 15.6 %collective-permute-start.7 = (bf16[4,48,128]{2,1,0:T(8,128)(2,1)S(1)}, bf16[4,48,128]{2,1,0:T(8,128)(2,1)S(1)}, u32[]{:S(2)}, u32[]{:S(2)}) collective-permute-start(bf16[4,48,128]{2,1,0:T(8,128)(2,1)S(1)} %get-tuple-element.43), channel_id=1, source_target_pairs={{0,8},{8,16},{16,24},{24,0},{1,9},{9,17},{17,25},{25,1},{2,10},{10... | collective-permute-start | bytes 147464 | tf_op jit(solution)/shard_map/ppermute | solution.py:264
  73.0 14.3 %collective-permute-start.8 = (bf16[4,48,128]{2,1,0:T(8,128)(2,1)S(1)}, bf16[4,48,128]{2,1,0:T(8,128)(2,1)S(1)}, u32[]{:S(2)}, u32[]{:S(2)}) collective-permute-start(bf16[4,48,128]{2,1,0:T(8,128)(2,1)S(1)} %get-tuple-element.44), channel_id=1, source_target_pairs={{0,24},{8,0},{16,8},{24,16},{1,25},{9,1},{17,9},{25,17},{2,26},{10... | collective-permute-start | bytes 147464 | tf_op jit(solution)/shard_map/ppermute | solution.py:264
  74.7 2.3 %copy-start.2 = (bf16[8,6,384,96]{3,2,1,0:T(8,128)(2,1)S(1)}, bf16[8,6,384,96]{3,2,1,0:T(8,128)(2,1)}, u32[]{:S(2)}) copy-start(bf16[8,6,384,96]{3,2,1,0:T(8,128)(2,1)} %copy.18.coup.cx.cy) | copy-start | bytes 10616836
  77.0 1.4 %copy-start.20 = (f32[8,384,128]{2,1,0:T(8,128)S(1)}, f32[8,384,128]{2,1,0:T(8,128)}, u32[]{:S(2)}) copy-start(f32[8,384,128]{2,1,0:T(8,128)} %copy-done.19) | copy-start | bytes 4718596
  78.5 8.9 %copy-start.5 = (bf16[8,384,384]{2,1,0:T(8,128)(2,1)S(1)}, bf16[8,384,384]{2,1,0:T(8,128)(2,1)}, u32[]{:S(2)}) copy-start(bf16[8,384,384]{2,1,0:T(8,128)(2,1)} %inv.5) | copy-start | bytes 7077892
  78.5 25.8 %slice-start.1 = ((s8[4718592]{0:T(1024)(128)(4,1)}), s8[4194304]{0:T(1024)(128)(4,1)S(1)}, s32[]{:S(2)}) async-start(s8[4718592]{0:T(1024)(128)(4,1)} %bitcast.5), calls=%async_computation.1 | async-start | bytes 8388608
  87.3 2.3 %copy-start.3 = (bf16[8,6,384,96]{3,2,1,0:T(8,128)(2,1)S(1)}, bf16[8,6,384,96]{3,2,1,0:T(8,128)(2,1)}, u32[]{:S(2)}) copy-start(bf16[8,6,384,96]{3,2,1,0:T(8,128)(2,1)} %copy.18.coup.cx.cy) | copy-start | bytes 10616836
  89.6 1.4 %copy-start.16 = (f32[8,384,128]{2,1,0:T(8,128)S(1)}, f32[8,384,128]{2,1,0:T(8,128)}, u32[]{:S(2)}) copy-start(f32[8,384,128]{2,1,0:T(8,128)} %copy-done.15) | copy-start | bytes 4718596
  91.1 1.4 %copy-start.18 = (f32[8,384,128]{2,1,0:T(8,128)S(1)}, f32[8,384,128]{2,1,0:T(8,128)}, u32[]{:S(2)}) copy-start(f32[8,384,128]{2,1,0:T(8,128)} %copy-done.17) | copy-start | bytes 4718596
  92.5 11.8 %copy-start.9 = (bf16[8,384,128]{2,1,0:T(8,128)(2,1)S(1)}, bf16[8,384,128]{2,1,0:T(8,128)(2,1)}, u32[]{:S(2)}) copy-start(bf16[8,384,128]{2,1,0:T(8,128)(2,1)} %rhs.5) | copy-start | bytes 2359300
  97.7 9.8 %collective-permute-start.9 = (bf16[4,96,128]{2,1,0:T(8,128)(2,1)S(1)}, bf16[4,96,128]{2,1,0:T(8,128)(2,1)S(1)}, u32[]{:S(2)}, u32[]{:S(2)}) collective-permute-start(bf16[4,96,128]{2,1,0:T(8,128)(2,1)S(1)} %get-tuple-element.47), channel_id=1, source_target_pairs={{0,8},{8,16},{16,24},{24,0},{1,9},{9,17},{17,25},{25,1},{2,10},{10... | collective-permute-start | bytes 294920 | tf_op jit(solution)/shard_map/ppermute | solution.py:264
  98.4 9.1 %collective-permute-start.10 = (bf16[4,96,128]{2,1,0:T(8,128)(2,1)S(1)}, bf16[4,96,128]{2,1,0:T(8,128)(2,1)S(1)}, u32[]{:S(2)}, u32[]{:S(2)}) collective-permute-start(bf16[4,96,128]{2,1,0:T(8,128)(2,1)S(1)} %get-tuple-element.48), channel_id=1, source_target_pairs={{0,24},{8,0},{16,8},{24,16},{1,25},{9,1},{17,9},{25,17},{2,26},{10... | collective-permute-start | bytes 294920 | tf_op jit(solution)/shard_map/ppermute | solution.py:264
  100.7 6.9 %collective-permute-start.11 = (bf16[4,96,128]{2,1,0:T(8,128)(2,1)S(1)}, bf16[4,96,128]{2,1,0:T(8,128)(2,1)S(1)}, u32[]{:S(2)}, u32[]{:S(2)}) collective-permute-start(bf16[4,96,128]{2,1,0:T(8,128)(2,1)S(1)} %get-tuple-element.49), channel_id=1, source_target_pairs={{0,1},{1,2},{2,3},{3,4},{4,5},{5,6},{6,7},{7,0},{8,9},{9,10},{10,1... | collective-permute-start | bytes 294920 | tf_op jit(solution)/shard_map/ppermute | solution.py:264
  100.7 6.9 %collective-permute-start.12 = (bf16[4,96,128]{2,1,0:T(8,128)(2,1)S(1)}, bf16[4,96,128]{2,1,0:T(8,128)(2,1)S(1)}, u32[]{:S(2)}, u32[]{:S(2)}) collective-permute-start(bf16[4,96,128]{2,1,0:T(8,128)(2,1)S(1)} %get-tuple-element.50), channel_id=1, source_target_pairs={{0,7},{1,0},{2,1},{3,2},{4,3},{5,4},{6,5},{7,6},{8,15},{9,8},{10,9... | collective-permute-start | bytes 294920 | tf_op jit(solution)/shard_map/ppermute | solution.py:264
  (9 other events, 10.3 us)

commit v2 on v0

v2 whole, which is shorter than its diff:
```python
import jax
import jax.numpy as jnp
from jax import lax
from jax.experimental import pallas as pl
from jax.experimental.pallas import tpu as pltpu
from jax.sharding import PartitionSpec as P

NVAR = 6
NP = 4
CITER = 4

relax_fine = 0.7
relax_coarse = 0.5

F32 = jnp.float32
BF16 = jnp.bfloat16
LIMIT = 24 * 1024 * 1024


def dot(a, b, precision=None):
    return jnp.dot(a, b, preferred_element_type=F32, precision=precision)


def place(e):
    return e % 2, e // 2 % 2, e // 4


def run(body, ins, outs, scratch, flops, far_ins=(), far_outs=()):
    size = sum(a.size * a.dtype.itemsize for a in list(ins) + list(outs))
    vmem = pl.BlockSpec(memory_space=pltpu.VMEM)
    smem = pl.BlockSpec(memory_space=pltpu.SMEM)
    hbm = pl.BlockSpec(memory_space=pltpu.HBM)
    ins = [
        pltpu.with_memory_space_constraint(a, pltpu.HBM) if n in far_ins else a
        for n, a in enumerate(ins)
    ]
    return pl.pallas_call(
        body,
        in_specs=[
            smem if a.dtype == jnp.int32 else hbm if n in far_ins else vmem
            for n, a in enumerate(ins)
        ],
        out_specs=[hbm if n in far_outs else vmem for n in range(len(outs))],
        out_shape=list(outs),
        scratch_shapes=scratch,
        compiler_params=pltpu.CompilerParams(vmem_limit_bytes=LIMIT),
        cost_estimate=pl.CostEstimate(flops=flops, bytes_accessed=size, transcendentals=0),
    )(*ins)


def fetch(e, pairs, sems):
    return [pltpu.make_async_copy(a.at[e], b.at[e], sems.at[n, e]) for n, (a, b) in enumerate(pairs)]


def begin(count, pairs, sems):
    for e in range(count):
        for copy in fetch(e, pairs, sems):
            copy.start()


def finish(e, pairs, sems):
    for copy in fetch(e, pairs, sems):
        copy.wait()


def read_traces(load, tmp):
    side = NP * NP
    layers = NVAR * NP
    faces = [load(0, layers * NP, NP), load(NP - 1, layers * NP, NP)]
    for g in (0, 1):
        for ii in range(NP):
            tmp[g, pl.ds(ii, layers, stride=NP), :] = load(g * NP * (NP - 1) + ii, layers, side)
        faces.append(tmp[g])
    for g in (0, 1):
        faces.append(
            jnp.concatenate(
                [load((v * NP + g * (NP - 1)) * side, side, 1) for v in range(NVAR)], axis=0
            )
        )
    return faces


def strided(ref):
    def load(start, size, stride):
        if stride == 1:
            return ref[pl.ds(start, size), :]
        return ref[pl.ds(start, size, stride=stride), :]

    return load


def emit_traces(e, state_ref, tr_ref, sides, tmp):
    faces = [f.astype(BF16) for f in read_traces(strided(state_ref.at[e]), tmp.at[e])]
    i, j, k = place(e)
    for f in (1 - i, 3 - j, 5 - k):
        tr_ref[e, f] = faces[f]
    sides[i, e // 2] = faces[i]
    sides[2 + j, i + 2 * k] = faces[2 + j]


def order(spots):
    return lax.rem(spots[3], 2) == 0, lax.rem(spots[0], 2) == 0


def pack_sends(spots, low, high, near, far):
    near[...] = jnp.where(spots, high, low)
    far[...] = jnp.where(spots, low, high)


def emit_sends(spots, sides, sends):
    for axis, even in enumerate(order(spots)):
        pack_sends(even, sides[2 * axis], sides[2 * axis + 1], sends[2 * axis], sends[2 * axis + 1])


def masked(face_source, e, f, value):
    return jnp.where(face_source[e, f] > 0, value, jnp.zeros_like(value))


def inner_faces(e):
    i, j, k = place(e)
    return (1 - i, e ^ 1, i), (3 - j, e ^ 2, 2 + j), (5 - k, e ^ 4, 4 + k)


def stack(parts, rows):
    have = sum(part.shape[0] for part in parts)
    if have < rows:
        parts = parts + [jnp.zeros((rows - have, parts[0].shape[1]), parts[0].dtype)]
    return jnp.concatenate(parts, axis=0)


def came(even, from_near, from_far, upper, at):
    first, second = (from_near, from_far) if upper else (from_far, from_near)
    return jnp.where(even, first[at], second[at])


def pick(e, halo, face_source, spots):
    i, j, k = place(e)
    even_x, even_y = order(spots)
    return [
        masked(face_source, e, i, came(even_x, halo[0], halo[1], i, e // 2)),
        masked(face_source, e, 2 + j, came(even_y, halo[2], halo[3], j, i + 2 * k)),
    ]


def first_body(rhs_far, inv_far, spots, first, tr, rhs, inv, s0, s1, s2, s3, tmp, sides, sems):
    pairs = ((inv_far, inv), (rhs_far, rhs))
    count = rhs.shape[0]
    begin(count, pairs, sems)
    for e in range(count):
        finish(e, pairs, sems)
        first[e] = relax_fine * dot(inv[e], rhs[e])
        emit_traces(e, first, tr, sides, tmp)
    emit_sends(spots, sides, (s0, s1, s2, s3))


def local_body(
    rhs, state, diag_far, coup_far, tr, pt, face_source, subset,
    acc, mats, oper, outer, pf, prolong,
    diag, coup, wide, tmp, msum, sems,
):
    coarse, dof = pt.shape
    count, _, cols = acc.shape
    near_rows = outer.shape[2]
    pairs = ((diag_far, diag), (coup_far, coup))
    begin(count, pairs, sems)
    wide[...] = stack([pt[...].astype(F32)], cols).T
    for f, face in enumerate(read_traces(strided(wide), tmp)):
        pf[f] = face.astype(BF16)
    base = wide[...].astype(BF16)
    prolong[...] = base
    msum[...] = jnp.zeros_like(msum)
    for e in range(count):
        i, j, k = place(e)
        inner = inner_faces(e)
        finish(e, pairs, sems)
        oper[e, :, 0:dof] = diag[e]
        oper[e, :, dof : 2 * dof] = stack([coup[e, f] for f, near, face in inner], dof).T
        outer[e] = stack([coup[e, i], coup[e, 2 + j]], near_rows).T
    stiffs = []
    for e in range(count):
        i, j, k = place(e)
        inner = inner_faces(e)
        values = [state[e].astype(BF16)] + [
            masked(face_source, e, f, tr[near, face]) for f, near, face in inner
        ]
        bases = [base] + [masked(face_source, e, f, pf[face]) for f, near, face in inner]
        both = jnp.concatenate([stack(values, 2 * dof), stack(bases, 2 * dof)], axis=1)
        total = dot(oper[e], both)
        acc[e] = rhs[e].astype(F32) - total[:, 0:cols]
        far = stack(
            [masked(face_source, e, i, pf[1 - i]), masked(face_source, e, 2 + j, pf[3 - j])],
            near_rows,
        )
        stiffs.append((total[:, cols:] + dot(outer[e], far)).astype(BF16))
    blocks = [dot(pt[...], stiff) for stiff in stiffs]
    lane = lax.broadcasted_iota(jnp.int32, (coarse, cols), 1)
    one = jnp.where(lane == coarse, 1.0, 0.0)
    for e in range(count):
        msum[subset[e]] += blocks[e] + one
    for s in range(mats.shape[0]):
        block = msum[s]
        low = jnp.where(lane == coarse, 0.0, block)[coarse // 2 :]
        mats[s] = block[: coarse // 2] + pltpu.roll(low, cols // 2, 1)


def restrict_body(part, outer, xm, xp, ym, yp, pt, mats, face_source, subset, spots, resid, keep, give, total):
    count = part.shape[0]
    coarse = pt.shape[0]
    total[...] = jnp.zeros_like(total)
    for e in range(count):
        far = stack(pick(e, (xm, xp, ym, yp), face_source, spots), outer.shape[2])
        resid[e] = part[e] - dot(outer[e], far)
    shares = [dot(pt[...], resid[e].astype(BF16)) for e in range(count)]
    for e in range(count):
        total[subset[e]] += shares[e]
    row = lax.broadcasted_iota(jnp.int32, (count, mats.shape[2]), 0)
    lane = lax.broadcasted_iota(jnp.int32, row.shape, 1)
    half = lax.rem(spots[0], 2)
    mine = (lane >= row.shape[1] // 2) == (half == 1)
    names = jnp.zeros(row.shape, F32)
    for e in range(count):
        names = jnp.where(mine & (row == e), subset[e].astype(F32), names)
    share = keep.shape[0]
    for which, ref in ((half, keep), (1 - half, give)):
        for s in range(share):
            own = jnp.where(lax.div(spots[0], 2) == s, names, 0.0)
            ref[s, 0:coarse] = total[which * share + s].astype(BF16)
            rest = stack([mats[which * share + s], own], ref.shape[1] - coarse)
            ref[s, coarse:] = rest.astype(BF16)


def split(value):
    high = value.astype(BF16)
    return high, (value - high.astype(F32)).astype(BF16)


def coarse_body(one, two, spots, y_own, names):
    groups, coarse, cols = y_own.shape
    half = coarse // 2
    rights, blocks, thetas, ys = [], [], [], []
    for s in range(groups):
        both = one[s].astype(F32) + two[s].astype(F32)
        right = both[0:coarse]
        packed = both[coarse : coarse + half]
        block = jnp.concatenate([packed, pltpu.roll(packed, cols // 2, 1)], axis=0)
        theta = relax_coarse / jnp.maximum(packed[:, coarse : coarse + 1], 1.0)
        theta = jnp.concatenate([theta, theta], axis=0)
        high, low = split(block[:, 0:coarse])
        rights.append(right)
        blocks.append(jnp.concatenate([high, high, low], axis=1))
        thetas.append(theta)
        ys.append(theta * right)
    for sweep in range(CITER - 1):
        sides = []
        for s in range(groups):
            high, low = split(ys[s])
            sides.append(jnp.concatenate([high, low, high], axis=0))
        applied = [dot(blocks[s], sides[s]) for s in range(groups)]
        ys = [ys[s] + thetas[s] * (rights[s] - applied[s]) for s in range(groups)]
    for s in range(groups):
        y_own[s] = ys[s].astype(BF16)
    start = coarse + half
    count = names.shape[1]
    lane = lax.broadcasted_iota(jnp.int32, (count, cols), 1)
    for side in (0, 1):
        slot = lax.div(spots[1 + side], 2)
        far = one[slot].astype(F32) + two[slot].astype(F32)
        mine = (lane >= cols // 2) == (lax.rem(spots[1 + side], 2) == 1)
        far = jnp.where(mine, far[start : start + count], 0.0)
        names[side] = far + pltpu.roll(far, cols // 2, 1)


def choose_body(y_own, y_other, subset, spots, y_all, near, far, sides):
    share = y_own.shape[0]
    half = lax.rem(spots[0], 2)
    for s in range(share):
        y_all[half * share + s] = y_own[s]
        y_all[(1 - half) * share + s] = y_other[s]
    for e in range(subset.shape[0]):
        sides[e % 2, e // 2] = y_all[subset[e]]
    pack_sends(order(spots)[0], sides[0], sides[1], near, far)


def second_body(resid, state, oper, outer, y_all, prolong, pf, names, face_source, subset, acc, second):
    coarse = y_all.shape[1]
    count, dof, _ = resid.shape
    inside, outside = [], []
    for e in range(count):
        i, j, k = place(e)
        step = dot(prolong[:, 0:coarse], y_all[subset[e]])
        second[e] = state[e] + step
        values = [step.astype(BF16)]
        for f, near, face in inner_faces(e):
            rows = dot(pf[face, :, 0:coarse], y_all[subset[near]]).astype(BF16)
            values.append(masked(face_source, e, f, rows))
        name = names[j, pl.ds(e ^ 2, 1), :]
        y_far = jnp.zeros(y_all.shape[1:], F32)
        for s in range(y_all.shape[0]):
            y_far = jnp.where(name == float(s), y_all[s].astype(F32), y_far)
        rows = dot(pf[3 - j, :, 0:coarse], y_far.astype(BF16)).astype(BF16)
        far = [jnp.zeros_like(rows), masked(face_source, e, 2 + j, rows)]
        inside.append(stack(values, 2 * dof))
        outside.append(stack(far, outer.shape[2]))
    for e in range(count):
        acc[e] = resid[e] - (dot(oper[e], inside[e]) + dot(outer[e], outside[e]))


def smooth_body(part, second, outer, inv, y0, y1, pf, face_source, spots, state, tr, s0, s1, s2, s3, tmp, sides, res):
    coarse = y0.shape[1]
    count = part.shape[0]
    rows = []
    for e in range(count):
        i = e % 2
        y_far = came(order(spots)[0], y0, y1, i, e // 2)
        value = dot(pf[1 - i, :, 0:coarse], y_far).astype(BF16)
        rows.append(stack([masked(face_source, e, i, value)], outer.shape[2]))
    for e in range(count):
        res[e] = (part[e] - dot(outer[e], rows[e])).astype(BF16)
    for e in range(count):
        state[e] = second[e] + relax_fine * dot(inv[e], res[e])
        emit_traces(e, state, tr, sides, tmp)
    emit_sends(spots, sides, (s0, s1, s2, s3))


def inner_body(rhs, state, oper, tr, face_source, acc):
    dof = state.shape[1]
    for e in range(state.shape[0]):
        values = [state[e].astype(BF16)] + [
            masked(face_source, e, f, tr[near, face]) for f, near, face in inner_faces(e)
        ]
        acc[e] = rhs[e].astype(F32) - dot(oper[e], stack(values, 2 * dof))


def final_body(part, state, outer, inv, xm, xp, ym, yp, face_source, spots, out_far, res, out, sems):
    count = state.shape[0]
    pairs = ((out, out_far),)
    for e in range(count):
        far = stack(pick(e, (xm, xp, ym, yp), face_source, spots), outer.shape[2])
        res[e] = (part[e] - dot(outer[e], far)).astype(BF16)
    for e in range(count):
        out[e] = state[e] + relax_fine * dot(inv[e], res[e])
        fetch(e, pairs, sems)[0].start()
    for e in range(count):
        finish(e, pairs, sems)


def swap(value, axis, start):
    count = lax.axis_size(axis)
    pairs = [(i % count, (i + 1) % count) for i in range(start, count, 2)]
    return lax.ppermute(value, axis, pairs + [(b, a) for a, b in pairs])


def exchange(sends):
    x0, x1, y0, y1 = sends
    x1 = swap(x1, "gx", 1)
    y1 = swap(y1, "gy", 1)
    x0 = swap(x0, "gx", 0)
    return x0, x1, swap(y0, "gy", 0), y1


def plus(one, two):
    return (one.astype(F32) + two.astype(F32)).astype(BF16)


def row_sum(keep, give):
    count = lax.axis_size("gy")
    one, two = keep, swap(give, "gy", 0)
    if count & (count - 1):
        part = plus(one, two)
        for step in range(2, count, 2):
            one, two = plus(one, two) if step > 2 else part, lax.ppermute(
                part, "gy", [(i, (i + step) % count) for i in range(count)]
            )
        return one, two
    step = 2
    while step < count:
        one = plus(one, two)
        two = lax.ppermute(one, "gy", [(i, i ^ step) for i in range(count)])
        step *= 2
    return one, two


def on_device(rhs, diag_blocks, inverse_blocks, couplings, prolong, face_source, subset):
    elements, dof, cols = rhs.shape
    fdof = couplings.shape[3]
    coarse = prolong.shape[1]
    groups = lax.axis_size("gy")
    half = elements // 2
    shape = jax.ShapeDtypeStruct
    state_s = shape((elements, dof, cols), F32)
    tr_s = shape((elements, 6, fdof, cols), BF16)
    sends_s = [shape((half, fdof, cols), BF16)] * 4
    y_s = shape((half, coarse, cols), BF16)
    near_rows = -(-2 * fdof // cols) * cols
    message = -(-(coarse + coarse // 2 + elements) // 16) * 16
    tmps = pltpu.VMEM((elements, 2, fdof, cols), F32)
    sides = pltpu.VMEM((4, half, fdof, cols), BF16)
    state_b = pltpu.VMEM((elements, dof, cols), BF16)
    square_b = pltpu.VMEM((elements, dof, dof), BF16)
    apply_flops = 2 * elements * dof * cols * (dof + 3 * fdof)
    inv_flops = 2 * elements * dof * dof * cols
    far_flops = 4 * elements * dof * fdof * cols
    coup = jnp.swapaxes(couplings, 2, 3)
    pt = prolong.T

    me = lax.axis_index("gy")
    spots = jnp.stack(
        [me, (me + groups - 1) % groups, (me + 1) % groups, lax.axis_index("gx")]
    ).astype(jnp.int32)
    first, tr, rhs, inv, *sends = run(
        first_body,
        (rhs, inverse_blocks, spots),
        [state_s, tr_s, shape(rhs.shape, BF16), shape(inverse_blocks.shape, BF16)] + sends_s,
        [tmps, sides, pltpu.SemaphoreType.DMA((2, elements))],
        inv_flops,
        far_ins=(0, 1),
    )
    xm, xp, ym, yp = exchange(sends)
    acc, mats, oper, outer, pf, wide = run(
        local_body,
        (rhs, first, diag_blocks, coup, tr, pt, face_source, subset),
        [
            state_s,
            shape((groups, coarse // 2, cols), F32),
            shape((elements, dof, 2 * dof), BF16),
            shape((elements, dof, near_rows), BF16),
            shape((6, fdof, cols), BF16),
            shape((dof, cols), BF16),
        ],
        [
            square_b,
            pltpu.VMEM(coup.shape, BF16),
            pltpu.VMEM((dof, cols), F32),
            pltpu.VMEM((2, fdof, cols), F32),
            pltpu.VMEM((groups, coarse, cols), F32),
            pltpu.SemaphoreType.DMA((2, elements)),
        ],
        2 * apply_flops,
        far_ins=(2, 3),
    )
    resid, keep, give = run(
        restrict_body,
        (acc, outer, xm, xp, ym, yp, pt, mats, face_source, subset, spots),
        [state_s] + [shape((groups // 2, message, cols), BF16)] * 2,
        [pltpu.VMEM((groups, coarse, cols), F32)],
        far_flops,
    )
    one, two = row_sum(keep, give)
    y_own, names = run(
        coarse_body,
        (one, two, spots),
        [shape((groups // 2, coarse, cols), BF16), shape((2, elements, cols), F32)],
        [],
        3 * groups * coarse * coarse * cols * CITER,
    )
    y_all, y0, y1 = run(
        choose_body,
        (y_own, swap(y_own, "gy", 0), subset, spots),
        [shape((groups, coarse, cols), BF16), y_s, y_s],
        [pltpu.VMEM((2, half, coarse, cols), BF16)],
        0,
    )
    y1 = swap(y1, "gx", 1)
    y0 = swap(y0, "gx", 0)
    acc, second = run(
        second_body,
        (resid, first, oper, outer, y_all, wide, pf, names, face_source, subset),
        [state_s, state_s],
        [],
        apply_flops,
    )
    state, tr, *sends = run(
        smooth_body,
        (acc, second, outer, inv, y0, y1, pf, face_source, spots),
        [state_s, tr_s] + sends_s,
        [tmps, sides, state_b],
        inv_flops,
    )
    xm, xp, ym, yp = exchange(sends)
    acc = run(inner_body, (rhs, state, oper, tr, face_source), [state_s], [], apply_flops)[0]
    return run(
        final_body,
        (acc, state, outer, inv, xm, xp, ym, yp, face_source, spots),
        [state_s],
        [state_b, pltpu.VMEM((elements, dof, cols), F32), pltpu.SemaphoreType.DMA((1, elements))],
        inv_flops + far_flops,
        far_outs=(0,),
    )[0]


def solution(mesh):
    return jax.shard_map(
        on_device,
        mesh=mesh,
        in_specs=(
            P(("gx", "gy"), None, None),
            P(("gx", "gy"), None, None),
            P(("gx", "gy"), None, None),
            P(("gx", "gy"), None, None, None),
            P(),
            P(("gx", "gy"), None),
            P(("gx", "gy")),
        ),
        out_specs=P(("gx", "gy"), None, None),
        check_vma=False,
    )
```

time: 175 us -> 54.2 us (0.31)
  matrix products: 44.4 us -> 0 us
  local copies, waits for them, and re-layouts: 42.4 us -> 0.01 us
  blocking collectives: 30.9 us -> 0 us
  Pallas kernels: 0 us -> 22.4 us
  between operations: 14.5 us -> 0.14 us
  other arithmetic: 5.22 us -> 0.13 us
  waiting for transfers between devices: 22.6 us -> 17.7 us
    dot_general x17 -> x0, matrix products: 44.4 us -> none  [the longest x2 13.4 us: on_device(): jnp.einsum('edk,ekr->edr', inverse_blocks, resid.astype(jnp.bfloat16), pr...]
    pallas_call x0 -> x9, Pallas kernels: none -> 22.4 us  [run(): pl.pallas_call(body, in_specs=[smem if a.dtype == jnp.int32 else hbm if n...]
    unnamed x48 -> x6, local copies, waits for them, and re-layouts: 20.3 us -> 0.01 us
    unnamed x1 -> x0, blocking collectives: 17 us -> none
    all_gather x1 -> x0, blocking collectives: 13.9 us -> none  [on_device(): coarse_all = lax.all_gather(coarse_own, 'gy', axis=0, tiled=True)]
    reduce_scatter x2 -> x0, waiting for transfers between devices: 11.4 us -> none  [the longest x1 11.4 us: on_device(): lax.psum_scatter(part_rhs.astype(jnp.bfloat16), 'gy', scatter_dimension=0...]
    slice x12 -> x0, local copies, waits for them, and re-layouts: 9.62 us -> none  [the longest x9 7.65 us: face_trace(): lax.index_in_dim(volume, (NP - 1) * (face_id % 2), 4 - face_id // 2, keep...]
    another operation x29 -> x0, local copies, waits for them, and re-layouts: 7.35 us -> none  [the longest x2 2.25 us: on_device(): jnp.stack([face_trace(prolong[None], face_id ^ 1)[0] for face_id in range...]
  transfers between devices with their start and end apart: 14 -> 14, of which waited for: 6 -> 8; matrix products, arithmetic and copies ran while one was open for 18% -> 0% of each run, Pallas kernels for 0% -> 19%
where the time goes in v2:
time: 54.2 us; the launch traced here: 54 us
  Pallas kernels  22.4 us (41%)
  waiting for transfers between devices  17.7 us (33%)
  starting transfers between devices  13.7 us (25%)
    pallas_call x9, Pallas kernels, run(): pl.pallas_call(body, in_specs=[smem if a.dtype == jnp.int32 else hbm if n...  22.4 us
    ppermute x12, starting transfers between devices, swap(): return lax.ppermute(value, axis, pairs + [(b, a) for a, b in pairs])  13.2 us
    ppermute x2, waiting for transfers between devices, row_sum(): two = lax.ppermute(one, 'gy', [(i, i ^ step) for i in range(count)])  10.4 us
    ppermute x12, waiting for transfers between devices, swap(): return lax.ppermute(value, axis, pairs + [(b, a) for a, b in pairs])  7.24 us
  transfers between devices with their start and end apart: 14, of which 8 were waited for; matrix products, arithmetic and copies ran while one was open for 0% of the time, Pallas kernels for 19%

profile of v2, /device:TPU:0, one launch (start us, length us, event | category | flops | bytes accessed | tf_op | source)
XLA Modules:
  0.0 54.0 jit_solution(16297855487288101107)
XLA Ops:
  0.0 0.1 pad_add_fusion.spots
  0.1 4.0 %shard_map.73 = (f32[8,384,128]{2,1,0:T(8,128)S(1)}, bf16[8,6,96,128]{3,2,1,0:T(8,128)(2,1)S(1)}, bf16[8,384,128]{2,1,0:T(8,128)(2,1)S(1)}, bf16[8,384,384]{2,1,...) custom-call(bf16[8,384,128]{2,1,0:T(8,128)(2,1)} %rhs_far.1, ...), custom_call_target="tpu_custom_call" | custom-call | flops 301989888 | bytes 9437200 | tf_op jit(solution)/shard_map/pallas_call | solution.py:37
  4.1 3.0 %collective-permute-start = (bf16[4,96,128]{2,1,0:T(8,128)(2,1)S(1)}, bf16[4,96,128]{2,1,0:T(8,128)(2,1)S(1)}, u32[]{:S(2)}, u32[]{:S(2)}) collective-permute-start(bf16[4,96,128]{2,1,0:T(8,128)(2,1)S(1)} %get-tuple-element.40), channel_id=1, source_target_pairs={{0,8},{16,24},{8,0},{24,16},{1,9},{17,25},{9,1},{25,17},{2,10},{18... | collective-permute-start | bytes 294920 | tf_op jit(solution)/shard_map/ppermute | solution.py:350
  7.1 1.5 %collective-permute-start.1 = (bf16[4,96,128]{2,1,0:T(8,128)(2,1)S(1)}, bf16[4,96,128]{2,1,0:T(8,128)(2,1)S(1)}, u32[]{:S(2)}, u32[]{:S(2)}) collective-permute-start(bf16[4,96,128]{2,1,0:T(8,128)(2,1)S(1)} %get-tuple-element.41), channel_id=1, source_target_pairs={{8,16},{24,0},{16,8},{0,24},{9,17},{25,1},{17,9},{1,25},{10,18},{2... | collective-permute-start | bytes 294920 | tf_op jit(solution)/shard_map/ppermute | solution.py:350
  8.6 0.0 collective-permute-start.2
  8.6 3.7 %collective-permute-start.3 = (bf16[4,96,128]{2,1,0:T(8,128)(2,1)S(1)}, bf16[4,96,128]{2,1,0:T(8,128)(2,1)S(1)}, u32[]{:S(2)}, u32[]{:S(2)}) collective-permute-start(bf16[4,96,128]{2,1,0:T(8,128)(2,1)S(1)} %get-tuple-element.43), channel_id=1, source_target_pairs={{1,2},{3,4},{5,6},{7,0},{2,1},{4,3},{6,5},{0,7},{9,10},{11,12},{13... | collective-permute-start | bytes 294920 | tf_op jit(solution)/shard_map/ppermute | solution.py:350
  12.3 5.5 %shard_map.74 = (f32[8,384,128]{2,1,0:T(8,128)S(1)}, f32[8,24,128]{2,1,0:T(8,128)S(1)}, bf16[8,384,768]{2,1,0:T(8,128)(2,1)S(1)}, bf16[8,384,256]{2,1,0:T(8,128)...) custom-call(bf16[8,384,128]{2,1,0:T(8,128)(2,1)S(1)} %get-tuple-element.35.rhs, ...), custom_call_target="tpu_custom_call" | custom-call | flops 1056964608 | bytes 17682656 | tf_op jit(solution)/shard_map/pallas_call | solution.py:37
  17.9 0.0 collective-permute-done.1.xp
  17.9 1.4 %shard_map.75 = (f32[8,384,128]{2,1,0:T(8,128)S(1)}, bf16[4,80,128]{2,1,0:T(8,128)(2,1)S(1)}, bf16[4,80,128]{2,1,0:T(8,128)(2,1)S(1)}) custom-call(f32[8,384,128]{2,1,0:T(8,128)S(1)} %get-tuple-element.38.part, bf16[8,384,256]{2,1,0:T(8,128)(2,1)S(1)} %get-tuple-element.39.outer, bf16[4,96,128]{2,1,0:T(8,128)(2,1)S(1)} %collective-permute-done.xm, ...), custom_call_target="tpu_custom_call" | custom-call | flops 150994944 | bytes 5411056 | tf_op jit(solution)/shard_map/pallas_call | solution.py:37
  19.3 0.1 collective-permute-start.4
  19.4 1.3 %collective-permute-done.4 = bf16[4,80,128]{2,1,0:T(8,128)(2,1)S(1)} collective-permute-done((bf16[4,80,128]{2,1,0:T(8,128)(2,1)S(1)}, bf16[4,80,128]{2,1,0:T(8,128)(2,1)S(1)}, u32[]{:S(2)}, u32[]{:S(2)}) %collective-permute-start.4) | collective-permute-done | bytes 81952 | tf_op jit(solution)/shard_map/ppermute | solution.py:350
  20.7 0.1 collective-permute-start.5
  20.8 4.5 %collective-permute-done.5 = bf16[4,80,128]{2,1,0:T(8,128)(2,1)S(1)} collective-permute-done((bf16[4,80,128]{2,1,0:T(8,128)(2,1)S(1)}, bf16[4,80,128]{2,1,0:T(8,128)(2,1)S(1)}, u32[]{:S(2)}, u32[]{:S(2)}) %collective-permute-start.5) | collective-permute-done | bytes 81952 | tf_op jit(solution)/shard_map/ppermute | solution.py:378
  25.3 0.5 collective-permute-start.6
  25.7 5.9 %collective-permute-done.6.two = bf16[4,80,128]{2,1,0:T(8,128)(2,1)S(1)} collective-permute-done((bf16[4,80,128]{2,1,0:T(8,128)(2,1)S(1)}, bf16[4,80,128]{2,1,0:T(8,128)(2,1)S(1)}, u32[]{:S(2)}, u32[]{:S(2)}) %collective-permute-start.6) | collective-permute-done | bytes 81952 | tf_op jit(solution)/shard_map/ppermute | solution.py:378
  31.7 1.1 %shard_map.76 = (bf16[4,48,128]{2,1,0:T(8,128)(2,1)S(1)}, f32[2,8,128]{2,1,0:T(8,128)S(1)}) custom-call(bf16[4,80,128]{2,1,0:T(8,128)(2,1)S(1)} %add_convert_fusion.one, bf16[4,80,128]{2,1,0:T(8,128)(2,1)S(1)} %collective-permute-done.6.two, s32[4]{0:T(128)S(1)} %pad_add_fusion.spots), custom_call_target="tpu_custom_call" | custom-call | flops 28311552 | bytes 221200 | tf_op jit(solution)/shard_map/pallas_call | solution.py:37
  32.8 0.1 collective-permute-start.7
  32.9 1.2 %collective-permute-done.7.y_other = bf16[4,48,128]{2,1,0:T(8,128)(2,1)S(1)} collective-permute-done((bf16[4,48,128]{2,1,0:T(8,128)(2,1)S(1)}, bf16[4,48,128]{2,1,0:T(8,128)(2,1)S(1)}, u32[]{:S(2)}, u32[]{:S(2)}) %collective-permute-start.7) | collective-permute-done | bytes 49184 | tf_op jit(solution)/shard_map/ppermute | solution.py:350
  34.1 0.6 %shard_map.77 = (bf16[8,48,128]{2,1,0:T(8,128)(2,1)S(1)}, bf16[4,48,128]{2,1,0:T(8,128)(2,1)S(1)}, bf16[4,48,128]{2,1,0:T(8,128)(2,1)S(1)}) custom-call(bf16[4,48,128]{2,1,0:T(8,128)(2,1)S(1)} %get-tuple-element.49.y_own, bf16[4,48,128]{2,1,0:T(8,128)(2,1)S(1)} %collective-permute-done.7.y_other, s32[8]{0:T(128)S(1)} %copy-done.2, s32[4]{0:T(128)S(1)} %pad_add_fusion.spots), custom_call_target="tpu_custom_call" | custom-call | bytes 294960 | tf_op jit(solution)/shard_map/pallas_call | solution.py:37
  34.7 1.5 %collective-permute-start.8 = (bf16[4,48,128]{2,1,0:T(8,128)(2,1)S(1)}, bf16[4,48,128]{2,1,0:T(8,128)(2,1)S(1)}, u32[]{:S(2)}, u32[]{:S(2)}) collective-permute-start(bf16[4,48,128]{2,1,0:T(8,128)(2,1)S(1)} %get-tuple-element.57), channel_id=1, source_target_pairs={{0,8},{16,24},{8,0},{24,16},{1,9},{17,25},{9,1},{25,17},{2,10},{18... | collective-permute-start | bytes 147464 | tf_op jit(solution)/shard_map/ppermute | solution.py:350
  36.3 0.5 collective-permute-start.9
  36.7 2.8 %shard_map.78 = (f32[8,384,128]{2,1,0:T(8,128)S(1)}, f32[8,384,128]{2,1,0:T(8,128)S(1)}) custom-call(f32[8,384,128]{2,1,0:T(8,128)S(1)} %get-tuple-element.45.resid, f32[8,384,128]{2,1,0:T(8,128)S(1)} %get-tuple-element.36.state, bf16[8,384,768]{2,1,0:T(8,128)(2,1)S(1)} %get-tuple-element.46.oper, bf16[8,384,256]{2,1,0:T(8,128)(2,1)S(1)} %get-tuple-element.39.outer, ...), custom_call_target="tpu_custom_call" | custom-call | flops 528482304 | bytes 12935392 | tf_op jit(solution)/shard_map/pallas_call | solution.py:37
  39.6 1.7 %collective-permute-done.9.y1 = bf16[4,48,128]{2,1,0:T(8,128)(2,1)S(1)} collective-permute-done((bf16[4,48,128]{2,1,0:T(8,128)(2,1)S(1)}, bf16[4,48,128]{2,1,0:T(8,128)(2,1)S(1)}, u32[]{:S(2)}, u32[]{:S(2)}) %collective-permute-start.9) | collective-permute-done | bytes 49184 | tf_op jit(solution)/shard_map/ppermute | solution.py:350
  41.2 2.3 %shard_map.79 = (f32[8,384,128]{2,1,0:T(8,128)S(1)}, bf16[8,6,96,128]{3,2,1,0:T(8,128)(2,1)S(1)}, bf16[4,96,128]{2,1,0:T(8,128)(2,1)S(1)}, bf16[4,96,128]{2,1,0:...) custom-call(f32[8,384,128]{2,1,0:T(8,128)S(1)} %get-tuple-element.54.part, ...), custom_call_target="tpu_custom_call" | custom-call | flops 301989888 | bytes 10469584 | tf_op jit(solution)/shard_map/pallas_call | solution.py:37
  43.5 0.6 %collective-permute-start.10 = (bf16[4,96,128]{2,1,0:T(8,128)(2,1)S(1)}, bf16[4,96,128]{2,1,0:T(8,128)(2,1)S(1)}, u32[]{:S(2)}, u32[]{:S(2)}) collective-permute-start(bf16[4,96,128]{2,1,0:T(8,128)(2,1)S(1)} %get-tuple-element.61), channel_id=1, source_target_pairs={{0,8},{16,24},{8,0},{24,16},{1,9},{17,25},{9,1},{25,17},{2,10},{18... | collective-permute-start | bytes 294920 | tf_op jit(solution)/shard_map/ppermute | solution.py:350
  44.1 1.4 %collective-permute-start.11 = (bf16[4,96,128]{2,1,0:T(8,128)(2,1)S(1)}, bf16[4,96,128]{2,1,0:T(8,128)(2,1)S(1)}, u32[]{:S(2)}, u32[]{:S(2)}) collective-permute-start(bf16[4,96,128]{2,1,0:T(8,128)(2,1)S(1)} %get-tuple-element.62), channel_id=1, source_target_pairs={{8,16},{24,0},{16,8},{0,24},{9,17},{25,1},{17,9},{1,25},{10,18},{2... | collective-permute-start | bytes 294920 | tf_op jit(solution)/shard_map/ppermute | solution.py:350
  45.6 0.8 %collective-permute-start.13 = (bf16[4,96,128]{2,1,0:T(8,128)(2,1)S(1)}, bf16[4,96,128]{2,1,0:T(8,128)(2,1)S(1)}, u32[]{:S(2)}, u32[]{:S(2)}) collective-permute-start(bf16[4,96,128]{2,1,0:T(8,128)(2,1)S(1)} %get-tuple-element.64), channel_id=1, source_target_pairs={{1,2},{3,4},{5,6},{7,0},{2,1},{4,3},{6,5},{0,7},{9,10},{11,12},{13... | collective-permute-start | bytes 294920 | tf_op jit(solution)/shard_map/ppermute | solution.py:350
  46.3 2.0 %shard_map.80.part = f32[8,384,128]{2,1,0:T(8,128)S(1)} custom-call(bf16[8,384,128]{2,1,0:T(8,128)(2,1)S(1)} %get-tuple-element.35.rhs, f32[8,384,128]{2,1,0:T(8,128)S(1)} %get-tuple-element.59.state, bf16[8,384,768]{2,1,0:T(8,128)(2,1)S(1)} %get-tuple-element.46.oper, bf16[8,6,96,128]{3,2,1,0:T(8,128)(2,1)S(1)} %get-tuple-element.60.tr, s32[8,6]{1,0:T(8,128)S(1)} %copy-done), custom_call_target="tpu_custom_call" | custom-call | flops 528482304 | bytes 9830592 | tf_op jit(solution)/shard_map/pallas_call | solution.py:37
  48.3 0.1 collective-permute-done.10.xm
  48.4 1.3 %collective-permute-done.11.xp = bf16[4,96,128]{2,1,0:T(8,128)(2,1)S(1)} collective-permute-done((bf16[4,96,128]{2,1,0:T(8,128)(2,1)S(1)}, bf16[4,96,128]{2,1,0:T(8,128)(2,1)S(1)}, u32[]{:S(2)}, u32[]{:S(2)}) %collective-permute-start.11) | collective-permute-done | bytes 98336 | tf_op jit(solution)/shard_map/ppermute | solution.py:350
  49.7 1.8 %collective-permute-done.13.yp = bf16[4,96,128]{2,1,0:T(8,128)(2,1)S(1)} collective-permute-done((bf16[4,96,128]{2,1,0:T(8,128)(2,1)S(1)}, bf16[4,96,128]{2,1,0:T(8,128)(2,1)S(1)}, u32[]{:S(2)}, u32[]{:S(2)}) %collective-permute-start.13) | collective-permute-done | bytes 98336 | tf_op jit(solution)/shard_map/ppermute | solution.py:350
  51.4 2.6 %shard_map.81 = f32[8,384,128]{2,1,0:T(8,128)} custom-call(f32[8,384,128]{2,1,0:T(8,128)S(1)} %shard_map.80.part, f32[8,384,128]{2,1,0:T(8,128)S(1)} %get-tuple-element.59.state, bf16[8,384,256]{2,1,0:T(8,128)(2,1)S(1)} %get-tuple-element.39.outer, bf16[8,384,384]{2,1,0:T(8,128)(2,1)S(1)} %get-tuple-element.56.inv, ...), custom_call_target="tpu_custom_call" | custom-call | flops 452984832 | bytes 9044176 | tf_op jit(solution)/shard_map/pallas_call | solution.py:37
  (14 shorter events, 0.1 us)
Async XLA Ops:
  0.1 12.3 %copy-start = (s32[8,6]{1,0:T(8,128)S(1)}, s32[8,6]{1,0:T(8,128)}, u32[]{:S(2)}) copy-start(s32[8,6]{1,0:T(8,128)} %face_source.11) | copy-start | bytes 580
  0.1 12.3 %copy-start.1 = (bf16[384,48]{0,1:T(8,128)(2,1)S(1)}, bf16[384,48]{0,1:T(8,128)(2,1)}, u32[]{:S(2)}) copy-start(bf16[384,48]{0,1:T(8,128)(2,1)} %param.11) | copy-start | bytes 110596
  0.1 12.3 %copy-start.2 = (s32[8]{0:T(128)S(1)}, s32[8]{0:T(128)}, u32[]{:S(2)}) copy-start(s32[8]{0:T(128)} %subset.7) | copy-start | bytes 100
  4.1 13.7 %collective-permute-start = (bf16[4,96,128]{2,1,0:T(8,128)(2,1)S(1)}, bf16[4,96,128]{2,1,0:T(8,128)(2,1)S(1)}, u32[]{:S(2)}, u32[]{:S(2)}) collective-permute-start(bf16[4,96,128]{2,1,0:T(8,128)(2,1)S(1)} %get-tuple-element.40), channel_id=1, source_target_pairs={{0,8},{16,24},{8,0},{24,16},{1,9},{17,25},{9,1},{25,17},{2,10},{18... | collective-permute-start | bytes 294920 | tf_op jit(solution)/shard_map/ppermute | solution.py:350
  7.1 10.8 %collective-permute-start.1 = (bf16[4,96,128]{2,1,0:T(8,128)(2,1)S(1)}, bf16[4,96,128]{2,1,0:T(8,128)(2,1)S(1)}, u32[]{:S(2)}, u32[]{:S(2)}) collective-permute-start(bf16[4,96,128]{2,1,0:T(8,128)(2,1)S(1)} %get-tuple-element.41), channel_id=1, source_target_pairs={{8,16},{24,0},{16,8},{0,24},{9,17},{25,1},{17,9},{1,25},{10,18},{2... | collective-permute-start | bytes 294920 | tf_op jit(solution)/shard_map/ppermute | solution.py:350
  8.6 9.3 %collective-permute-start.2 = (bf16[4,96,128]{2,1,0:T(8,128)(2,1)S(1)}, bf16[4,96,128]{2,1,0:T(8,128)(2,1)S(1)}, u32[]{:S(2)}, u32[]{:S(2)}) collective-permute-start(bf16[4,96,128]{2,1,0:T(8,128)(2,1)S(1)} %get-tuple-element.42), channel_id=1, source_target_pairs={{0,1},{2,3},{4,5},{6,7},{1,0},{3,2},{5,4},{7,6},{8,9},{10,11},{12,... | collective-permute-start | bytes 294920 | tf_op jit(solution)/shard_map/ppermute | solution.py:350
  8.6 9.3 %collective-permute-start.3 = (bf16[4,96,128]{2,1,0:T(8,128)(2,1)S(1)}, bf16[4,96,128]{2,1,0:T(8,128)(2,1)S(1)}, u32[]{:S(2)}, u32[]{:S(2)}) collective-permute-start(bf16[4,96,128]{2,1,0:T(8,128)(2,1)S(1)} %get-tuple-element.43), channel_id=1, source_target_pairs={{1,2},{3,4},{5,6},{7,0},{2,1},{4,3},{6,5},{0,7},{9,10},{11,12},{13... | collective-permute-start | bytes 294920 | tf_op jit(solution)/shard_map/ppermute | solution.py:350
  19.3 1.3 %collective-permute-start.4 = (bf16[4,80,128]{2,1,0:T(8,128)(2,1)S(1)}, bf16[4,80,128]{2,1,0:T(8,128)(2,1)S(1)}, u32[]{:S(2)}, u32[]{:S(2)}) collective-permute-start(bf16[4,80,128]{2,1,0:T(8,128)(2,1)S(1)} %get-tuple-element.48), channel_id=1, source_target_pairs={{0,1},{2,3},{4,5},{6,7},{1,0},{3,2},{5,4},{7,6},{8,9},{10,11},{12,... | collective-permute-start | bytes 245768 | tf_op jit(solution)/shard_map/ppermute | solution.py:350
  20.7 4.6 %collective-permute-start.5 = (bf16[4,80,128]{2,1,0:T(8,128)(2,1)S(1)}, bf16[4,80,128]{2,1,0:T(8,128)(2,1)S(1)}, u32[]{:S(2)}, u32[]{:S(2)}) collective-permute-start(bf16[4,80,128]{2,1,0:T(8,128)(2,1)S(1)} %add_convert_fusion.1), channel_id=1, source_target_pairs={{0,2},{1,3},{2,0},{3,1},{4,6},{5,7},{6,4},{7,5},{8,10},{9,11},{10,... | collective-permute-start | bytes 245768 | tf_op jit(solution)/shard_map/ppermute | solution.py:378
  25.3 6.4 %collective-permute-start.6 = (bf16[4,80,128]{2,1,0:T(8,128)(2,1)S(1)}, bf16[4,80,128]{2,1,0:T(8,128)(2,1)S(1)}, u32[]{:S(2)}, u32[]{:S(2)}) collective-permute-start(bf16[4,80,128]{2,1,0:T(8,128)(2,1)S(1)} %add_convert_fusion.one), channel_id=1, source_target_pairs={{0,4},{1,5},{2,6},{3,7},{4,0},{5,1},{6,2},{7,3},{8,12},{9,13},{10,... | collective-permute-start | bytes 245768 | tf_op jit(solution)/shard_map/ppermute | solution.py:378
  32.8 1.3 %collective-permute-start.7 = (bf16[4,48,128]{2,1,0:T(8,128)(2,1)S(1)}, bf16[4,48,128]{2,1,0:T(8,128)(2,1)S(1)}, u32[]{:S(2)}, u32[]{:S(2)}) collective-permute-start(bf16[4,48,128]{2,1,0:T(8,128)(2,1)S(1)} %get-tuple-element.49.y_own), channel_id=1, source_target_pairs={{0,1},{2,3},{4,5},{6,7},{1,0},{3,2},{5,4},{7,6},{8,9},{10,11},{12,... | collective-permute-start | bytes 147464 | tf_op jit(solution)/shard_map/ppermute | solution.py:350
  34.7 4.9 %collective-permute-start.8 = (bf16[4,48,128]{2,1,0:T(8,128)(2,1)S(1)}, bf16[4,48,128]{2,1,0:T(8,128)(2,1)S(1)}, u32[]{:S(2)}, u32[]{:S(2)}) collective-permute-start(bf16[4,48,128]{2,1,0:T(8,128)(2,1)S(1)} %get-tuple-element.57), channel_id=1, source_target_pairs={{0,8},{16,24},{8,0},{24,16},{1,9},{17,25},{9,1},{25,17},{2,10},{18... | collective-permute-start | bytes 147464 | tf_op jit(solution)/shard_map/ppermute | solution.py:350
  36.3 5.0 %collective-permute-start.9 = (bf16[4,48,128]{2,1,0:T(8,128)(2,1)S(1)}, bf16[4,48,128]{2,1,0:T(8,128)(2,1)S(1)}, u32[]{:S(2)}, u32[]{:S(2)}) collective-permute-start(bf16[4,48,128]{2,1,0:T(8,128)(2,1)S(1)} %get-tuple-element.58), channel_id=1, source_target_pairs={{8,16},{24,0},{16,8},{0,24},{9,17},{25,1},{17,9},{1,25},{10,18},{2... | collective-permute-start | bytes 147464 | tf_op jit(solution)/shard_map/ppermute | solution.py:350
  43.5 4.9 %collective-permute-start.10 = (bf16[4,96,128]{2,1,0:T(8,128)(2,1)S(1)}, bf16[4,96,128]{2,1,0:T(8,128)(2,1)S(1)}, u32[]{:S(2)}, u32[]{:S(2)}) collective-permute-start(bf16[4,96,128]{2,1,0:T(8,128)(2,1)S(1)} %get-tuple-element.61), channel_id=1, source_target_pairs={{0,8},{16,24},{8,0},{24,16},{1,9},{17,25},{9,1},{25,17},{2,10},{18... | collective-permute-start | bytes 294920 | tf_op jit(solution)/shard_map/ppermute | solution.py:350
  44.1 5.5 %collective-permute-start.11 = (bf16[4,96,128]{2,1,0:T(8,128)(2,1)S(1)}, bf16[4,96,128]{2,1,0:T(8,128)(2,1)S(1)}, u32[]{:S(2)}, u32[]{:S(2)}) collective-permute-start(bf16[4,96,128]{2,1,0:T(8,128)(2,1)S(1)} %get-tuple-element.62), channel_id=1, source_target_pairs={{8,16},{24,0},{16,8},{0,24},{9,17},{25,1},{17,9},{1,25},{10,18},{2... | collective-permute-start | bytes 294920 | tf_op jit(solution)/shard_map/ppermute | solution.py:350
  45.6 4.1 %collective-permute-start.12 = (bf16[4,96,128]{2,1,0:T(8,128)(2,1)S(1)}, bf16[4,96,128]{2,1,0:T(8,128)(2,1)S(1)}, u32[]{:S(2)}, u32[]{:S(2)}) collective-permute-start(bf16[4,96,128]{2,1,0:T(8,128)(2,1)S(1)} %get-tuple-element.63), channel_id=1, source_target_pairs={{0,1},{2,3},{4,5},{6,7},{1,0},{3,2},{5,4},{7,6},{8,9},{10,11},{12,... | collective-permute-start | bytes 294920 | tf_op jit(solution)/shard_map/ppermute | solution.py:350
  45.6 5.8 %collective-permute-start.13 = (bf16[4,96,128]{2,1,0:T(8,128)(2,1)S(1)}, bf16[4,96,128]{2,1,0:T(8,128)(2,1)S(1)}, u32[]{:S(2)}, u32[]{:S(2)}) collective-permute-start(bf16[4,96,128]{2,1,0:T(8,128)(2,1)S(1)} %get-tuple-element.64), channel_id=1, source_target_pairs={{1,2},{3,4},{5,6},{7,0},{2,1},{4,3},{6,5},{0,7},{9,10},{11,12},{13... | collective-permute-start | bytes 294920 | tf_op jit(solution)/shard_map/ppermute | solution.py:350

commit v3 on v2

--- a/solution.py
+++ b/solution.py
@@ -15,6 +15,8 @@
 F32 = jnp.float32
 BF16 = jnp.bfloat16
 LIMIT = 24 * 1024 * 1024
+PARTS = 2
+OUT_PARTS = 8
 
 
 def dot(a, b, precision=None):
@@ -48,19 +50,15 @@
     )(*ins)
 
 
-def fetch(e, pairs, sems):
-    return [pltpu.make_async_copy(a.at[e], b.at[e], sems.at[n, e]) for n, (a, b) in enumerate(pairs)]
-
-
-def begin(count, pairs, sems):
-    for e in range(count):
-        for copy in fetch(e, pairs, sems):
-            copy.start()
-
-
-def finish(e, pairs, sems):
-    for copy in fetch(e, pairs, sems):
-        copy.wait()
+def chunks(count, pairs, sems, parts):
+    size = count // parts
+    return [
+        [
+            pltpu.make_async_copy(a.at[pl.ds(q * size, size)], b.at[pl.ds(q * size, size)], sems.at[n, q])
+            for n, (a, b) in enumerate(pairs)
+        ]
+        for q in range(parts)
+    ]
 
 
 def read_traces(load, tmp):
@@ -142,27 +140,36 @@
     ]
 
 
-def first_body(rhs_far, inv_far, spots, first, tr, rhs, inv, s0, s1, s2, s3, tmp, sides, sems):
-    pairs = ((inv_far, inv), (rhs_far, rhs))
+def first_body(
+    rhs_far, inv_far, coup_far, spots,
+    first, tr, rhs, inv, coup, s0, s1, s2, s3,
+    tmp, sides, sems,
+):
     count = rhs.shape[0]
-    begin(count, pairs, sems)
-    for e in range(count):
-        finish(e, pairs, sems)
+    shares = chunks(count, ((inv_far, inv), (rhs_far, rhs)), sems, PARTS)
+    later = pltpu.make_async_copy(coup_far, coup, sems.at[0, PARTS])
+    for share in shares:
+        for copy in share:
+            copy.start()
+    later.start()
+    for e in range(count):
+        if e % (count // PARTS) == 0:
+            for copy in shares[e * PARTS // count]:
+                copy.wait()
         first[e] = relax_fine * dot(inv[e], rhs[e])
         emit_traces(e, first, tr, sides, tmp)
     emit_sends(spots, sides, (s0, s1, s2, s3))
+    later.wait()
 
 
 def local_body(
-    rhs, state, diag_far, coup_far, tr, pt, face_source, subset,
+    rhs, state, diag, coup, tr, pt, face_source, subset,
     acc, mats, oper, outer, pf, prolong,
-    diag, coup, wide, tmp, msum, sems,
+    wide, tmp, msum,
 ):
     coarse, dof = pt.shape
     count, _, cols = acc.shape
     near_rows = outer.shape[2]
-    pairs = ((diag_far, diag), (coup_far, coup))
-    begin(count, pairs, sems)
     wide[...] = stack([pt[...].astype(F32)], cols).T
     for f, face in enumerate(read_traces(strided(wide), tmp)):
         pf[f] = face.astype(BF16)
@@ -172,7 +179,6 @@
     for e in range(count):
         i, j, k = place(e)
         inner = inner_faces(e)
-        finish(e, pairs, sems)
         oper[e, :, 0:dof] = diag[e]
         oper[e, :, dof : 2 * dof] = stack([coup[e, f] for f, near, face in inner], dof).T
         outer[e] = stack([coup[e, i], coup[e, 2 + j]], near_rows).T
@@ -333,15 +339,17 @@
 
 def final_body(part, state, outer, inv, xm, xp, ym, yp, face_source, spots, out_far, res, out, sems):
     count = state.shape[0]
-    pairs = ((out, out_far),)
+    copies = chunks(count, ((out, out_far),), sems, OUT_PARTS)
     for e in range(count):
         far = stack(pick(e, (xm, xp, ym, yp), face_source, spots), outer.shape[2])
         res[e] = (part[e] - dot(outer[e], far)).astype(BF16)
+    size = count // OUT_PARTS
     for e in range(count):
         out[e] = state[e] + relax_fine * dot(inv[e], res[e])
-        fetch(e, pairs, sems)[0].start()
-    for e in range(count):
-        finish(e, pairs, sems)
+        if e % size == size - 1:
+            copies[e // size][0].start()
+    for (copy,) in copies:
+        copy.wait()
 
 
 def swap(value, axis, start):
@@ -396,7 +404,6 @@
     tmps = pltpu.VMEM((elements, 2, fdof, cols), F32)
     sides = pltpu.VMEM((4, half, fdof, cols), BF16)
     state_b = pltpu.VMEM((elements, dof, cols), BF16)
-    square_b = pltpu.VMEM((elements, dof, dof), BF16)
     apply_flops = 2 * elements * dof * cols * (dof + 3 * fdof)
     inv_flops = 2 * elements * dof * dof * cols
     far_flops = 4 * elements * dof * fdof * cols
@@ -407,13 +414,13 @@
     spots = jnp.stack(
         [me, (me + groups - 1) % groups, (me + 1) % groups, lax.axis_index("gx")]
     ).astype(jnp.int32)
-    first, tr, rhs, inv, *sends = run(
+    first, tr, rhs, inv, coup, *sends = run(
         first_body,
-        (rhs, inverse_blocks, spots),
-        [state_s, tr_s, shape(rhs.shape, BF16), shape(inverse_blocks.shape, BF16)] + sends_s,
-        [tmps, sides, pltpu.SemaphoreType.DMA((2, elements))],
+        (rhs, inverse_blocks, coup, spots),
+        [state_s, tr_s] + [shape(a.shape, BF16) for a in (rhs, inverse_blocks, coup)] + sends_s,
+        [tmps, sides, pltpu.SemaphoreType.DMA((2, PARTS + 1))],
         inv_flops,
-        far_ins=(0, 1),
+        far_ins=(0, 1, 2),
     )
     xm, xp, ym, yp = exchange(sends)
     acc, mats, oper, outer, pf, wide = run(
@@ -428,15 +435,11 @@
             shape((dof, cols), BF16),
         ],
         [
-            square_b,
-            pltpu.VMEM(coup.shape, BF16),
             pltpu.VMEM((dof, cols), F32),
             pltpu.VMEM((2, fdof, cols), F32),
             pltpu.VMEM((groups, coarse, cols), F32),
-            pltpu.SemaphoreType.DMA((2, elements)),
         ],
         2 * apply_flops,
-        far_ins=(2, 3),
     )
     resid, keep, give = run(
         restrict_body,

time: 54.2 us -> 52.4 us (0.967)
  starting transfers between devices: 13.7 us -> 17.7 us
  waiting for transfers between devices: 17.7 us -> 14.6 us
  Pallas kernels: 22.4 us -> 19.6 us
    pallas_call x9, Pallas kernels: 22.4 us -> 19.6 us  [run(): pl.pallas_call(body, in_specs=[smem if a.dtype == jnp.int32 else hbm if n...]
    ppermute x12, starting transfers between devices: 13.2 us -> 15.7 us  [swap(): return lax.ppermute(value, axis, pairs + [(b, a) for a, b in pairs])]
    ppermute x12, waiting for transfers between devices: 7.24 us -> 5.63 us  [swap(): return lax.ppermute(value, axis, pairs + [(b, a) for a, b in pairs])]
    ppermute x2, starting transfers between devices: 0.54 us -> 1.99 us  [row_sum(): two = lax.ppermute(one, 'gy', [(i, i ^ step) for i in range(count)])]
    ppermute x2, waiting for transfers between devices: 10.4 us -> 8.97 us  [row_sum(): two = lax.ppermute(one, 'gy', [(i, i ^ step) for i in range(count)])]
  transfers between devices with their start and end apart: 14 -> 14, of which waited for: 8 -> 6; matrix products, arithmetic and copies ran while one was open for 0% -> 0% of each run, Pallas kernels for 19% -> 15%
where the time goes in v3:
time: 52.4 us; the launch traced here: 52.2 us
  Pallas kernels  19.6 us (37%)
  starting transfers between devices  17.7 us (34%)
  waiting for transfers between devices  14.6 us (28%)
    pallas_call x9, Pallas kernels, run(): pl.pallas_call(body, in_specs=[smem if a.dtype == jnp.int32 else hbm if n...  19.6 us
    ppermute x12, starting transfers between devices, swap(): return lax.ppermute(value, axis, pairs + [(b, a) for a, b in pairs])  15.7 us
    ppermute x2, waiting for transfers between devices, row_sum(): two = lax.ppermute(one, 'gy', [(i, i ^ step) for i in range(count)])  8.97 us
    ppermute x12, waiting for transfers between devices, swap(): return lax.ppermute(value, axis, pairs + [(b, a) for a, b in pairs])  5.63 us
    ppermute x2, starting transfers between devices, row_sum(): two = lax.ppermute(one, 'gy', [(i, i ^ step) for i in range(count)])  1.99 us
  transfers between devices with their start and end apart: 14, of which 6 were waited for; matrix products, arithmetic and copies ran while one was open for 0% of the time, Pallas kernels for 15%

profile of v3, /device:TPU:0, one launch (start us, length us, event | category | flops | bytes accessed | tf_op | source)
XLA Modules:
  0.0 52.2 jit_solution(2469913355202909377)
XLA Ops:
  0.0 0.1 pad_add_fusion.spots
  0.1 3.7 %shard_map.73 = (f32[8,384,128]{2,1,0:T(8,128)S(1)}, bf16[8,6,96,128]{3,2,1,0:T(8,128)(2,1)S(1)}, bf16[8,384,128]{2,1,0:T(8,128)(2,1)S(1)}, bf16[8,384,384]{2,1,...) custom-call(bf16[8,384,128]{2,1,0:T(8,128)(2,1)} %rhs_far.1, ...), custom_call_target="tpu_custom_call" | custom-call | flops 301989888 | bytes 16515088 | tf_op jit(solution)/shard_map/pallas_call | solution.py:39
  3.8 3.0 %collective-permute-start = (bf16[4,96,128]{2,1,0:T(8,128)(2,1)S(1)}, bf16[4,96,128]{2,1,0:T(8,128)(2,1)S(1)}, u32[]{:S(2)}, u32[]{:S(2)}) collective-permute-start(bf16[4,96,128]{2,1,0:T(8,128)(2,1)S(1)} %get-tuple-element.42), channel_id=1, source_target_pairs={{0,8},{16,24},{8,0},{24,16},{1,9},{17,25},{9,1},{25,17},{2,10},{18... | collective-permute-start | bytes 294920 | tf_op jit(solution)/shard_map/ppermute | solution.py:358
  6.8 1.5 %collective-permute-start.1 = (bf16[4,96,128]{2,1,0:T(8,128)(2,1)S(1)}, bf16[4,96,128]{2,1,0:T(8,128)(2,1)S(1)}, u32[]{:S(2)}, u32[]{:S(2)}) collective-permute-start(bf16[4,96,128]{2,1,0:T(8,128)(2,1)S(1)} %get-tuple-element.43), channel_id=1, source_target_pairs={{8,16},{24,0},{16,8},{0,24},{9,17},{25,1},{17,9},{1,25},{10,18},{2... | collective-permute-start | bytes 294920 | tf_op jit(solution)/shard_map/ppermute | solution.py:358
  8.3 0.0 collective-permute-start.2
  8.3 3.7 %collective-permute-start.3 = (bf16[4,96,128]{2,1,0:T(8,128)(2,1)S(1)}, bf16[4,96,128]{2,1,0:T(8,128)(2,1)S(1)}, u32[]{:S(2)}, u32[]{:S(2)}) collective-permute-start(bf16[4,96,128]{2,1,0:T(8,128)(2,1)S(1)} %get-tuple-element.45), channel_id=1, source_target_pairs={{1,2},{3,4},{5,6},{7,0},{2,1},{4,3},{6,5},{0,7},{9,10},{11,12},{13... | collective-permute-start | bytes 294920 | tf_op jit(solution)/shard_map/ppermute | solution.py:358
  12.1 3.0 %shard_map.74 = (f32[8,384,128]{2,1,0:T(8,128)S(1)}, f32[8,24,128]{2,1,0:T(8,128)S(1)}, bf16[8,384,768]{2,1,0:T(8,128)(2,1)S(1)}, bf16[8,384,256]{2,1,0:T(8,128)...) custom-call(bf16[8,384,128]{2,1,0:T(8,128)(2,1)S(1)} %get-tuple-element.36.rhs, ...), custom_call_target="tpu_custom_call" | custom-call | flops 1056964608 | bytes 17682656 | tf_op jit(solution)/shard_map/pallas_call | solution.py:39
  15.1 0.0 collective-permute-done.1.xp
  15.1 0.0 collective-permute-done.2.ym
  15.1 1.4 %shard_map.75 = (f32[8,384,128]{2,1,0:T(8,128)S(1)}, bf16[4,80,128]{2,1,0:T(8,128)(2,1)S(1)}, bf16[4,80,128]{2,1,0:T(8,128)(2,1)S(1)}) custom-call(f32[8,384,128]{2,1,0:T(8,128)S(1)} %get-tuple-element.40.part, bf16[8,384,256]{2,1,0:T(8,128)(2,1)S(1)} %get-tuple-element.41.outer, bf16[4,96,128]{2,1,0:T(8,128)(2,1)S(1)} %collective-permute-done.xm, ...), custom_call_target="tpu_custom_call" | custom-call | flops 150994944 | bytes 5411056 | tf_op jit(solution)/shard_map/pallas_call | solution.py:39
  16.5 0.1 collective-permute-start.4
  16.6 1.3 %collective-permute-done.4 = bf16[4,80,128]{2,1,0:T(8,128)(2,1)S(1)} collective-permute-done((bf16[4,80,128]{2,1,0:T(8,128)(2,1)S(1)}, bf16[4,80,128]{2,1,0:T(8,128)(2,1)S(1)}, u32[]{:S(2)}, u32[]{:S(2)}) %collective-permute-start.4) | collective-permute-done | bytes 81952 | tf_op jit(solution)/shard_map/ppermute | solution.py:358
  17.9 0.1 collective-permute-start.5
  18.0 4.5 %collective-permute-done.5 = bf16[4,80,128]{2,1,0:T(8,128)(2,1)S(1)} collective-permute-done((bf16[4,80,128]{2,1,0:T(8,128)(2,1)S(1)}, bf16[4,80,128]{2,1,0:T(8,128)(2,1)S(1)}, u32[]{:S(2)}, u32[]{:S(2)}) %collective-permute-start.5) | collective-permute-done | bytes 81952 | tf_op jit(solution)/shard_map/ppermute | solution.py:386
  22.5 1.9 %collective-permute-start.6 = (bf16[4,80,128]{2,1,0:T(8,128)(2,1)S(1)}, bf16[4,80,128]{2,1,0:T(8,128)(2,1)S(1)}, u32[]{:S(2)}, u32[]{:S(2)}) collective-permute-start(bf16[4,80,128]{2,1,0:T(8,128)(2,1)S(1)} %add_convert_fusion.one), channel_id=1, source_target_pairs={{0,4},{1,5},{2,6},{3,7},{4,0},{5,1},{6,2},{7,3},{8,12},{9,13},{10,... | collective-permute-start | bytes 245768 | tf_op jit(solution)/shard_map/ppermute | solution.py:386
  24.4 4.5 %collective-permute-done.6.two = bf16[4,80,128]{2,1,0:T(8,128)(2,1)S(1)} collective-permute-done((bf16[4,80,128]{2,1,0:T(8,128)(2,1)S(1)}, bf16[4,80,128]{2,1,0:T(8,128)(2,1)S(1)}, u32[]{:S(2)}, u32[]{:S(2)}) %collective-permute-start.6) | collective-permute-done | bytes 81952 | tf_op jit(solution)/shard_map/ppermute | solution.py:386
  28.9 1.1 %shard_map.76 = (bf16[4,48,128]{2,1,0:T(8,128)(2,1)S(1)}, f32[2,8,128]{2,1,0:T(8,128)S(1)}) custom-call(bf16[4,80,128]{2,1,0:T(8,128)(2,1)S(1)} %add_convert_fusion.one, bf16[4,80,128]{2,1,0:T(8,128)(2,1)S(1)} %collective-permute-done.6.two, s32[4]{0:T(128)S(1)} %pad_add_fusion.spots), custom_call_target="tpu_custom_call" | custom-call | flops 28311552 | bytes 221200 | tf_op jit(solution)/shard_map/pallas_call | solution.py:39
  30.0 0.1 collective-permute-start.7
  30.1 1.2 %collective-permute-done.7.y_other = bf16[4,48,128]{2,1,0:T(8,128)(2,1)S(1)} collective-permute-done((bf16[4,48,128]{2,1,0:T(8,128)(2,1)S(1)}, bf16[4,48,128]{2,1,0:T(8,128)(2,1)S(1)}, u32[]{:S(2)}, u32[]{:S(2)}) %collective-permute-start.7) | collective-permute-done | bytes 49184 | tf_op jit(solution)/shard_map/ppermute | solution.py:358
  31.3 0.6 %shard_map.77 = (bf16[8,48,128]{2,1,0:T(8,128)(2,1)S(1)}, bf16[4,48,128]{2,1,0:T(8,128)(2,1)S(1)}, bf16[4,48,128]{2,1,0:T(8,128)(2,1)S(1)}) custom-call(bf16[4,48,128]{2,1,0:T(8,128)(2,1)S(1)} %get-tuple-element.51.y_own, bf16[4,48,128]{2,1,0:T(8,128)(2,1)S(1)} %collective-permute-done.7.y_other, s32[8]{0:T(128)S(1)} %copy-done.3, s32[4]{0:T(128)S(1)} %pad_add_fusion.spots), custom_call_target="tpu_custom_call" | custom-call | bytes 294960 | tf_op jit(solution)/shard_map/pallas_call | solution.py:39
  31.9 1.6 %collective-permute-start.8 = (bf16[4,48,128]{2,1,0:T(8,128)(2,1)S(1)}, bf16[4,48,128]{2,1,0:T(8,128)(2,1)S(1)}, u32[]{:S(2)}, u32[]{:S(2)}) collective-permute-start(bf16[4,48,128]{2,1,0:T(8,128)(2,1)S(1)} %get-tuple-element.59), channel_id=1, source_target_pairs={{0,8},{16,24},{8,0},{24,16},{1,9},{17,25},{9,1},{25,17},{2,10},{18... | collective-permute-start | bytes 147464 | tf_op jit(solution)/shard_map/ppermute | solution.py:358
  33.5 0.5 collective-permute-start.9
  33.9 2.9 %shard_map.78 = (f32[8,384,128]{2,1,0:T(8,128)S(1)}, f32[8,384,128]{2,1,0:T(8,128)S(1)}) custom-call(f32[8,384,128]{2,1,0:T(8,128)S(1)} %get-tuple-element.47.resid, f32[8,384,128]{2,1,0:T(8,128)S(1)} %get-tuple-element.37.state, bf16[8,384,768]{2,1,0:T(8,128)(2,1)S(1)} %get-tuple-element.48.oper, bf16[8,384,256]{2,1,0:T(8,128)(2,1)S(1)} %get-tuple-element.41.outer, ...), custom_call_target="tpu_custom_call" | custom-call | flops 528482304 | bytes 12935392 | tf_op jit(solution)/shard_map/pallas_call | solution.py:39
  36.8 1.6 %collective-permute-done.9.y1 = bf16[4,48,128]{2,1,0:T(8,128)(2,1)S(1)} collective-permute-done((bf16[4,48,128]{2,1,0:T(8,128)(2,1)S(1)}, bf16[4,48,128]{2,1,0:T(8,128)(2,1)S(1)}, u32[]{:S(2)}, u32[]{:S(2)}) %collective-permute-start.9) | collective-permute-done | bytes 49184 | tf_op jit(solution)/shard_map/ppermute | solution.py:358
  38.5 2.3 %shard_map.79 = (f32[8,384,128]{2,1,0:T(8,128)S(1)}, bf16[8,6,96,128]{3,2,1,0:T(8,128)(2,1)S(1)}, bf16[4,96,128]{2,1,0:T(8,128)(2,1)S(1)}, bf16[4,96,128]{2,1,0:...) custom-call(f32[8,384,128]{2,1,0:T(8,128)S(1)} %get-tuple-element.56.part, ...), custom_call_target="tpu_custom_call" | custom-call | flops 301989888 | bytes 10469584 | tf_op jit(solution)/shard_map/pallas_call | solution.py:39
  40.7 0.6 %collective-permute-start.10 = (bf16[4,96,128]{2,1,0:T(8,128)(2,1)S(1)}, bf16[4,96,128]{2,1,0:T(8,128)(2,1)S(1)}, u32[]{:S(2)}, u32[]{:S(2)}) collective-permute-start(bf16[4,96,128]{2,1,0:T(8,128)(2,1)S(1)} %get-tuple-element.63), channel_id=1, source_target_pairs={{0,8},{16,24},{8,0},{24,16},{1,9},{17,25},{9,1},{25,17},{2,10},{18... | collective-permute-start | bytes 294920 | tf_op jit(solution)/shard_map/ppermute | solution.py:358
  41.3 1.4 %collective-permute-start.11 = (bf16[4,96,128]{2,1,0:T(8,128)(2,1)S(1)}, bf16[4,96,128]{2,1,0:T(8,128)(2,1)S(1)}, u32[]{:S(2)}, u32[]{:S(2)}) collective-permute-start(bf16[4,96,128]{2,1,0:T(8,128)(2,1)S(1)} %get-tuple-element.64), channel_id=1, source_target_pairs={{8,16},{24,0},{16,8},{0,24},{9,17},{25,1},{17,9},{1,25},{10,18},{2... | collective-permute-start | bytes 294920 | tf_op jit(solution)/shard_map/ppermute | solution.py:358
  42.8 3.3 %collective-permute-start.13 = (bf16[4,96,128]{2,1,0:T(8,128)(2,1)S(1)}, bf16[4,96,128]{2,1,0:T(8,128)(2,1)S(1)}, u32[]{:S(2)}, u32[]{:S(2)}) collective-permute-start(bf16[4,96,128]{2,1,0:T(8,128)(2,1)S(1)} %get-tuple-element.66), channel_id=1, source_target_pairs={{1,2},{3,4},{5,6},{7,0},{2,1},{4,3},{6,5},{0,7},{9,10},{11,12},{13... | collective-permute-start | bytes 294920 | tf_op jit(solution)/shard_map/ppermute | solution.py:358
  46.0 2.0 %shard_map.80.part = f32[8,384,128]{2,1,0:T(8,128)S(1)} custom-call(bf16[8,384,128]{2,1,0:T(8,128)(2,1)S(1)} %get-tuple-element.36.rhs, f32[8,384,128]{2,1,0:T(8,128)S(1)} %get-tuple-element.61.state, bf16[8,384,768]{2,1,0:T(8,128)(2,1)S(1)} %get-tuple-element.48.oper, bf16[8,6,96,128]{3,2,1,0:T(8,128)(2,1)S(1)} %get-tuple-element.62.tr, s32[8,6]{1,0:T(8,128)S(1)} %copy-done.1), custom_call_target="tpu_custom_call" | custom-call | flops 528482304 | bytes 9830592 | tf_op jit(solution)/shard_map/pallas_call | solution.py:39
  48.1 0.0 collective-permute-done.11.xp
  48.1 1.5 %collective-permute-done.13.yp = bf16[4,96,128]{2,1,0:T(8,128)(2,1)S(1)} collective-permute-done((bf16[4,96,128]{2,1,0:T(8,128)(2,1)S(1)}, bf16[4,96,128]{2,1,0:T(8,128)(2,1)S(1)}, u32[]{:S(2)}, u32[]{:S(2)}) %collective-permute-start.13) | collective-permute-done | bytes 98336 | tf_op jit(solution)/shard_map/ppermute | solution.py:358
  49.6 2.6 %shard_map.81 = f32[8,384,128]{2,1,0:T(8,128)} custom-call(f32[8,384,128]{2,1,0:T(8,128)S(1)} %shard_map.80.part, f32[8,384,128]{2,1,0:T(8,128)S(1)} %get-tuple-element.61.state, bf16[8,384,256]{2,1,0:T(8,128)(2,1)S(1)} %get-tuple-element.41.outer, bf16[8,384,384]{2,1,0:T(8,128)(2,1)S(1)} %get-tuple-element.58.inv, ...), custom_call_target="tpu_custom_call" | custom-call | flops 452984832 | bytes 9044176 | tf_op jit(solution)/shard_map/pallas_call | solution.py:39
  (16 shorter events, 0.1 us)
Async XLA Ops:
  0.1 12.0 %copy-start = (bf16[8,384,384]{2,1,0:T(8,128)(2,1)S(1)}, bf16[8,384,384]{2,1,0:T(8,128)(2,1)}, u32[]{:S(2)}) copy-start(bf16[8,384,384]{2,1,0:T(8,128)(2,1)} %diag.1) | copy-start | bytes 7077892
  0.1 12.0 %copy-start.1 = (s32[8,6]{1,0:T(8,128)S(1)}, s32[8,6]{1,0:T(8,128)}, u32[]{:S(2)}) copy-start(s32[8,6]{1,0:T(8,128)} %face_source.11) | copy-start | bytes 580
  0.1 12.0 %copy-start.2 = (bf16[384,48]{0,1:T(8,128)(2,1)S(1)}, bf16[384,48]{0,1:T(8,128)(2,1)}, u32[]{:S(2)}) copy-start(bf16[384,48]{0,1:T(8,128)(2,1)} %param.11) | copy-start | bytes 110596
  0.1 12.0 %copy-start.3 = (s32[8]{0:T(128)S(1)}, s32[8]{0:T(128)}, u32[]{:S(2)}) copy-start(s32[8]{0:T(128)} %subset.7) | copy-start | bytes 100
  3.8 11.2 %collective-permute-start = (bf16[4,96,128]{2,1,0:T(8,128)(2,1)S(1)}, bf16[4,96,128]{2,1,0:T(8,128)(2,1)S(1)}, u32[]{:S(2)}, u32[]{:S(2)}) collective-permute-start(bf16[4,96,128]{2,1,0:T(8,128)(2,1)S(1)} %get-tuple-element.42), channel_id=1, source_target_pairs={{0,8},{16,24},{8,0},{24,16},{1,9},{17,25},{9,1},{25,17},{2,10},{18... | collective-permute-start | bytes 294920 | tf_op jit(solution)/shard_map/ppermute | solution.py:358
  6.8 8.2 %collective-permute-start.1 = (bf16[4,96,128]{2,1,0:T(8,128)(2,1)S(1)}, bf16[4,96,128]{2,1,0:T(8,128)(2,1)S(1)}, u32[]{:S(2)}, u32[]{:S(2)}) collective-permute-start(bf16[4,96,128]{2,1,0:T(8,128)(2,1)S(1)} %get-tuple-element.43), channel_id=1, source_target_pairs={{8,16},{24,0},{16,8},{0,24},{9,17},{25,1},{17,9},{1,25},{10,18},{2... | collective-permute-start | bytes 294920 | tf_op jit(solution)/shard_map/ppermute | solution.py:358
  8.3 6.8 %collective-permute-start.2 = (bf16[4,96,128]{2,1,0:T(8,128)(2,1)S(1)}, bf16[4,96,128]{2,1,0:T(8,128)(2,1)S(1)}, u32[]{:S(2)}, u32[]{:S(2)}) collective-permute-start(bf16[4,96,128]{2,1,0:T(8,128)(2,1)S(1)} %get-tuple-element.44), channel_id=1, source_target_pairs={{0,1},{2,3},{4,5},{6,7},{1,0},{3,2},{5,4},{7,6},{8,9},{10,11},{12,... | collective-permute-start | bytes 294920 | tf_op jit(solution)/shard_map/ppermute | solution.py:358
  8.3 6.8 %collective-permute-start.3 = (bf16[4,96,128]{2,1,0:T(8,128)(2,1)S(1)}, bf16[4,96,128]{2,1,0:T(8,128)(2,1)S(1)}, u32[]{:S(2)}, u32[]{:S(2)}) collective-permute-start(bf16[4,96,128]{2,1,0:T(8,128)(2,1)S(1)} %get-tuple-element.45), channel_id=1, source_target_pairs={{1,2},{3,4},{5,6},{7,0},{2,1},{4,3},{6,5},{0,7},{9,10},{11,12},{13... | collective-permute-start | bytes 294920 | tf_op jit(solution)/shard_map/ppermute | solution.py:358
  16.5 1.3 %collective-permute-start.4 = (bf16[4,80,128]{2,1,0:T(8,128)(2,1)S(1)}, bf16[4,80,128]{2,1,0:T(8,128)(2,1)S(1)}, u32[]{:S(2)}, u32[]{:S(2)}) collective-permute-start(bf16[4,80,128]{2,1,0:T(8,128)(2,1)S(1)} %get-tuple-element.50), channel_id=1, source_target_pairs={{0,1},{2,3},{4,5},{6,7},{1,0},{3,2},{5,4},{7,6},{8,9},{10,11},{12,... | collective-permute-start | bytes 245768 | tf_op jit(solution)/shard_map/ppermute | solution.py:358
  17.9 4.6 %collective-permute-start.5 = (bf16[4,80,128]{2,1,0:T(8,128)(2,1)S(1)}, bf16[4,80,128]{2,1,0:T(8,128)(2,1)S(1)}, u32[]{:S(2)}, u32[]{:S(2)}) collective-permute-start(bf16[4,80,128]{2,1,0:T(8,128)(2,1)S(1)} %add_convert_fusion.1), channel_id=1, source_target_pairs={{0,2},{1,3},{2,0},{3,1},{4,6},{5,7},{6,4},{7,5},{8,10},{9,11},{10,... | collective-permute-start | bytes 245768 | tf_op jit(solution)/shard_map/ppermute | solution.py:386
  22.5 6.4 %collective-permute-start.6 = (bf16[4,80,128]{2,1,0:T(8,128)(2,1)S(1)}, bf16[4,80,128]{2,1,0:T(8,128)(2,1)S(1)}, u32[]{:S(2)}, u32[]{:S(2)}) collective-permute-start(bf16[4,80,128]{2,1,0:T(8,128)(2,1)S(1)} %add_convert_fusion.one), channel_id=1, source_target_pairs={{0,4},{1,5},{2,6},{3,7},{4,0},{5,1},{6,2},{7,3},{8,12},{9,13},{10,... | collective-permute-start | bytes 245768 | tf_op jit(solution)/shard_map/ppermute | solution.py:386
  30.0 1.3 %collective-permute-start.7 = (bf16[4,48,128]{2,1,0:T(8,128)(2,1)S(1)}, bf16[4,48,128]{2,1,0:T(8,128)(2,1)S(1)}, u32[]{:S(2)}, u32[]{:S(2)}) collective-permute-start(bf16[4,48,128]{2,1,0:T(8,128)(2,1)S(1)} %get-tuple-element.51.y_own), channel_id=1, source_target_pairs={{0,1},{2,3},{4,5},{6,7},{1,0},{3,2},{5,4},{7,6},{8,9},{10,11},{12,... | collective-permute-start | bytes 147464 | tf_op jit(solution)/shard_map/ppermute | solution.py:358
  31.9 4.9 %collective-permute-start.8 = (bf16[4,48,128]{2,1,0:T(8,128)(2,1)S(1)}, bf16[4,48,128]{2,1,0:T(8,128)(2,1)S(1)}, u32[]{:S(2)}, u32[]{:S(2)}) collective-permute-start(bf16[4,48,128]{2,1,0:T(8,128)(2,1)S(1)} %get-tuple-element.59), channel_id=1, source_target_pairs={{0,8},{16,24},{8,0},{24,16},{1,9},{17,25},{9,1},{25,17},{2,10},{18... | collective-permute-start | bytes 147464 | tf_op jit(solution)/shard_map/ppermute | solution.py:358
  33.5 5.0 %collective-permute-start.9 = (bf16[4,48,128]{2,1,0:T(8,128)(2,1)S(1)}, bf16[4,48,128]{2,1,0:T(8,128)(2,1)S(1)}, u32[]{:S(2)}, u32[]{:S(2)}) collective-permute-start(bf16[4,48,128]{2,1,0:T(8,128)(2,1)S(1)} %get-tuple-element.60), channel_id=1, source_target_pairs={{8,16},{24,0},{16,8},{0,24},{9,17},{25,1},{17,9},{1,25},{10,18},{2... | collective-permute-start | bytes 147464 | tf_op jit(solution)/shard_map/ppermute | solution.py:358
  40.7 7.3 %collective-permute-start.10 = (bf16[4,96,128]{2,1,0:T(8,128)(2,1)S(1)}, bf16[4,96,128]{2,1,0:T(8,128)(2,1)S(1)}, u32[]{:S(2)}, u32[]{:S(2)}) collective-permute-start(bf16[4,96,128]{2,1,0:T(8,128)(2,1)S(1)} %get-tuple-element.63), channel_id=1, source_target_pairs={{0,8},{16,24},{8,0},{24,16},{1,9},{17,25},{9,1},{25,17},{2,10},{18... | collective-permute-start | bytes 294920 | tf_op jit(solution)/shard_map/ppermute | solution.py:358
  41.3 6.7 %collective-permute-start.11 = (bf16[4,96,128]{2,1,0:T(8,128)(2,1)S(1)}, bf16[4,96,128]{2,1,0:T(8,128)(2,1)S(1)}, u32[]{:S(2)}, u32[]{:S(2)}) collective-permute-start(bf16[4,96,128]{2,1,0:T(8,128)(2,1)S(1)} %get-tuple-element.64), channel_id=1, source_target_pairs={{8,16},{24,0},{16,8},{0,24},{9,17},{25,1},{17,9},{1,25},{10,18},{2... | collective-permute-start | bytes 294920 | tf_op jit(solution)/shard_map/ppermute | solution.py:358
  42.7 5.3 %collective-permute-start.12 = (bf16[4,96,128]{2,1,0:T(8,128)(2,1)S(1)}, bf16[4,96,128]{2,1,0:T(8,128)(2,1)S(1)}, u32[]{:S(2)}, u32[]{:S(2)}) collective-permute-start(bf16[4,96,128]{2,1,0:T(8,128)(2,1)S(1)} %get-tuple-element.65), channel_id=1, source_target_pairs={{0,1},{2,3},{4,5},{6,7},{1,0},{3,2},{5,4},{7,6},{8,9},{10,11},{12,... | collective-permute-start | bytes 294920 | tf_op jit(solution)/shard_map/ppermute | solution.py:358
  42.8 6.8 %collective-permute-start.13 = (bf16[4,96,128]{2,1,0:T(8,128)(2,1)S(1)}, bf16[4,96,128]{2,1,0:T(8,128)(2,1)S(1)}, u32[]{:S(2)}, u32[]{:S(2)}) collective-permute-start(bf16[4,96,128]{2,1,0:T(8,128)(2,1)S(1)} %get-tuple-element.66), channel_id=1, source_target_pairs={{1,2},{3,4},{5,6},{7,0},{2,1},{4,3},{6,5},{0,7},{9,10},{11,12},{13... | collective-permute-start | bytes 294920 | tf_op jit(solution)/shard_map/ppermute | solution.py:358

commit v4 on v3

--- a/solution.py
+++ b/solution.py
@@ -209,7 +209,7 @@
         mats[s] = block[: coarse // 2] + pltpu.roll(low, cols // 2, 1)
 
 
-def restrict_body(part, outer, xm, xp, ym, yp, pt, mats, face_source, subset, spots, resid, keep, give, total):
+def restrict_body(part, outer, xp, yp, xm, ym, pt, mats, face_source, subset, spots, resid, keep, give, total):
     count = part.shape[0]
     coarse = pt.shape[0]
     total[...] = jnp.zeros_like(total)
@@ -311,7 +311,7 @@
         acc[e] = resid[e] - (dot(oper[e], inside[e]) + dot(outer[e], outside[e]))
 
 
-def smooth_body(part, second, outer, inv, y0, y1, pf, face_source, spots, state, tr, s0, s1, s2, s3, tmp, sides, res):
+def smooth_body(part, second, outer, inv, y1, y0, pf, face_source, spots, state, tr, s0, s1, s2, s3, tmp, sides, res):
     coarse = y0.shape[1]
     count = part.shape[0]
     rows = []
@@ -337,7 +337,7 @@
         acc[e] = rhs[e].astype(F32) - dot(oper[e], stack(values, 2 * dof))
 
 
-def final_body(part, state, outer, inv, xm, xp, ym, yp, face_source, spots, out_far, res, out, sems):
+def final_body(part, state, outer, inv, xp, yp, xm, ym, face_source, spots, out_far, res, out, sems):
     count = state.shape[0]
     copies = chunks(count, ((out, out_far),), sems, OUT_PARTS)
     for e in range(count):
@@ -363,7 +363,8 @@
     x1 = swap(x1, "gx", 1)
     y1 = swap(y1, "gy", 1)
     x0 = swap(x0, "gx", 0)
-    return x0, x1, swap(y0, "gy", 0), y1
+    y0 = swap(y0, "gy", 0)
+    return x0, x1, y0, y1
 
 
 def plus(one, two):
@@ -443,7 +444,7 @@
     )
     resid, keep, give = run(
         restrict_body,
-        (acc, outer, xm, xp, ym, yp, pt, mats, face_source, subset, spots),
+        (acc, outer, xp, yp, xm, ym, pt, mats, face_source, subset, spots),
         [state_s] + [shape((groups // 2, message, cols), BF16)] * 2,
         [pltpu.VMEM((groups, coarse, cols), F32)],
         far_flops,
@@ -474,7 +475,7 @@
     )
     state, tr, *sends = run(
         smooth_body,
-        (acc, second, outer, inv, y0, y1, pf, face_source, spots),
+        (acc, second, outer, inv, y1, y0, pf, face_source, spots),
         [state_s, tr_s] + sends_s,
         [tmps, sides, state_b],
         inv_flops,
@@ -483,7 +484,7 @@
     acc = run(inner_body, (rhs, state, oper, tr, face_source), [state_s], [], apply_flops)[0]
     return run(
         final_body,
-        (acc, state, outer, inv, xm, xp, ym, yp, face_source, spots),
+        (acc, state, outer, inv, xp, yp, xm, ym, face_source, spots),
         [state_s],
         [state_b, pltpu.VMEM((elements, dof, cols), F32), pltpu.SemaphoreType.DMA((1, elements))],
         inv_flops + far_flops,

time: 52.4 us -> 50 us (0.954)
  starting transfers between devices: 17.7 us -> 13.1 us
  waiting for transfers between devices: 14.6 us -> 16.9 us
    ppermute x12, starting transfers between devices: 15.7 us -> 12.4 us  [swap(): return lax.ppermute(value, axis, pairs + [(b, a) for a, b in pairs])]
    ppermute x2, starting transfers between devices: 1.99 us -> 0.68 us  [row_sum(): two = lax.ppermute(one, 'gy', [(i, i ^ step) for i in range(count)])]
    ppermute x2, waiting for transfers between devices: 8.97 us -> 10.3 us  [row_sum(): two = lax.ppermute(one, 'gy', [(i, i ^ step) for i in range(count)])]
    ppermute x12, waiting for transfers between devices: 5.63 us -> 6.62 us  [swap(): return lax.ppermute(value, axis, pairs + [(b, a) for a, b in pairs])]
  transfers between devices with their start and end apart: 14 -> 14, of which waited for: 6 -> 9; matrix products, arithmetic and copies ran while one was open for 0% -> 0% of each run, Pallas kernels for 15% -> 16%
where the time goes in v4:
time: 50 us; the launch traced here: 49.9 us
  Pallas kernels  19.6 us (39%)
  waiting for transfers between devices  16.9 us (34%)
  starting transfers between devices  13.1 us (26%)
    pallas_call x9, Pallas kernels, run(): pl.pallas_call(body, in_specs=[smem if a.dtype == jnp.int32 else hbm if n...  19.6 us
    ppermute x12, starting transfers between devices, swap(): return lax.ppermute(value, axis, pairs + [(b, a) for a, b in pairs])  12.4 us
    ppermute x2, waiting for transfers between devices, row_sum(): two = lax.ppermute(one, 'gy', [(i, i ^ step) for i in range(count)])  10.3 us
    ppermute x12, waiting for transfers between devices, swap(): return lax.ppermute(value, axis, pairs + [(b, a) for a, b in pairs])  6.62 us
  transfers between devices with their start and end apart: 14, of which 9 were waited for; matrix products, arithmetic and copies ran while one was open for 0% of the time, Pallas kernels for 16%

profile of v4, /device:TPU:0, one launch (start us, length us, event | category | flops | bytes accessed | tf_op | source)
XLA Modules:
  0.0 49.9 jit_solution(14752504048256432386)
XLA Ops:
  0.0 0.1 pad_add_fusion.spots
  0.1 3.7 %shard_map.73 = (f32[8,384,128]{2,1,0:T(8,128)S(1)}, bf16[8,6,96,128]{3,2,1,0:T(8,128)(2,1)S(1)}, bf16[8,384,128]{2,1,0:T(8,128)(2,1)S(1)}, bf16[8,384,384]{2,1,...) custom-call(bf16[8,384,128]{2,1,0:T(8,128)(2,1)} %rhs_far.1, ...), custom_call_target="tpu_custom_call" | custom-call | flops 301989888 | bytes 16515088 | tf_op jit(solution)/shard_map/pallas_call | solution.py:39
  3.8 4.0 %collective-permute-start = (bf16[4,96,128]{2,1,0:T(8,128)(2,1)S(1)}, bf16[4,96,128]{2,1,0:T(8,128)(2,1)S(1)}, u32[]{:S(2)}, u32[]{:S(2)}) collective-permute-start(bf16[4,96,128]{2,1,0:T(8,128)(2,1)S(1)} %get-tuple-element.42), channel_id=1, source_target_pairs={{8,16},{24,0},{16,8},{0,24},{9,17},{25,1},{17,9},{1,25},{10,18},{2... | collective-permute-start | bytes 294920 | tf_op jit(solution)/shard_map/ppermute | solution.py:358
  7.8 2.8 %collective-permute-start.1 = (bf16[4,96,128]{2,1,0:T(8,128)(2,1)S(1)}, bf16[4,96,128]{2,1,0:T(8,128)(2,1)S(1)}, u32[]{:S(2)}, u32[]{:S(2)}) collective-permute-start(bf16[4,96,128]{2,1,0:T(8,128)(2,1)S(1)} %get-tuple-element.43), channel_id=1, source_target_pairs={{1,2},{3,4},{5,6},{7,0},{2,1},{4,3},{6,5},{0,7},{9,10},{11,12},{13... | collective-permute-start | bytes 294920 | tf_op jit(solution)/shard_map/ppermute | solution.py:358
  10.6 0.5 %collective-permute-start.2 = (bf16[4,96,128]{2,1,0:T(8,128)(2,1)S(1)}, bf16[4,96,128]{2,1,0:T(8,128)(2,1)S(1)}, u32[]{:S(2)}, u32[]{:S(2)}) collective-permute-start(bf16[4,96,128]{2,1,0:T(8,128)(2,1)S(1)} %get-tuple-element.44), channel_id=1, source_target_pairs={{0,8},{16,24},{8,0},{24,16},{1,9},{17,25},{9,1},{25,17},{2,10},{18... | collective-permute-start | bytes 294920 | tf_op jit(solution)/shard_map/ppermute | solution.py:358
  11.1 0.0 collective-permute-start.3
  11.1 3.0 %shard_map.74 = (f32[8,384,128]{2,1,0:T(8,128)S(1)}, f32[8,24,128]{2,1,0:T(8,128)S(1)}, bf16[8,384,768]{2,1,0:T(8,128)(2,1)S(1)}, bf16[8,384,256]{2,1,0:T(8,128)...) custom-call(bf16[8,384,128]{2,1,0:T(8,128)(2,1)S(1)} %get-tuple-element.36.rhs, ...), custom_call_target="tpu_custom_call" | custom-call | flops 1056964608 | bytes 17682656 | tf_op jit(solution)/shard_map/pallas_call | solution.py:39
  14.2 0.3 collective-permute-done.1.yp
  14.4 0.7 %collective-permute-done.2.xm = bf16[4,96,128]{2,1,0:T(8,128)(2,1)S(1)} collective-permute-done((bf16[4,96,128]{2,1,0:T(8,128)(2,1)S(1)}, bf16[4,96,128]{2,1,0:T(8,128)(2,1)S(1)}, u32[]{:S(2)}, u32[]{:S(2)}) %collective-permute-start.2) | collective-permute-done | bytes 98336 | tf_op jit(solution)/shard_map/ppermute | solution.py:358
  15.2 1.4 %shard_map.75 = (f32[8,384,128]{2,1,0:T(8,128)S(1)}, bf16[4,80,128]{2,1,0:T(8,128)(2,1)S(1)}, bf16[4,80,128]{2,1,0:T(8,128)(2,1)S(1)}) custom-call(f32[8,384,128]{2,1,0:T(8,128)S(1)} %get-tuple-element.40.part, bf16[8,384,256]{2,1,0:T(8,128)(2,1)S(1)} %get-tuple-element.41.outer, bf16[4,96,128]{2,1,0:T(8,128)(2,1)S(1)} %collective-permute-done.xp, ...), custom_call_target="tpu_custom_call" | custom-call | flops 150994944 | bytes 5411056 | tf_op jit(solution)/shard_map/pallas_call | solution.py:39
  16.6 0.1 collective-permute-start.4
  16.6 1.3 %collective-permute-done.4 = bf16[4,80,128]{2,1,0:T(8,128)(2,1)S(1)} collective-permute-done((bf16[4,80,128]{2,1,0:T(8,128)(2,1)S(1)}, bf16[4,80,128]{2,1,0:T(8,128)(2,1)S(1)}, u32[]{:S(2)}, u32[]{:S(2)}) %collective-permute-start.4) | collective-permute-done | bytes 81952 | tf_op jit(solution)/shard_map/ppermute | solution.py:358
  17.9 0.1 collective-permute-start.5
  18.0 4.5 %collective-permute-done.5 = bf16[4,80,128]{2,1,0:T(8,128)(2,1)S(1)} collective-permute-done((bf16[4,80,128]{2,1,0:T(8,128)(2,1)S(1)}, bf16[4,80,128]{2,1,0:T(8,128)(2,1)S(1)}, u32[]{:S(2)}, u32[]{:S(2)}) %collective-permute-start.5) | collective-permute-done | bytes 81952 | tf_op jit(solution)/shard_map/ppermute | solution.py:387
  22.5 0.6 %collective-permute-start.6 = (bf16[4,80,128]{2,1,0:T(8,128)(2,1)S(1)}, bf16[4,80,128]{2,1,0:T(8,128)(2,1)S(1)}, u32[]{:S(2)}, u32[]{:S(2)}) collective-permute-start(bf16[4,80,128]{2,1,0:T(8,128)(2,1)S(1)} %add_convert_fusion.one), channel_id=1, source_target_pairs={{0,4},{1,5},{2,6},{3,7},{4,0},{5,1},{6,2},{7,3},{8,12},{9,13},{10,... | collective-permute-start | bytes 245768 | tf_op jit(solution)/shard_map/ppermute | solution.py:387
  23.2 5.8 %collective-permute-done.6.two = bf16[4,80,128]{2,1,0:T(8,128)(2,1)S(1)} collective-permute-done((bf16[4,80,128]{2,1,0:T(8,128)(2,1)S(1)}, bf16[4,80,128]{2,1,0:T(8,128)(2,1)S(1)}, u32[]{:S(2)}, u32[]{:S(2)}) %collective-permute-start.6) | collective-permute-done | bytes 81952 | tf_op jit(solution)/shard_map/ppermute | solution.py:387
  28.9 1.1 %shard_map.76 = (bf16[4,48,128]{2,1,0:T(8,128)(2,1)S(1)}, f32[2,8,128]{2,1,0:T(8,128)S(1)}) custom-call(bf16[4,80,128]{2,1,0:T(8,128)(2,1)S(1)} %add_convert_fusion.one, bf16[4,80,128]{2,1,0:T(8,128)(2,1)S(1)} %collective-permute-done.6.two, s32[4]{0:T(128)S(1)} %pad_add_fusion.spots), custom_call_target="tpu_custom_call" | custom-call | flops 28311552 | bytes 221200 | tf_op jit(solution)/shard_map/pallas_call | solution.py:39
  30.1 0.1 collective-permute-start.7
  30.2 1.2 %collective-permute-done.7.y_other = bf16[4,48,128]{2,1,0:T(8,128)(2,1)S(1)} collective-permute-done((bf16[4,48,128]{2,1,0:T(8,128)(2,1)S(1)}, bf16[4,48,128]{2,1,0:T(8,128)(2,1)S(1)}, u32[]{:S(2)}, u32[]{:S(2)}) %collective-permute-start.7) | collective-permute-done | bytes 49184 | tf_op jit(solution)/shard_map/ppermute | solution.py:358
  31.4 0.6 %shard_map.77 = (bf16[8,48,128]{2,1,0:T(8,128)(2,1)S(1)}, bf16[4,48,128]{2,1,0:T(8,128)(2,1)S(1)}, bf16[4,48,128]{2,1,0:T(8,128)(2,1)S(1)}) custom-call(bf16[4,48,128]{2,1,0:T(8,128)(2,1)S(1)} %get-tuple-element.51.y_own, bf16[4,48,128]{2,1,0:T(8,128)(2,1)S(1)} %collective-permute-done.7.y_other, s32[8]{0:T(128)S(1)} %copy-done.3, s32[4]{0:T(128)S(1)} %pad_add_fusion.spots), custom_call_target="tpu_custom_call" | custom-call | bytes 294960 | tf_op jit(solution)/shard_map/pallas_call | solution.py:39
  32.0 1.0 %collective-permute-start.8 = (bf16[4,48,128]{2,1,0:T(8,128)(2,1)S(1)}, bf16[4,48,128]{2,1,0:T(8,128)(2,1)S(1)}, u32[]{:S(2)}, u32[]{:S(2)}) collective-permute-start(bf16[4,48,128]{2,1,0:T(8,128)(2,1)S(1)} %get-tuple-element.59), channel_id=1, source_target_pairs={{8,16},{24,0},{16,8},{0,24},{9,17},{25,1},{17,9},{1,25},{10,18},{2... | collective-permute-start | bytes 147464 | tf_op jit(solution)/shard_map/ppermute | solution.py:358
  33.0 1.0 %collective-permute-start.9 = (bf16[4,48,128]{2,1,0:T(8,128)(2,1)S(1)}, bf16[4,48,128]{2,1,0:T(8,128)(2,1)S(1)}, u32[]{:S(2)}, u32[]{:S(2)}) collective-permute-start(bf16[4,48,128]{2,1,0:T(8,128)(2,1)S(1)} %get-tuple-element.60), channel_id=1, source_target_pairs={{0,8},{16,24},{8,0},{24,16},{1,9},{17,25},{9,1},{25,17},{2,10},{18... | collective-permute-start | bytes 147464 | tf_op jit(solution)/shard_map/ppermute | solution.py:358
  34.0 2.9 %shard_map.78 = (f32[8,384,128]{2,1,0:T(8,128)S(1)}, f32[8,384,128]{2,1,0:T(8,128)S(1)}) custom-call(f32[8,384,128]{2,1,0:T(8,128)S(1)} %get-tuple-element.47.resid, f32[8,384,128]{2,1,0:T(8,128)S(1)} %get-tuple-element.37.state, bf16[8,384,768]{2,1,0:T(8,128)(2,1)S(1)} %get-tuple-element.48.oper, bf16[8,384,256]{2,1,0:T(8,128)(2,1)S(1)} %get-tuple-element.41.outer, ...), custom_call_target="tpu_custom_call" | custom-call | flops 528482304 | bytes 12935392 | tf_op jit(solution)/shard_map/pallas_call | solution.py:39
  36.9 0.6 %collective-permute-done.8.y1 = bf16[4,48,128]{2,1,0:T(8,128)(2,1)S(1)} collective-permute-done((bf16[4,48,128]{2,1,0:T(8,128)(2,1)S(1)}, bf16[4,48,128]{2,1,0:T(8,128)(2,1)S(1)}, u32[]{:S(2)}, u32[]{:S(2)}) %collective-permute-start.8) | collective-permute-done | bytes 49184 | tf_op jit(solution)/shard_map/ppermute | solution.py:358
  37.5 2.3 %shard_map.79 = (f32[8,384,128]{2,1,0:T(8,128)S(1)}, bf16[8,6,96,128]{3,2,1,0:T(8,128)(2,1)S(1)}, bf16[4,96,128]{2,1,0:T(8,128)(2,1)S(1)}, bf16[4,96,128]{2,1,0:...) custom-call(f32[8,384,128]{2,1,0:T(8,128)S(1)} %get-tuple-element.56.part, ...), custom_call_target="tpu_custom_call" | custom-call | flops 301989888 | bytes 10469584 | tf_op jit(solution)/shard_map/pallas_call | solution.py:39
  39.7 1.6 %collective-permute-start.10 = (bf16[4,96,128]{2,1,0:T(8,128)(2,1)S(1)}, bf16[4,96,128]{2,1,0:T(8,128)(2,1)S(1)}, u32[]{:S(2)}, u32[]{:S(2)}) collective-permute-start(bf16[4,96,128]{2,1,0:T(8,128)(2,1)S(1)} %get-tuple-element.63), channel_id=1, source_target_pairs={{8,16},{24,0},{16,8},{0,24},{9,17},{25,1},{17,9},{1,25},{10,18},{2... | collective-permute-start | bytes 294920 | tf_op jit(solution)/shard_map/ppermute | solution.py:358
  41.4 0.3 collective-permute-start.11
  41.7 1.0 %collective-permute-start.12 = (bf16[4,96,128]{2,1,0:T(8,128)(2,1)S(1)}, bf16[4,96,128]{2,1,0:T(8,128)(2,1)S(1)}, u32[]{:S(2)}, u32[]{:S(2)}) collective-permute-start(bf16[4,96,128]{2,1,0:T(8,128)(2,1)S(1)} %get-tuple-element.65), channel_id=1, source_target_pairs={{0,8},{16,24},{8,0},{24,16},{1,9},{17,25},{9,1},{25,17},{2,10},{18... | collective-permute-start | bytes 294920 | tf_op jit(solution)/shard_map/ppermute | solution.py:358
  42.7 2.0 %shard_map.80.part = f32[8,384,128]{2,1,0:T(8,128)S(1)} custom-call(bf16[8,384,128]{2,1,0:T(8,128)(2,1)S(1)} %get-tuple-element.36.rhs, f32[8,384,128]{2,1,0:T(8,128)S(1)} %get-tuple-element.61.state, bf16[8,384,768]{2,1,0:T(8,128)(2,1)S(1)} %get-tuple-element.48.oper, bf16[8,6,96,128]{3,2,1,0:T(8,128)(2,1)S(1)} %get-tuple-element.62.tr, s32[8,6]{1,0:T(8,128)S(1)} %copy-done.1), custom_call_target="tpu_custom_call" | custom-call | flops 528482304 | bytes 9830592 | tf_op jit(solution)/shard_map/pallas_call | solution.py:39
  44.7 0.9 %collective-permute-done.10.xp = bf16[4,96,128]{2,1,0:T(8,128)(2,1)S(1)} collective-permute-done((bf16[4,96,128]{2,1,0:T(8,128)(2,1)S(1)}, bf16[4,96,128]{2,1,0:T(8,128)(2,1)S(1)}, u32[]{:S(2)}, u32[]{:S(2)}) %collective-permute-start.10) | collective-permute-done | bytes 98336 | tf_op jit(solution)/shard_map/ppermute | solution.py:358
  45.6 1.6 %collective-permute-done.11.yp = bf16[4,96,128]{2,1,0:T(8,128)(2,1)S(1)} collective-permute-done((bf16[4,96,128]{2,1,0:T(8,128)(2,1)S(1)}, bf16[4,96,128]{2,1,0:T(8,128)(2,1)S(1)}, u32[]{:S(2)}, u32[]{:S(2)}) %collective-permute-start.11) | collective-permute-done | bytes 98336 | tf_op jit(solution)/shard_map/ppermute | solution.py:358
  47.2 2.6 %shard_map.81 = f32[8,384,128]{2,1,0:T(8,128)} custom-call(f32[8,384,128]{2,1,0:T(8,128)S(1)} %shard_map.80.part, f32[8,384,128]{2,1,0:T(8,128)S(1)} %get-tuple-element.61.state, bf16[8,384,256]{2,1,0:T(8,128)(2,1)S(1)} %get-tuple-element.41.outer, bf16[8,384,384]{2,1,0:T(8,128)(2,1)S(1)} %get-tuple-element.58.inv, ...), custom_call_target="tpu_custom_call" | custom-call | flops 452984832 | bytes 9044176 | tf_op jit(solution)/shard_map/pallas_call | solution.py:39
  (16 shorter events, 0.1 us)
Async XLA Ops:
  0.1 11.0 %copy-start = (bf16[8,384,384]{2,1,0:T(8,128)(2,1)S(1)}, bf16[8,384,384]{2,1,0:T(8,128)(2,1)}, u32[]{:S(2)}) copy-start(bf16[8,384,384]{2,1,0:T(8,128)(2,1)} %diag.1) | copy-start | bytes 7077892
  0.1 11.0 %copy-start.1 = (s32[8,6]{1,0:T(8,128)S(1)}, s32[8,6]{1,0:T(8,128)}, u32[]{:S(2)}) copy-start(s32[8,6]{1,0:T(8,128)} %face_source.11) | copy-start | bytes 580
  0.1 11.0 %copy-start.2 = (bf16[384,48]{0,1:T(8,128)(2,1)S(1)}, bf16[384,48]{0,1:T(8,128)(2,1)}, u32[]{:S(2)}) copy-start(bf16[384,48]{0,1:T(8,128)(2,1)} %param.11) | copy-start | bytes 110596
  0.1 11.0 %copy-start.3 = (s32[8]{0:T(128)S(1)}, s32[8]{0:T(128)}, u32[]{:S(2)}) copy-start(s32[8]{0:T(128)} %subset.7) | copy-start | bytes 100
  3.8 10.3 %collective-permute-start = (bf16[4,96,128]{2,1,0:T(8,128)(2,1)S(1)}, bf16[4,96,128]{2,1,0:T(8,128)(2,1)S(1)}, u32[]{:S(2)}, u32[]{:S(2)}) collective-permute-start(bf16[4,96,128]{2,1,0:T(8,128)(2,1)S(1)} %get-tuple-element.42), channel_id=1, source_target_pairs={{8,16},{24,0},{16,8},{0,24},{9,17},{25,1},{17,9},{1,25},{10,18},{2... | collective-permute-start | bytes 294920 | tf_op jit(solution)/shard_map/ppermute | solution.py:358
  7.8 6.6 %collective-permute-start.1 = (bf16[4,96,128]{2,1,0:T(8,128)(2,1)S(1)}, bf16[4,96,128]{2,1,0:T(8,128)(2,1)S(1)}, u32[]{:S(2)}, u32[]{:S(2)}) collective-permute-start(bf16[4,96,128]{2,1,0:T(8,128)(2,1)S(1)} %get-tuple-element.43), channel_id=1, source_target_pairs={{1,2},{3,4},{5,6},{7,0},{2,1},{4,3},{6,5},{0,7},{9,10},{11,12},{13... | collective-permute-start | bytes 294920 | tf_op jit(solution)/shard_map/ppermute | solution.py:358
  10.6 4.6 %collective-permute-start.2 = (bf16[4,96,128]{2,1,0:T(8,128)(2,1)S(1)}, bf16[4,96,128]{2,1,0:T(8,128)(2,1)S(1)}, u32[]{:S(2)}, u32[]{:S(2)}) collective-permute-start(bf16[4,96,128]{2,1,0:T(8,128)(2,1)S(1)} %get-tuple-element.44), channel_id=1, source_target_pairs={{0,8},{16,24},{8,0},{24,16},{1,9},{17,25},{9,1},{25,17},{2,10},{18... | collective-permute-start | bytes 294920 | tf_op jit(solution)/shard_map/ppermute | solution.py:358
  11.1 4.1 %collective-permute-start.3 = (bf16[4,96,128]{2,1,0:T(8,128)(2,1)S(1)}, bf16[4,96,128]{2,1,0:T(8,128)(2,1)S(1)}, u32[]{:S(2)}, u32[]{:S(2)}) collective-permute-start(bf16[4,96,128]{2,1,0:T(8,128)(2,1)S(1)} %get-tuple-element.45), channel_id=1, source_target_pairs={{0,1},{2,3},{4,5},{6,7},{1,0},{3,2},{5,4},{7,6},{8,9},{10,11},{12,... | collective-permute-start | bytes 294920 | tf_op jit(solution)/shard_map/ppermute | solution.py:358
  16.6 1.3 %collective-permute-start.4 = (bf16[4,80,128]{2,1,0:T(8,128)(2,1)S(1)}, bf16[4,80,128]{2,1,0:T(8,128)(2,1)S(1)}, u32[]{:S(2)}, u32[]{:S(2)}) collective-permute-start(bf16[4,80,128]{2,1,0:T(8,128)(2,1)S(1)} %get-tuple-element.50), channel_id=1, source_target_pairs={{0,1},{2,3},{4,5},{6,7},{1,0},{3,2},{5,4},{7,6},{8,9},{10,11},{12,... | collective-permute-start | bytes 245768 | tf_op jit(solution)/shard_map/ppermute | solution.py:358
  17.9 4.6 %collective-permute-start.5 = (bf16[4,80,128]{2,1,0:T(8,128)(2,1)S(1)}, bf16[4,80,128]{2,1,0:T(8,128)(2,1)S(1)}, u32[]{:S(2)}, u32[]{:S(2)}) collective-permute-start(bf16[4,80,128]{2,1,0:T(8,128)(2,1)S(1)} %add_convert_fusion.1), channel_id=1, source_target_pairs={{0,2},{1,3},{2,0},{3,1},{4,6},{5,7},{6,4},{7,5},{8,10},{9,11},{10,... | collective-permute-start | bytes 245768 | tf_op jit(solution)/shard_map/ppermute | solution.py:387
  22.5 6.4 %collective-permute-start.6 = (bf16[4,80,128]{2,1,0:T(8,128)(2,1)S(1)}, bf16[4,80,128]{2,1,0:T(8,128)(2,1)S(1)}, u32[]{:S(2)}, u32[]{:S(2)}) collective-permute-start(bf16[4,80,128]{2,1,0:T(8,128)(2,1)S(1)} %add_convert_fusion.one), channel_id=1, source_target_pairs={{0,4},{1,5},{2,6},{3,7},{4,0},{5,1},{6,2},{7,3},{8,12},{9,13},{10,... | collective-permute-start | bytes 245768 | tf_op jit(solution)/shard_map/ppermute | solution.py:387
  30.1 1.3 %collective-permute-start.7 = (bf16[4,48,128]{2,1,0:T(8,128)(2,1)S(1)}, bf16[4,48,128]{2,1,0:T(8,128)(2,1)S(1)}, u32[]{:S(2)}, u32[]{:S(2)}) collective-permute-start(bf16[4,48,128]{2,1,0:T(8,128)(2,1)S(1)} %get-tuple-element.51.y_own), channel_id=1, source_target_pairs={{0,1},{2,3},{4,5},{6,7},{1,0},{3,2},{5,4},{7,6},{8,9},{10,11},{12,... | collective-permute-start | bytes 147464 | tf_op jit(solution)/shard_map/ppermute | solution.py:358
  32.0 5.5 %collective-permute-start.8 = (bf16[4,48,128]{2,1,0:T(8,128)(2,1)S(1)}, bf16[4,48,128]{2,1,0:T(8,128)(2,1)S(1)}, u32[]{:S(2)}, u32[]{:S(2)}) collective-permute-start(bf16[4,48,128]{2,1,0:T(8,128)(2,1)S(1)} %get-tuple-element.59), channel_id=1, source_target_pairs={{8,16},{24,0},{16,8},{0,24},{9,17},{25,1},{17,9},{1,25},{10,18},{2... | collective-permute-start | bytes 147464 | tf_op jit(solution)/shard_map/ppermute | solution.py:358
  33.0 4.5 %collective-permute-start.9 = (bf16[4,48,128]{2,1,0:T(8,128)(2,1)S(1)}, bf16[4,48,128]{2,1,0:T(8,128)(2,1)S(1)}, u32[]{:S(2)}, u32[]{:S(2)}) collective-permute-start(bf16[4,48,128]{2,1,0:T(8,128)(2,1)S(1)} %get-tuple-element.60), channel_id=1, source_target_pairs={{0,8},{16,24},{8,0},{24,16},{1,9},{17,25},{9,1},{25,17},{2,10},{18... | collective-permute-start | bytes 147464 | tf_op jit(solution)/shard_map/ppermute | solution.py:358
  39.7 5.9 %collective-permute-start.10 = (bf16[4,96,128]{2,1,0:T(8,128)(2,1)S(1)}, bf16[4,96,128]{2,1,0:T(8,128)(2,1)S(1)}, u32[]{:S(2)}, u32[]{:S(2)}) collective-permute-start(bf16[4,96,128]{2,1,0:T(8,128)(2,1)S(1)} %get-tuple-element.63), channel_id=1, source_target_pairs={{8,16},{24,0},{16,8},{0,24},{9,17},{25,1},{17,9},{1,25},{10,18},{2... | collective-permute-start | bytes 294920 | tf_op jit(solution)/shard_map/ppermute | solution.py:358
  41.4 5.8 %collective-permute-start.11 = (bf16[4,96,128]{2,1,0:T(8,128)(2,1)S(1)}, bf16[4,96,128]{2,1,0:T(8,128)(2,1)S(1)}, u32[]{:S(2)}, u32[]{:S(2)}) collective-permute-start(bf16[4,96,128]{2,1,0:T(8,128)(2,1)S(1)} %get-tuple-element.64), channel_id=1, source_target_pairs={{1,2},{3,4},{5,6},{7,0},{2,1},{4,3},{6,5},{0,7},{9,10},{11,12},{13... | collective-permute-start | bytes 294920 | tf_op jit(solution)/shard_map/ppermute | solution.py:358
  41.7 5.5 %collective-permute-start.12 = (bf16[4,96,128]{2,1,0:T(8,128)(2,1)S(1)}, bf16[4,96,128]{2,1,0:T(8,128)(2,1)S(1)}, u32[]{:S(2)}, u32[]{:S(2)}) collective-permute-start(bf16[4,96,128]{2,1,0:T(8,128)(2,1)S(1)} %get-tuple-element.65), channel_id=1, source_target_pairs={{0,8},{16,24},{8,0},{24,16},{1,9},{17,25},{9,1},{25,17},{2,10},{18... | collective-permute-start | bytes 294920 | tf_op jit(solution)/shard_map/ppermute | solution.py:358
  42.7 4.5 %collective-permute-start.13 = (bf16[4,96,128]{2,1,0:T(8,128)(2,1)S(1)}, bf16[4,96,128]{2,1,0:T(8,128)(2,1)S(1)}, u32[]{:S(2)}, u32[]{:S(2)}) collective-permute-start(bf16[4,96,128]{2,1,0:T(8,128)(2,1)S(1)} %get-tuple-element.66), channel_id=1, source_target_pairs={{0,1},{2,3},{4,5},{6,7},{1,0},{3,2},{5,4},{7,6},{8,9},{10,11},{12,... | collective-permute-start | bytes 294920 | tf_op jit(solution)/shard_map/ppermute | solution.py:358

commit v5 on v4

--- a/solution.py
+++ b/solution.py
@@ -240,12 +240,14 @@
     return high, (value - high.astype(F32)).astype(BF16)
 
 
-def coarse_body(one, two, spots, y_own, names):
-    groups, coarse, cols = y_own.shape
+def coarse_body(own, other, subset, spots, y_all, near, far_y, names, held):
+    groups, coarse, cols = y_all.shape
+    share = groups // 2
+    core = lax.rem(spots[0], 2)
     half = coarse // 2
     rights, blocks, thetas, ys = [], [], [], []
     for s in range(groups):
-        both = one[s].astype(F32) + two[s].astype(F32)
+        both = (own[s] if s < share else other[s - share]).astype(F32)
         right = both[0:coarse]
         packed = both[coarse : coarse + half]
         block = jnp.concatenate([packed, pltpu.roll(packed, cols // 2, 1)], axis=0)
@@ -263,28 +265,21 @@
             sides.append(jnp.concatenate([high, low, high], axis=0))
         applied = [dot(blocks[s], sides[s]) for s in range(groups)]
         ys = [ys[s] + thetas[s] * (rights[s] - applied[s]) for s in range(groups)]
-    for s in range(groups):
-        y_own[s] = ys[s].astype(BF16)
+    for s in range(share):
+        y_all[core * share + s] = ys[s].astype(BF16)
+        y_all[(1 - core) * share + s] = ys[share + s].astype(BF16)
+    for e in range(subset.shape[0]):
+        held[e % 2, e // 2] = y_all[subset[e]]
+    pack_sends(order(spots)[0], held[0], held[1], near, far_y)
     start = coarse + half
     count = names.shape[1]
     lane = lax.broadcasted_iota(jnp.int32, (count, cols), 1)
     for side in (0, 1):
         slot = lax.div(spots[1 + side], 2)
-        far = one[slot].astype(F32) + two[slot].astype(F32)
+        far = own[slot].astype(F32)
         mine = (lane >= cols // 2) == (lax.rem(spots[1 + side], 2) == 1)
         far = jnp.where(mine, far[start : start + count], 0.0)
         names[side] = far + pltpu.roll(far, cols // 2, 1)
-
-
-def choose_body(y_own, y_other, subset, spots, y_all, near, far, sides):
-    share = y_own.shape[0]
-    half = lax.rem(spots[0], 2)
-    for s in range(share):
-        y_all[half * share + s] = y_own[s]
-        y_all[(1 - half) * share + s] = y_other[s]
-    for e in range(subset.shape[0]):
-        sides[e % 2, e // 2] = y_all[subset[e]]
-    pack_sends(order(spots)[0], sides[0], sides[1], near, far)
 
 
 def second_body(resid, state, oper, outer, y_all, prolong, pf, names, face_source, subset, acc, second):
@@ -373,20 +368,13 @@
 
 def row_sum(keep, give):
     count = lax.axis_size("gy")
-    one, two = keep, swap(give, "gy", 0)
-    if count & (count - 1):
-        part = plus(one, two)
-        for step in range(2, count, 2):
-            one, two = plus(one, two) if step > 2 else part, lax.ppermute(
-                part, "gy", [(i, (i + step) % count) for i in range(count)]
-            )
-        return one, two
-    step = 2
-    while step < count:
-        one = plus(one, two)
-        two = lax.ppermute(one, "gy", [(i, i ^ step) for i in range(count)])
-        step *= 2
-    return one, two
+    part = plus(keep, swap(give, "gy", 0))
+    pairs = not count & (count - 1)
+    parts = [part] + [
+        lax.ppermute(part, "gy", [(i, i ^ step if pairs else (i + step) % count) for i in range(count)])
+        for step in range(2, count, 2)
+    ]
+    return sum(part.astype(F32) for part in parts).astype(BF16)
 
 
 def on_device(rhs, diag_blocks, inverse_blocks, couplings, prolong, face_source, subset):
@@ -449,20 +437,13 @@
         [pltpu.VMEM((groups, coarse, cols), F32)],
         far_flops,
     )
-    one, two = row_sum(keep, give)
-    y_own, names = run(
+    own = row_sum(keep, give)
+    y_all, y0, y1, names = run(
         coarse_body,
-        (one, two, spots),
-        [shape((groups // 2, coarse, cols), BF16), shape((2, elements, cols), F32)],
-        [],
-        3 * groups * coarse * coarse * cols * CITER,
-    )
-    y_all, y0, y1 = run(
-        choose_body,
-        (y_own, swap(y_own, "gy", 0), subset, spots),
-        [shape((groups, coarse, cols), BF16), y_s, y_s],
+        (own, swap(own, "gy", 0), subset, spots),
+        [shape((groups, coarse, cols), BF16), y_s, y_s, shape((2, elements, cols), F32)],
         [pltpu.VMEM((2, half, coarse, cols), BF16)],
-        0,
+        6 * groups * coarse * coarse * cols * CITER,
     )
     y1 = swap(y1, "gx", 1)
     y0 = swap(y0, "gx", 0)

time: 50 us -> 48.5 us (0.970)
  waiting for transfers between devices: 16.9 us -> 12 us
  starting transfers between devices: 13.1 us -> 17 us
  Pallas kernels: 19.6 us -> 19.1 us
    ppermute x2 -> x3, waiting for transfers between devices: 10.3 us -> 5.43 us  [row_sum(): lax.ppermute(part, 'gy', [(i, i ^ step if pairs else (i + step) % count)...]
    ppermute x2 -> x3, starting transfers between devices: 0.68 us -> 4.45 us  [row_sum(): lax.ppermute(part, 'gy', [(i, i ^ step if pairs else (i + step) % count)...]
    pallas_call x9 -> x8, Pallas kernels: 19.6 us -> 19.1 us  [run(): pl.pallas_call(body, in_specs=[smem if a.dtype == jnp.int32 else hbm if n...]
  transfers between devices with their start and end apart: 14 -> 15, of which waited for: 9 -> 9; matrix products, arithmetic and copies ran while one was open for 0% -> 0% of each run, Pallas kernels for 16% -> 16%
where the time goes in v5:
time: 48.5 us; the launch traced here: 48.4 us
  Pallas kernels  19.1 us (39%)
  starting transfers between devices  17 us (35%)
  waiting for transfers between devices  12 us (25%)
    pallas_call x8, Pallas kernels, run(): pl.pallas_call(body, in_specs=[smem if a.dtype == jnp.int32 else hbm if n...  19.1 us
    ppermute x12, starting transfers between devices, swap(): return lax.ppermute(value, axis, pairs + [(b, a) for a, b in pairs])  12.5 us
    ppermute x12, waiting for transfers between devices, swap(): return lax.ppermute(value, axis, pairs + [(b, a) for a, b in pairs])  6.61 us
    ppermute x3, waiting for transfers between devices, row_sum(): lax.ppermute(part, 'gy', [(i, i ^ step if pairs else (i + step) % count)...  5.43 us
    ppermute x3, starting transfers between devices, row_sum(): lax.ppermute(part, 'gy', [(i, i ^ step if pairs else (i + step) % count)...  4.45 us
  transfers between devices with their start and end apart: 15, of which 9 were waited for; matrix products, arithmetic and copies ran while one was open for 0% of the time, Pallas kernels for 16%

profile of v5, /device:TPU:0, one launch (start us, length us, event | category | flops | bytes accessed | tf_op | source)
XLA Modules:
  0.0 48.4 jit_solution(13965887346787743340)
XLA Ops:
  0.0 0.1 pad_add_fusion.spots
  0.1 3.7 %shard_map.73 = (f32[8,384,128]{2,1,0:T(8,128)S(1)}, bf16[8,6,96,128]{3,2,1,0:T(8,128)(2,1)S(1)}, bf16[8,384,128]{2,1,0:T(8,128)(2,1)S(1)}, bf16[8,384,384]{2,1,...) custom-call(bf16[8,384,128]{2,1,0:T(8,128)(2,1)} %rhs_far.1, ...), custom_call_target="tpu_custom_call" | custom-call | flops 301989888 | bytes 16515088 | tf_op jit(solution)/shard_map/pallas_call | solution.py:39
  3.8 4.0 %collective-permute-start = (bf16[4,96,128]{2,1,0:T(8,128)(2,1)S(1)}, bf16[4,96,128]{2,1,0:T(8,128)(2,1)S(1)}, u32[]{:S(2)}, u32[]{:S(2)}) collective-permute-start(bf16[4,96,128]{2,1,0:T(8,128)(2,1)S(1)} %get-tuple-element.41), channel_id=1, source_target_pairs={{8,16},{24,0},{16,8},{0,24},{9,17},{25,1},{17,9},{1,25},{10,18},{2... | collective-permute-start | bytes 294920 | tf_op jit(solution)/shard_map/ppermute | solution.py:353
  7.8 2.8 %collective-permute-start.1 = (bf16[4,96,128]{2,1,0:T(8,128)(2,1)S(1)}, bf16[4,96,128]{2,1,0:T(8,128)(2,1)S(1)}, u32[]{:S(2)}, u32[]{:S(2)}) collective-permute-start(bf16[4,96,128]{2,1,0:T(8,128)(2,1)S(1)} %get-tuple-element.42), channel_id=1, source_target_pairs={{1,2},{3,4},{5,6},{7,0},{2,1},{4,3},{6,5},{0,7},{9,10},{11,12},{13... | collective-permute-start | bytes 294920 | tf_op jit(solution)/shard_map/ppermute | solution.py:353
  10.6 0.5 %collective-permute-start.2 = (bf16[4,96,128]{2,1,0:T(8,128)(2,1)S(1)}, bf16[4,96,128]{2,1,0:T(8,128)(2,1)S(1)}, u32[]{:S(2)}, u32[]{:S(2)}) collective-permute-start(bf16[4,96,128]{2,1,0:T(8,128)(2,1)S(1)} %get-tuple-element.43), channel_id=1, source_target_pairs={{0,8},{16,24},{8,0},{24,16},{1,9},{17,25},{9,1},{25,17},{2,10},{18... | collective-permute-start | bytes 294920 | tf_op jit(solution)/shard_map/ppermute | solution.py:353
  11.1 0.0 collective-permute-start.3
  11.1 3.0 %shard_map.74 = (f32[8,384,128]{2,1,0:T(8,128)S(1)}, f32[8,24,128]{2,1,0:T(8,128)S(1)}, bf16[8,384,768]{2,1,0:T(8,128)(2,1)S(1)}, bf16[8,384,256]{2,1,0:T(8,128)...) custom-call(bf16[8,384,128]{2,1,0:T(8,128)(2,1)S(1)} %get-tuple-element.35.rhs, ...), custom_call_target="tpu_custom_call" | custom-call | flops 1056964608 | bytes 17682656 | tf_op jit(solution)/shard_map/pallas_call | solution.py:39
  14.1 0.3 collective-permute-done.1.yp
  14.4 0.7 %collective-permute-done.2.xm = bf16[4,96,128]{2,1,0:T(8,128)(2,1)S(1)} collective-permute-done((bf16[4,96,128]{2,1,0:T(8,128)(2,1)S(1)}, bf16[4,96,128]{2,1,0:T(8,128)(2,1)S(1)}, u32[]{:S(2)}, u32[]{:S(2)}) %collective-permute-start.2) | collective-permute-done | bytes 98336 | tf_op jit(solution)/shard_map/ppermute | solution.py:353
  15.2 0.0 collective-permute-done.3.ym
  15.2 1.4 %shard_map.75 = (f32[8,384,128]{2,1,0:T(8,128)S(1)}, bf16[4,80,128]{2,1,0:T(8,128)(2,1)S(1)}, bf16[4,80,128]{2,1,0:T(8,128)(2,1)S(1)}) custom-call(f32[8,384,128]{2,1,0:T(8,128)S(1)} %get-tuple-element.39.part, bf16[8,384,256]{2,1,0:T(8,128)(2,1)S(1)} %get-tuple-element.40.outer, bf16[4,96,128]{2,1,0:T(8,128)(2,1)S(1)} %collective-permute-done.xp, ...), custom_call_target="tpu_custom_call" | custom-call | flops 150994944 | bytes 5411056 | tf_op jit(solution)/shard_map/pallas_call | solution.py:39
  16.6 0.1 collective-permute-start.4
  16.6 1.3 %collective-permute-done.4 = bf16[4,80,128]{2,1,0:T(8,128)(2,1)S(1)} collective-permute-done((bf16[4,80,128]{2,1,0:T(8,128)(2,1)S(1)}, bf16[4,80,128]{2,1,0:T(8,128)(2,1)S(1)}, u32[]{:S(2)}, u32[]{:S(2)}) %collective-permute-start.4) | collective-permute-done | bytes 81952 | tf_op jit(solution)/shard_map/ppermute | solution.py:353
  17.9 1.5 %collective-permute-start.7 = (bf16[4,80,128]{2,1,0:T(8,128)(2,1)S(1)}, bf16[4,80,128]{2,1,0:T(8,128)(2,1)S(1)}, u32[]{:S(2)}, u32[]{:S(2)}) collective-permute-start(bf16[4,80,128]{2,1,0:T(8,128)(2,1)S(1)} %add_convert_fusion.1), channel_id=1, source_target_pairs={{0,6},{1,7},{2,4},{3,5},{4,2},{5,3},{6,0},{7,1},{8,14},{9,15},{10,... | collective-permute-start | bytes 245768 | tf_op jit(solution)/shard_map/ppermute | solution.py:374
  19.5 2.9 %collective-permute-start.5 = (bf16[4,80,128]{2,1,0:T(8,128)(2,1)S(1)}, bf16[4,80,128]{2,1,0:T(8,128)(2,1)S(1)}, u32[]{:S(2)}, u32[]{:S(2)}) collective-permute-start(bf16[4,80,128]{2,1,0:T(8,128)(2,1)S(1)} %add_convert_fusion.1), channel_id=1, source_target_pairs={{0,2},{1,3},{2,0},{3,1},{4,6},{5,7},{6,4},{7,5},{8,10},{9,11},{10,... | collective-permute-start | bytes 245768 | tf_op jit(solution)/shard_map/ppermute | solution.py:374
  22.4 2.8 %collective-permute-done.7 = bf16[4,80,128]{2,1,0:T(8,128)(2,1)S(1)} collective-permute-done((bf16[4,80,128]{2,1,0:T(8,128)(2,1)S(1)}, bf16[4,80,128]{2,1,0:T(8,128)(2,1)S(1)}, u32[]{:S(2)}, u32[]{:S(2)}) %collective-permute-start.7) | collective-permute-done | bytes 81952 | tf_op jit(solution)/shard_map/ppermute | solution.py:374
  25.2 2.6 %collective-permute-done.6 = bf16[4,80,128]{2,1,0:T(8,128)(2,1)S(1)} collective-permute-done((bf16[4,80,128]{2,1,0:T(8,128)(2,1)S(1)}, bf16[4,80,128]{2,1,0:T(8,128)(2,1)S(1)}, u32[]{:S(2)}, u32[]{:S(2)}) %collective-permute-start.6) | collective-permute-done | bytes 81952 | tf_op jit(solution)/shard_map/ppermute | solution.py:374
  27.9 0.1 collective-permute-start.8
  28.0 1.3 %collective-permute-done.8.other = bf16[4,80,128]{2,1,0:T(8,128)(2,1)S(1)} collective-permute-done((bf16[4,80,128]{2,1,0:T(8,128)(2,1)S(1)}, bf16[4,80,128]{2,1,0:T(8,128)(2,1)S(1)}, u32[]{:S(2)}, u32[]{:S(2)}) %collective-permute-start.8) | collective-permute-done | bytes 81952 | tf_op jit(solution)/shard_map/ppermute | solution.py:353
  29.2 1.2 %shard_map.76 = (bf16[8,48,128]{2,1,0:T(8,128)(2,1)S(1)}, bf16[4,48,128]{2,1,0:T(8,128)(2,1)S(1)}, bf16[4,48,128]{2,1,0:T(8,128)(2,1)S(1)}, f32[2,8,128]{2,1,0:T(8,128)S(1)}) custom-call(bf16[4,80,128]{2,1,0:T(8,128)(2,1)S(1)} %add_convert_fusion.own, bf16[4,80,128]{2,1,0:T(8,128)(2,1)S(1)} %collective-permute-done.8.other, s32[8]{0:T(128)S(1)} %copy-done.3, ...), custom_call_target="tpu_custom_call" | custom-call | flops 56623104 | bytes 368688 | tf_op jit(solution)/shard_map/pallas_call | solution.py:39
  30.5 0.8 %collective-permute-start.9 = (bf16[4,48,128]{2,1,0:T(8,128)(2,1)S(1)}, bf16[4,48,128]{2,1,0:T(8,128)(2,1)S(1)}, u32[]{:S(2)}, u32[]{:S(2)}) collective-permute-start(bf16[4,48,128]{2,1,0:T(8,128)(2,1)S(1)} %get-tuple-element.57), channel_id=1, source_target_pairs={{8,16},{24,0},{16,8},{0,24},{9,17},{25,1},{17,9},{1,25},{10,18},{2... | collective-permute-start | bytes 147464 | tf_op jit(solution)/shard_map/ppermute | solution.py:353
  31.3 1.2 %collective-permute-start.10 = (bf16[4,48,128]{2,1,0:T(8,128)(2,1)S(1)}, bf16[4,48,128]{2,1,0:T(8,128)(2,1)S(1)}, u32[]{:S(2)}, u32[]{:S(2)}) collective-permute-start(bf16[4,48,128]{2,1,0:T(8,128)(2,1)S(1)} %get-tuple-element.58), channel_id=1, source_target_pairs={{0,8},{16,24},{8,0},{24,16},{1,9},{17,25},{9,1},{25,17},{2,10},{18... | collective-permute-start | bytes 147464 | tf_op jit(solution)/shard_map/ppermute | solution.py:353
  32.5 2.9 %shard_map.77 = (f32[8,384,128]{2,1,0:T(8,128)S(1)}, f32[8,384,128]{2,1,0:T(8,128)S(1)}) custom-call(f32[8,384,128]{2,1,0:T(8,128)S(1)} %get-tuple-element.46.resid, f32[8,384,128]{2,1,0:T(8,128)S(1)} %get-tuple-element.36.state, bf16[8,384,768]{2,1,0:T(8,128)(2,1)S(1)} %get-tuple-element.47.oper, bf16[8,384,256]{2,1,0:T(8,128)(2,1)S(1)} %get-tuple-element.40.outer, ...), custom_call_target="tpu_custom_call" | custom-call | flops 528482304 | bytes 12935392 | tf_op jit(solution)/shard_map/pallas_call | solution.py:39
  35.4 0.4 collective-permute-done.9.y1
  35.8 2.3 %shard_map.78 = (f32[8,384,128]{2,1,0:T(8,128)S(1)}, bf16[8,6,96,128]{3,2,1,0:T(8,128)(2,1)S(1)}, bf16[4,96,128]{2,1,0:T(8,128)(2,1)S(1)}, bf16[4,96,128]{2,1,0:...) custom-call(f32[8,384,128]{2,1,0:T(8,128)S(1)} %get-tuple-element.54.part, ...), custom_call_target="tpu_custom_call" | custom-call | flops 301989888 | bytes 10469584 | tf_op jit(solution)/shard_map/pallas_call | solution.py:39
  38.0 1.8 %collective-permute-start.11 = (bf16[4,96,128]{2,1,0:T(8,128)(2,1)S(1)}, bf16[4,96,128]{2,1,0:T(8,128)(2,1)S(1)}, u32[]{:S(2)}, u32[]{:S(2)}) collective-permute-start(bf16[4,96,128]{2,1,0:T(8,128)(2,1)S(1)} %get-tuple-element.61), channel_id=1, source_target_pairs={{8,16},{24,0},{16,8},{0,24},{9,17},{25,1},{17,9},{1,25},{10,18},{2... | collective-permute-start | bytes 294920 | tf_op jit(solution)/shard_map/ppermute | solution.py:353
  39.9 0.6 %collective-permute-start.12 = (bf16[4,96,128]{2,1,0:T(8,128)(2,1)S(1)}, bf16[4,96,128]{2,1,0:T(8,128)(2,1)S(1)}, u32[]{:S(2)}, u32[]{:S(2)}) collective-permute-start(bf16[4,96,128]{2,1,0:T(8,128)(2,1)S(1)} %get-tuple-element.62), channel_id=1, source_target_pairs={{1,2},{3,4},{5,6},{7,0},{2,1},{4,3},{6,5},{0,7},{9,10},{11,12},{13... | collective-permute-start | bytes 294920 | tf_op jit(solution)/shard_map/ppermute | solution.py:353
  40.5 0.6 %collective-permute-start.13 = (bf16[4,96,128]{2,1,0:T(8,128)(2,1)S(1)}, bf16[4,96,128]{2,1,0:T(8,128)(2,1)S(1)}, u32[]{:S(2)}, u32[]{:S(2)}) collective-permute-start(bf16[4,96,128]{2,1,0:T(8,128)(2,1)S(1)} %get-tuple-element.63), channel_id=1, source_target_pairs={{0,8},{16,24},{8,0},{24,16},{1,9},{17,25},{9,1},{25,17},{2,10},{18... | collective-permute-start | bytes 294920 | tf_op jit(solution)/shard_map/ppermute | solution.py:353
  41.1 2.0 %shard_map.79.part = f32[8,384,128]{2,1,0:T(8,128)S(1)} custom-call(bf16[8,384,128]{2,1,0:T(8,128)(2,1)S(1)} %get-tuple-element.35.rhs, f32[8,384,128]{2,1,0:T(8,128)S(1)} %get-tuple-element.59.state, bf16[8,384,768]{2,1,0:T(8,128)(2,1)S(1)} %get-tuple-element.47.oper, bf16[8,6,96,128]{3,2,1,0:T(8,128)(2,1)S(1)} %get-tuple-element.60.tr, s32[8,6]{1,0:T(8,128)S(1)} %copy-done.1), custom_call_target="tpu_custom_call" | custom-call | flops 528482304 | bytes 9830592 | tf_op jit(solution)/shard_map/pallas_call | solution.py:39
  43.1 1.3 %collective-permute-done.11.xp = bf16[4,96,128]{2,1,0:T(8,128)(2,1)S(1)} collective-permute-done((bf16[4,96,128]{2,1,0:T(8,128)(2,1)S(1)}, bf16[4,96,128]{2,1,0:T(8,128)(2,1)S(1)}, u32[]{:S(2)}, u32[]{:S(2)}) %collective-permute-start.11) | collective-permute-done | bytes 98336 | tf_op jit(solution)/shard_map/ppermute | solution.py:353
  44.4 1.3 %collective-permute-done.12.yp = bf16[4,96,128]{2,1,0:T(8,128)(2,1)S(1)} collective-permute-done((bf16[4,96,128]{2,1,0:T(8,128)(2,1)S(1)}, bf16[4,96,128]{2,1,0:T(8,128)(2,1)S(1)}, u32[]{:S(2)}, u32[]{:S(2)}) %collective-permute-start.12) | collective-permute-done | bytes 98336 | tf_op jit(solution)/shard_map/ppermute | solution.py:353
  45.7 2.6 %shard_map.80 = f32[8,384,128]{2,1,0:T(8,128)} custom-call(f32[8,384,128]{2,1,0:T(8,128)S(1)} %shard_map.79.part, f32[8,384,128]{2,1,0:T(8,128)S(1)} %get-tuple-element.59.state, bf16[8,384,256]{2,1,0:T(8,128)(2,1)S(1)} %get-tuple-element.40.outer, bf16[8,384,384]{2,1,0:T(8,128)(2,1)S(1)} %get-tuple-element.56.inv, ...), custom_call_target="tpu_custom_call" | custom-call | flops 452984832 | bytes 9044176 | tf_op jit(solution)/shard_map/pallas_call | solution.py:39
  (17 shorter events, 0.1 us)
Async XLA Ops:
  0.1 11.0 %copy-start = (bf16[8,384,384]{2,1,0:T(8,128)(2,1)S(1)}, bf16[8,384,384]{2,1,0:T(8,128)(2,1)}, u32[]{:S(2)}) copy-start(bf16[8,384,384]{2,1,0:T(8,128)(2,1)} %diag.1) | copy-start | bytes 7077892
  0.1 11.0 %copy-start.1 = (s32[8,6]{1,0:T(8,128)S(1)}, s32[8,6]{1,0:T(8,128)}, u32[]{:S(2)}) copy-start(s32[8,6]{1,0:T(8,128)} %face_source.11) | copy-start | bytes 580
  0.1 11.0 %copy-start.2 = (bf16[384,48]{0,1:T(8,128)(2,1)S(1)}, bf16[384,48]{0,1:T(8,128)(2,1)}, u32[]{:S(2)}) copy-start(bf16[384,48]{0,1:T(8,128)(2,1)} %param.11) | copy-start | bytes 110596
  0.1 11.0 %copy-start.3 = (s32[8]{0:T(128)S(1)}, s32[8]{0:T(128)}, u32[]{:S(2)}) copy-start(s32[8]{0:T(128)} %subset.7) | copy-start | bytes 100
  3.8 10.3 %collective-permute-start = (bf16[4,96,128]{2,1,0:T(8,128)(2,1)S(1)}, bf16[4,96,128]{2,1,0:T(8,128)(2,1)S(1)}, u32[]{:S(2)}, u32[]{:S(2)}) collective-permute-start(bf16[4,96,128]{2,1,0:T(8,128)(2,1)S(1)} %get-tuple-element.41), channel_id=1, source_target_pairs={{8,16},{24,0},{16,8},{0,24},{9,17},{25,1},{17,9},{1,25},{10,18},{2... | collective-permute-start | bytes 294920 | tf_op jit(solution)/shard_map/ppermute | solution.py:353
  7.8 6.6 %collective-permute-start.1 = (bf16[4,96,128]{2,1,0:T(8,128)(2,1)S(1)}, bf16[4,96,128]{2,1,0:T(8,128)(2,1)S(1)}, u32[]{:S(2)}, u32[]{:S(2)}) collective-permute-start(bf16[4,96,128]{2,1,0:T(8,128)(2,1)S(1)} %get-tuple-element.42), channel_id=1, source_target_pairs={{1,2},{3,4},{5,6},{7,0},{2,1},{4,3},{6,5},{0,7},{9,10},{11,12},{13... | collective-permute-start | bytes 294920 | tf_op jit(solution)/shard_map/ppermute | solution.py:353
  10.6 4.6 %collective-permute-start.2 = (bf16[4,96,128]{2,1,0:T(8,128)(2,1)S(1)}, bf16[4,96,128]{2,1,0:T(8,128)(2,1)S(1)}, u32[]{:S(2)}, u32[]{:S(2)}) collective-permute-start(bf16[4,96,128]{2,1,0:T(8,128)(2,1)S(1)} %get-tuple-element.43), channel_id=1, source_target_pairs={{0,8},{16,24},{8,0},{24,16},{1,9},{17,25},{9,1},{25,17},{2,10},{18... | collective-permute-start | bytes 294920 | tf_op jit(solution)/shard_map/ppermute | solution.py:353
  11.1 4.1 %collective-permute-start.3 = (bf16[4,96,128]{2,1,0:T(8,128)(2,1)S(1)}, bf16[4,96,128]{2,1,0:T(8,128)(2,1)S(1)}, u32[]{:S(2)}, u32[]{:S(2)}) collective-permute-start(bf16[4,96,128]{2,1,0:T(8,128)(2,1)S(1)} %get-tuple-element.44), channel_id=1, source_target_pairs={{0,1},{2,3},{4,5},{6,7},{1,0},{3,2},{5,4},{7,6},{8,9},{10,11},{12,... | collective-permute-start | bytes 294920 | tf_op jit(solution)/shard_map/ppermute | solution.py:353
  16.6 1.3 %collective-permute-start.4 = (bf16[4,80,128]{2,1,0:T(8,128)(2,1)S(1)}, bf16[4,80,128]{2,1,0:T(8,128)(2,1)S(1)}, u32[]{:S(2)}, u32[]{:S(2)}) collective-permute-start(bf16[4,80,128]{2,1,0:T(8,128)(2,1)S(1)} %get-tuple-element.49), channel_id=1, source_target_pairs={{0,1},{2,3},{4,5},{6,7},{1,0},{3,2},{5,4},{7,6},{8,9},{10,11},{12,... | collective-permute-start | bytes 245768 | tf_op jit(solution)/shard_map/ppermute | solution.py:353
  17.9 7.3 %collective-permute-start.7 = (bf16[4,80,128]{2,1,0:T(8,128)(2,1)S(1)}, bf16[4,80,128]{2,1,0:T(8,128)(2,1)S(1)}, u32[]{:S(2)}, u32[]{:S(2)}) collective-permute-start(bf16[4,80,128]{2,1,0:T(8,128)(2,1)S(1)} %add_convert_fusion.1), channel_id=1, source_target_pairs={{0,6},{1,7},{2,4},{3,5},{4,2},{5,3},{6,0},{7,1},{8,14},{9,15},{10,... | collective-permute-start | bytes 245768 | tf_op jit(solution)/shard_map/ppermute | solution.py:374
  19.5 8.4 %collective-permute-start.6 = (bf16[4,80,128]{2,1,0:T(8,128)(2,1)S(1)}, bf16[4,80,128]{2,1,0:T(8,128)(2,1)S(1)}, u32[]{:S(2)}, u32[]{:S(2)}) collective-permute-start(bf16[4,80,128]{2,1,0:T(8,128)(2,1)S(1)} %add_convert_fusion.1), channel_id=1, source_target_pairs={{0,4},{1,5},{2,6},{3,7},{4,0},{5,1},{6,2},{7,3},{8,12},{9,13},{10,... | collective-permute-start | bytes 245768 | tf_op jit(solution)/shard_map/ppermute | solution.py:374
  19.5 8.4 %collective-permute-start.5 = (bf16[4,80,128]{2,1,0:T(8,128)(2,1)S(1)}, bf16[4,80,128]{2,1,0:T(8,128)(2,1)S(1)}, u32[]{:S(2)}, u32[]{:S(2)}) collective-permute-start(bf16[4,80,128]{2,1,0:T(8,128)(2,1)S(1)} %add_convert_fusion.1), channel_id=1, source_target_pairs={{0,2},{1,3},{2,0},{3,1},{4,6},{5,7},{6,4},{7,5},{8,10},{9,11},{10,... | collective-permute-start | bytes 245768 | tf_op jit(solution)/shard_map/ppermute | solution.py:374
  27.9 1.3 %collective-permute-start.8 = (bf16[4,80,128]{2,1,0:T(8,128)(2,1)S(1)}, bf16[4,80,128]{2,1,0:T(8,128)(2,1)S(1)}, u32[]{:S(2)}, u32[]{:S(2)}) collective-permute-start(bf16[4,80,128]{2,1,0:T(8,128)(2,1)S(1)} %add_convert_fusion.own), channel_id=1, source_target_pairs={{0,1},{2,3},{4,5},{6,7},{1,0},{3,2},{5,4},{7,6},{8,9},{10,11},{12,... | collective-permute-start | bytes 245768 | tf_op jit(solution)/shard_map/ppermute | solution.py:353
  30.5 5.3 %collective-permute-start.9 = (bf16[4,48,128]{2,1,0:T(8,128)(2,1)S(1)}, bf16[4,48,128]{2,1,0:T(8,128)(2,1)S(1)}, u32[]{:S(2)}, u32[]{:S(2)}) collective-permute-start(bf16[4,48,128]{2,1,0:T(8,128)(2,1)S(1)} %get-tuple-element.57), channel_id=1, source_target_pairs={{8,16},{24,0},{16,8},{0,24},{9,17},{25,1},{17,9},{1,25},{10,18},{2... | collective-permute-start | bytes 147464 | tf_op jit(solution)/shard_map/ppermute | solution.py:353
  31.3 4.5 %collective-permute-start.10 = (bf16[4,48,128]{2,1,0:T(8,128)(2,1)S(1)}, bf16[4,48,128]{2,1,0:T(8,128)(2,1)S(1)}, u32[]{:S(2)}, u32[]{:S(2)}) collective-permute-start(bf16[4,48,128]{2,1,0:T(8,128)(2,1)S(1)} %get-tuple-element.58), channel_id=1, source_target_pairs={{0,8},{16,24},{8,0},{24,16},{1,9},{17,25},{9,1},{25,17},{2,10},{18... | collective-permute-start | bytes 147464 | tf_op jit(solution)/shard_map/ppermute | solution.py:353
  38.0 6.4 %collective-permute-start.11 = (bf16[4,96,128]{2,1,0:T(8,128)(2,1)S(1)}, bf16[4,96,128]{2,1,0:T(8,128)(2,1)S(1)}, u32[]{:S(2)}, u32[]{:S(2)}) collective-permute-start(bf16[4,96,128]{2,1,0:T(8,128)(2,1)S(1)} %get-tuple-element.61), channel_id=1, source_target_pairs={{8,16},{24,0},{16,8},{0,24},{9,17},{25,1},{17,9},{1,25},{10,18},{2... | collective-permute-start | bytes 294920 | tf_op jit(solution)/shard_map/ppermute | solution.py:353
  39.9 5.8 %collective-permute-start.12 = (bf16[4,96,128]{2,1,0:T(8,128)(2,1)S(1)}, bf16[4,96,128]{2,1,0:T(8,128)(2,1)S(1)}, u32[]{:S(2)}, u32[]{:S(2)}) collective-permute-start(bf16[4,96,128]{2,1,0:T(8,128)(2,1)S(1)} %get-tuple-element.62), channel_id=1, source_target_pairs={{1,2},{3,4},{5,6},{7,0},{2,1},{4,3},{6,5},{0,7},{9,10},{11,12},{13... | collective-permute-start | bytes 294920 | tf_op jit(solution)/shard_map/ppermute | solution.py:353
  40.5 5.2 %collective-permute-start.13 = (bf16[4,96,128]{2,1,0:T(8,128)(2,1)S(1)}, bf16[4,96,128]{2,1,0:T(8,128)(2,1)S(1)}, u32[]{:S(2)}, u32[]{:S(2)}) collective-permute-start(bf16[4,96,128]{2,1,0:T(8,128)(2,1)S(1)} %get-tuple-element.63), channel_id=1, source_target_pairs={{0,8},{16,24},{8,0},{24,16},{1,9},{17,25},{9,1},{25,17},{2,10},{18... | collective-permute-start | bytes 294920 | tf_op jit(solution)/shard_map/ppermute | solution.py:353
  41.1 4.6 %collective-permute-start.14 = (bf16[4,96,128]{2,1,0:T(8,128)(2,1)S(1)}, bf16[4,96,128]{2,1,0:T(8,128)(2,1)S(1)}, u32[]{:S(2)}, u32[]{:S(2)}) collective-permute-start(bf16[4,96,128]{2,1,0:T(8,128)(2,1)S(1)} %get-tuple-element.64), channel_id=1, source_target_pairs={{0,1},{2,3},{4,5},{6,7},{1,0},{3,2},{5,4},{7,6},{8,9},{10,11},{12,... | collective-permute-start | bytes 294920 | tf_op jit(solution)/shard_map/ppermute | solution.py:353
